TPU v7x, 256 devices: a whole 4x4x8 slice. The times are simulated.
256 devices in a mesh: thick: 8 (over z), facade: 32 (over y, x, core).
Axes of the slice: x: 4, y: 4, z: 8, core: 2. Of those that a mesh axis runs over, the one named last changes fastest.
Arguments:
- solid_occupancy: float32 [64, 16, 16384], P('thick', None, 'facade'), may hold values from 0 to 1
- newer_occupancy_shift: float32 [64, 16, 16384], P('thick', None, 'facade'), may hold values from -0.1 to 0.1
- older_occupancy_shift: float32 [64, 16, 16384], P('thick', None, 'facade'), may hold values from -0.1 to 0.1
- below_limit_spacing: float32 [64, 16, 16384], P('thick', None, 'facade'), may hold values from 0.05 to 0.5
- above_limit_spacing: float32 [64, 16, 16384], P('thick', None, 'facade'), may hold values from 0.05 to 0.5
- thermal_state: float32 [64, 16, 16384], P('thick', None, 'facade'), may hold values from -6 to 6
- loss_state_derivative: float32 [64, 16, 16384], P('thick', None, 'facade'), may hold values from -6 to 6
- prior_dual_state: float32 [64, 16, 16384], P('thick', None, 'facade'), may hold values from -3 to 3
- cell_material: int32 [64, 16, 16384], P('thick', None, 'facade'), may hold values from 0 to 2
Outputs:
- density_new: float32 [64, 16, 16384], P('thick', None, 'facade')
- below_limit_line: float32 [64, 16, 16384], P('thick', None, 'facade')
- above_limit_line: float32 [64, 16, 16384], P('thick', None, 'facade')
- dual_state: float32 [64, 16, 16384], P('thick', None, 'facade')
Inputs may be any that keep to these rules, and one draw needn't show every extreme that they name: `cell_material`: 0 marks glass, 1 frame (the design voxels), 2 steel anchors.
All inputs are finite; a program needn't handle non-finite values. Where the computation divides by a largest or mean magnitude, that divisor is 1e-20 or more.
Results may differ from a plain program's by a relative error of at most 0.0003.
Values sent between devices are 32-bit elements; how exact they have to be, the bound alone decides.
No kernel may reach another device: no remote copies, remote signals or barrier semaphores. Data moves between devices by JAX's collectives and lax.ppermute only.
A program may use at most 64 MiB of HBM per device.

v0:
```python
import jax
import jax.numpy as jnp
from jax import lax
from jax.sharding import PartitionSpec as P

RADIUS = 4
SWEEPS = 3
NEWTON = 8


k_void = 0.03
k_frame = 160.0
k_glass = 1.0
k_anchor = 50.0
loss_rate = 0.05
spectrum_low = 0.05
spectrum_high = 2.0
solid_allowance = 0.35
curve_floor = 0.05
move_limit = 0.2
gamma_slope = 200.0


def with_halo(value, sides, width):
    for axis, dim in sides:
        size, length = (lax.axis_size(axis), value.shape[dim])
        up = [(i, (i + 1) % size) for i in range(size - 1)]
        down = [(j, i) for i, j in up]
        last = lax.slice_in_dim(value, length - width, length, axis=dim)
        first = lax.slice_in_dim(value, 0, width, axis=dim)
        before = lax.ppermute(last, axis, up)
        after = lax.ppermute(first, axis, down)
        value = jnp.concatenate([before, value, after], axis=dim)
    return value


def convolve_axis(values, axis, radius):
    count = values.shape[axis] - 2 * radius
    total = None
    for offset in range(-radius, radius + 1):
        weight = float(radius + 1 - abs(offset))
        piece = lax.slice_in_dim(values, radius + offset, radius + offset + count, axis=axis)
        total = weight * piece if total is None else total + weight * piece
    return total


def smooth(values, radius):
    out = convolve_axis(values, 0, radius)
    out = jnp.pad(out, ((0, 0), (radius, radius), (0, 0)))
    out = convolve_axis(out, 1, radius)
    return convolve_axis(out, 2, radius)


def axis_norm(start, count, total, radius):
    position = start + jnp.arange(count, dtype=jnp.int32)
    acc = jnp.zeros((count,), jnp.float32)
    for offset in range(-radius, radius + 1):
        weight = float(radius + 1 - abs(offset))
        inside = ((position + offset >= 0) & (position + offset < total)).astype(jnp.float32)
        acc = acc + weight * inside
    return acc


def neighbour_views(padded):
    center = padded[1:-1, 1:-1, 1:-1]
    views = [
        padded[2:, 1:-1, 1:-1],
        padded[:-2, 1:-1, 1:-1],
        padded[1:-1, 2:, 1:-1],
        padded[1:-1, :-2, 1:-1],
        padded[1:-1, 1:-1, 2:],
        padded[1:-1, 1:-1, :-2],
    ]
    return (center, views)


def pad_middle(values):
    return jnp.pad(values, ((0, 0), (1, 1), (0, 0)))


def conductances(padded_conductance_rim):
    center, views = neighbour_views(pad_middle(padded_conductance_rim))
    faces = []
    for view in views:
        summed = center + view
        positive = summed > 0.0
        safe_sum = jnp.where(positive, summed, 1.0)
        faces.append(jnp.where(positive, 2.0 * center * view / safe_sum, 0.0))
    return faces


def matrix_product(field_rim, heat_flux):
    center, views = neighbour_views(pad_middle(field_rim))
    total = loss_rate * center
    for face, view in zip(heat_flux, views):
        total = total + face * (center - view)
    return total


def fraction_derivative(padded_conductance_rim, adjoint_rim, temp_rim):
    k_center, k_views = neighbour_views(pad_middle(padded_conductance_rim))
    a_center, a_views = neighbour_views(pad_middle(adjoint_rim))
    t_center, t_views = neighbour_views(pad_middle(temp_rim))
    total = jnp.zeros_like(k_center)
    for k_view, a_view, t_view in zip(k_views, a_views, t_views):
        share = k_view / (k_center + k_view)
        total = total - 2.0 * share * share * (a_center - a_view) * (t_center - t_view)
    return total


def conductivity(rho, layout_candidate, glass):
    frame_value = k_void + (k_frame - k_void) * rho * rho * rho
    return jnp.where(layout_candidate, frame_value, jnp.where(glass, k_glass, k_anchor))


def diagonal_of(heat_flux):
    diagonal = loss_rate + heat_flux[0]
    for face in heat_flux[1:]:
        diagonal = diagonal + face
    return diagonal


def ready_limit_lines(
    solid_occupancy,
    newer_occupancy_shift,
    older_occupancy_shift,
    below_limit_spacing,
    above_limit_spacing,
    normalised_element,
):
    spectral_weight = 0.95 + 0.25 * jnp.tanh(
        gamma_slope * newer_occupancy_shift * older_occupancy_shift
    )
    below_limit_line = solid_occupancy - spectral_weight * below_limit_spacing
    above_limit_line = solid_occupancy + spectral_weight * above_limit_spacing
    floor_limit = jnp.maximum(
        jnp.maximum(0.0, below_limit_line + 0.1 * (solid_occupancy - below_limit_line)),
        solid_occupancy - move_limit,
    )
    ceiling_limit = jnp.minimum(
        jnp.minimum(1.0, above_limit_line - 0.1 * (above_limit_line - solid_occupancy)),
        solid_occupancy + move_limit,
    )
    up_sq = (above_limit_line - solid_occupancy) ** 2
    low_sq = (solid_occupancy - below_limit_line) ** 2
    plus = jnp.maximum(normalised_element, 0.0)
    minus = jnp.maximum(-normalised_element, 0.0)
    above_dividend_offset = up_sq * (1.001 * plus + 0.001 * minus + 1e-05)
    below_dividend_offset = low_sq * (0.001 * plus + 1.001 * minus + 1e-05)
    above_dividend_scale = up_sq * (1.001 + 1e-05)
    below_dividend_scale = low_sq * (0.001 + 1e-05)
    shared_summands = (
        solid_occupancy
        - solid_allowance
        - above_dividend_scale / (above_limit_line - solid_occupancy)
        - below_dividend_scale / (solid_occupancy - below_limit_line)
    )
    return (
        below_limit_line,
        above_limit_line,
        floor_limit,
        ceiling_limit,
        above_dividend_offset,
        below_dividend_offset,
        above_dividend_scale,
        below_dividend_scale,
        shared_summands,
    )


def dual_terms(
    multiplier,
    below_limit_line,
    above_limit_line,
    floor_limit,
    ceiling_limit,
    above_dividend_offset,
    below_dividend_offset,
    above_dividend_scale,
    below_dividend_scale,
):
    root_upper = jnp.sqrt(above_dividend_offset + multiplier * above_dividend_scale)
    root_lower = jnp.sqrt(below_dividend_offset + multiplier * below_dividend_scale)
    total = root_upper + root_lower
    trial = below_limit_line + (above_limit_line - below_limit_line) * root_lower / total
    chosen = jnp.clip(trial, floor_limit, ceiling_limit)
    free = (trial > floor_limit) & (trial < ceiling_limit)
    rate = (
        (above_limit_line - below_limit_line)
        * (
            root_upper * below_dividend_scale / (2.0 * root_lower)
            - root_lower * above_dividend_scale / (2.0 * root_upper)
        )
        / (total * total)
    )
    rate = jnp.where(free, rate, 0.0)
    slope = (
        above_dividend_scale / (above_limit_line - chosen) ** 2
        - below_dividend_scale / (chosen - below_limit_line) ** 2
    )
    g_terms = above_dividend_scale / (above_limit_line - chosen) + below_dividend_scale / (
        chosen - below_limit_line
    )
    h_terms = curve_floor + jnp.abs(slope * rate)
    return (chosen, g_terms, h_terms)


def iteration_margin(values):
    return with_halo(values, (("thick", 0), ("facade", 2)), 1)


def dual_reduce(slope_part, curve_part):
    return lax.psum((slope_part, curve_part), ("thick", "facade"))


def on_device(
    solid_occupancy,
    newer_occupancy_shift,
    older_occupancy_shift,
    below_limit_spacing,
    above_limit_spacing,
    thermal_state,
    loss_state_derivative,
    prior_dual_state,
    cell_material,
):
    rows_dev, height, cols_dev = solid_occupancy.shape
    rows_total = rows_dev * lax.axis_size("thick")
    cols_total = cols_dev * lax.axis_size("facade")
    row_start = lax.axis_index("thick") * rows_dev
    col_start = lax.axis_index("facade") * cols_dev
    layout_candidate = cell_material == 1
    glass = cell_material == 0
    first = axis_norm(row_start - 0, rows_dev + 2 * 0, rows_total, RADIUS)
    middle = axis_norm(0, height, height, RADIUS)
    last = axis_norm(col_start - 0, cols_dev + 2 * 0, cols_total, RADIUS)
    norm = first[:, None, None] * middle[None, :, None] * last[None, None, :]
    centre_value = 0.5 * (spectrum_high + spectrum_low)
    half_width = 0.5 * (spectrum_high - spectrum_low)
    ratio_value = centre_value / half_width
    density_ext = with_halo(solid_occupancy, (("thick", 0), ("facade", 2)), RADIUS)
    rho = smooth(density_ext, RADIUS) / norm
    material_coefficient = conductivity(rho, layout_candidate, glass)
    both_sides = with_halo(
        jnp.stack([material_coefficient, thermal_state]), (("thick", 1), ("facade", 3)), 1
    )
    padded_conductance_rim = both_sides[0]
    temp_rim = both_sides[1]
    heat_flux = conductances(padded_conductance_rim)
    diagonal = diagonal_of(heat_flux)
    dual_state = prior_dual_state
    equation_mismatch = loss_state_derivative - matrix_product(
        iteration_margin(dual_state), heat_flux
    )
    direction = equation_mismatch / diagonal / centre_value
    factor = 1.0 / ratio_value
    for sweep in range(SWEEPS):
        dual_state = dual_state + direction
        if sweep < SWEEPS - 1:
            equation_mismatch = equation_mismatch - matrix_product(
                iteration_margin(direction), heat_flux
            )
            factor_next = 1.0 / (2.0 * ratio_value - factor)
            direction = factor_next * factor * direction + 2.0 * factor_next / half_width * (
                equation_mismatch / diagonal
            )
            factor = factor_next
    derivative_map = fraction_derivative(
        padded_conductance_rim, iteration_margin(dual_state), temp_rim
    )
    weighted = (
        jnp.where(layout_candidate, derivative_map * (3.0 * (k_frame - k_void)) * rho * rho, 0.0)
        / norm
    )
    weighted_ext = with_halo(weighted, (("thick", 0), ("facade", 2)), RADIUS)
    grad = smooth(weighted_ext, RADIUS)
    scale = lax.pmax(jnp.max(jnp.where(layout_candidate, jnp.abs(grad), 0.0)), ("thick", "facade"))
    normalised_element = grad / (scale + 1e-06)
    (
        below_limit_line,
        above_limit_line,
        floor_limit,
        ceiling_limit,
        above_dividend_offset,
        below_dividend_offset,
        above_dividend_scale,
        below_dividend_scale,
        shared_summands,
    ) = ready_limit_lines(
        solid_occupancy,
        newer_occupancy_shift,
        older_occupancy_shift,
        below_limit_spacing,
        above_limit_spacing,
        normalised_element,
    )
    reference_point_here = jnp.sum(jnp.where(layout_candidate, shared_summands, 0.0))
    multiplier = jnp.float32(1.0)
    for step in range(NEWTON):
        chosen, g_terms, h_terms = dual_terms(
            multiplier,
            below_limit_line,
            above_limit_line,
            floor_limit,
            ceiling_limit,
            above_dividend_offset,
            below_dividend_offset,
            above_dividend_scale,
            below_dividend_scale,
        )
        slope_sum, curve = dual_reduce(
            reference_point_here + jnp.sum(jnp.where(layout_candidate, g_terms, 0.0)),
            jnp.sum(jnp.where(layout_candidate, h_terms, 0.0)),
        )
        multiplier = jnp.maximum(jnp.float32(0.0), multiplier + slope_sum / curve)
    chosen, g_terms, h_terms = dual_terms(
        multiplier,
        below_limit_line,
        above_limit_line,
        floor_limit,
        ceiling_limit,
        above_dividend_offset,
        below_dividend_offset,
        above_dividend_scale,
        below_dividend_scale,
    )
    density_new = jnp.where(layout_candidate, chosen, solid_occupancy)
    return (density_new, below_limit_line, above_limit_line, dual_state)


def solution(mesh):
    return jax.shard_map(
        on_device,
        mesh=mesh,
        in_specs=(
            P("thick", None, "facade"),
            P("thick", None, "facade"),
            P("thick", None, "facade"),
            P("thick", None, "facade"),
            P("thick", None, "facade"),
            P("thick", None, "facade"),
            P("thick", None, "facade"),
            P("thick", None, "facade"),
            P("thick", None, "facade"),
        ),
        out_specs=(
            P("thick", None, "facade"),
            P("thick", None, "facade"),
            P("thick", None, "facade"),
            P("thick", None, "facade"),
        ),
        check_vma=False,
    )
```

profile of v0, /device:TPU:1, one launch (start us, length us, event | category | flops | bytes accessed | tf_op | source)
XLA Modules:
  0.0 852.6 jit_solution(6462052266821622398)
XLA Ops:
  0.6 0.8 fusion.206
  1.4 1.3 collective-permute-start.8
  2.7 5.1 collective-permute-start.9
  7.9 1.0 fusion.207
  8.8 1.3 collective-permute-start.1
  10.1 4.2 collective-permute-start
  14.5 1.7 collective-permute-done
  16.4 5.0 collective-permute-start.2
  21.4 1.9 collective-permute-start.3
  23.4 4.3 collective-permute-done.3
  30.1 4.1 collective-permute-start.4
  34.2 1.3 collective-permute-start.5
  35.6 1.9 collective-permute-start.11
  37.5 3.6 collective-permute-start.10
  41.3 1.9 collective-permute-start.6
  43.2 2.4 collective-permute-start.7
  45.9 3.9 collective-permute-done.7
  50.2 0.9 copy-done.11
  51.1 0.9 broadcast_multiply_fusion.2
  52.0 4.8 collective-permute-start.13
  56.8 1.3 collective-permute-start.12
  58.1 5.2 collective-permute-done.12
  63.3 1.9 collective-permute-start.15
  65.3 3.6 collective-permute-start.14
  69.1 1.3 collective-permute-done.14
  71.2 5.1 collective-permute-start.17
  76.4 1.3 collective-permute-start.16
  77.7 4.4 collective-permute-done.16
  82.1 1.9 collective-permute-start.19
  84.1 5.4 collective-permute-start.18
  89.7 1.3 collective-permute-done.18
  91.2 0.9 fusion.91
  92.2 4.6 collective-permute-start.21
  96.8 1.3 collective-permute-start.20
  98.1 3.6 collective-permute-done.20
  101.8 1.9 collective-permute-start.23
  103.7 5.4 collective-permute-start.22
  109.3 1.3 collective-permute-done.22
  110.9 1.2 multiply_divide_fusion
  112.2 3.6 collective-permute-start.24
  115.8 1.3 collective-permute-start.25
  117.7 3.8 collective-permute-done.25
  121.6 5.8 collective-permute-start.26
  127.5 1.9 collective-permute-start.27
  129.4 4.3 collective-permute-done.27
  134.6 1.2 select_reduce_fusion.17
  135.8 91.8 %pmax.7 = f32[]{:T(128)} all-reduce(f32[]{:T(128)} %get-tuple-element.40), channel_id=1, replica_groups=mesh['thick'=8,'facade'=32] {'thick','facade'}, use_global_device_ids=true, to_apply=%region_1.2 | all-reduce | flops 1 | bytes 8 | tf_op jit(solution)/shard_map/pmax | solution.py:277
  228.3 1.8 select_reduce_fusion.14
  231.4 73.3 %all-reduce.15 = (f32[]{:T(128)}, f32[]{:T(128)}) all-reduce(f32[]{:T(128)S(6)} %add.1077, f32[]{:T(128)} %get-tuple-element.18), channel_id=1, replica_groups=mesh['thick'=8,'facade'=32] {'thick','facade'}, use_global_device_ids=true, to_apply=%region_4.5 | all-reduce | flops 2 | bytes 16 | tf_op jit(solution)/shard_map/psum | solution.py:213
  305.9 1.5 select_reduce_fusion.12
  308.7 73.9 %all-reduce.14 = (f32[]{:T(128)}, f32[]{:T(128)}) all-reduce(f32[]{:T(128)S(6)} %add.1085, f32[]{:T(128)} %get-tuple-element.16), channel_id=1, replica_groups=mesh['thick'=8,'facade'=32] {'thick','facade'}, use_global_device_ids=true, to_apply=%region_8.9 | all-reduce | flops 2 | bytes 16 | tf_op jit(solution)/shard_map/psum | solution.py:213
  383.8 1.5 select_reduce_fusion.10
  386.5 73.9 %all-reduce.13 = (f32[]{:T(128)}, f32[]{:T(128)}) all-reduce(f32[]{:T(128)S(6)} %add.1093, f32[]{:T(128)} %get-tuple-element.14), channel_id=1, replica_groups=mesh['thick'=8,'facade'=32] {'thick','facade'}, use_global_device_ids=true, to_apply=%region_12.13 | all-reduce | flops 2 | bytes 16 | tf_op jit(solution)/shard_map/psum | solution.py:213
  461.7 1.5 select_reduce_fusion.8
  464.4 73.9 %all-reduce.12 = (f32[]{:T(128)}, f32[]{:T(128)}) all-reduce(f32[]{:T(128)S(6)} %add.1101, f32[]{:T(128)} %get-tuple-element.12), channel_id=1, replica_groups=mesh['thick'=8,'facade'=32] {'thick','facade'}, use_global_device_ids=true, to_apply=%region_16.17 | all-reduce | flops 2 | bytes 16 | tf_op jit(solution)/shard_map/psum | solution.py:213
  539.6 1.5 select_reduce_fusion.6
  542.3 73.9 %all-reduce.11 = (f32[]{:T(128)}, f32[]{:T(128)}) all-reduce(f32[]{:T(128)S(6)} %add.1109, f32[]{:T(128)} %get-tuple-element.10), channel_id=1, replica_groups=mesh['thick'=8,'facade'=32] {'thick','facade'}, use_global_device_ids=true, to_apply=%region_20.21 | all-reduce | flops 2 | bytes 16 | tf_op jit(solution)/shard_map/psum | solution.py:213
  617.4 1.5 select_reduce_fusion.4
  620.2 74.2 %all-reduce.10 = (f32[]{:T(128)}, f32[]{:T(128)}) all-reduce(f32[]{:T(128)S(6)} %add.1117, f32[]{:T(128)} %get-tuple-element.8), channel_id=1, replica_groups=mesh['thick'=8,'facade'=32] {'thick','facade'}, use_global_device_ids=true, to_apply=%region_24.25 | all-reduce | flops 2 | bytes 16 | tf_op jit(solution)/shard_map/psum | solution.py:213
  695.6 1.5 select_reduce_fusion.2
  698.3 73.9 %all-reduce.9 = (f32[]{:T(128)}, f32[]{:T(128)}) all-reduce(f32[]{:T(128)S(6)} %add.1125, f32[]{:T(128)} %get-tuple-element.6), channel_id=1, replica_groups=mesh['thick'=8,'facade'=32] {'thick','facade'}, use_global_device_ids=true, to_apply=%region_28.29 | all-reduce | flops 2 | bytes 16 | tf_op jit(solution)/shard_map/psum | solution.py:213
  773.4 1.5 select_reduce_fusion
  776.2 73.8 %all-reduce.8 = (f32[]{:T(128)}, f32[]{:T(128)}) all-reduce(f32[]{:T(128)S(6)} %add.1133, f32[]{:T(128)} %get-tuple-element.4), channel_id=1, replica_groups=mesh['thick'=8,'facade'=32] {'thick','facade'}, use_global_device_ids=true, to_apply=%region_32.33 | all-reduce | flops 2 | bytes 16 | tf_op jit(solution)/shard_map/psum | solution.py:213
  851.4 1.2 minimum_select_fusion
  (76 shorter events, 7.1 us)
Async XLA Ops:
  1.4 22.0 %collective-permute-start.8 = (f32[1,16,512]{2,1,0:T(8,128)S(1)}, f32[1,16,512]{2,1,0:T(8,128)S(1)}, u32[]{:S(2)}, u32[]{:S(2)}) collective-permute-start(f32[1,16,512]{2,1,0:T(8,128)S(1)} %get-tuple-element.79), channel_id=1, source_target_pairs={{32,0},{64,32},{96,64},{128,96},{160,128},{192,160},{224,192},{33,... | collective-permute-start | bytes 98312 | tf_op jit(solution)/shard_map/ppermute | solution.py:32
  2.7 11.8 %copy-start.4 = (f32[8,16,512]{2,1,0:T(8,128)S(1)}, f32[8,16,512]{2,1,0:T(8,128)}, u32[]{:S(2)}) copy-start(f32[8,16,512]{2,1,0:T(8,128)} %param.16) | copy-start | bytes 786436
  2.7 11.8 %collective-permute-start.9 = (f32[1,16,512]{2,1,0:T(8,128)S(1)}, f32[1,16,512]{2,1,0:T(8,128)S(1)}, u32[]{:S(2)}, u32[]{:S(2)}) collective-permute-start(f32[1,16,512]{2,1,0:T(8,128)S(1)} %get-tuple-element.80), channel_id=1, source_target_pairs={{0,32},{32,64},{64,96},{96,128},{128,160},{160,192},{192,224},{1,3... | collective-permute-start | bytes 98312 | tf_op jit(solution)/shard_map/ppermute | solution.py:31
  8.8 7.5 collective-permute-start.1
  10.1 6.1 collective-permute-start
  14.5 1.8 copy-start
  16.4 7.0 collective-permute-start.2
  21.4 6.3 collective-permute-start.3
  28.2 1.0 copy-start.6
  29.1 0.9 copy-start.5
  30.1 11.0 %collective-permute-start.4 = (f32[2,1,16,512]{3,2,1,0:T(8,128)S(1)}, f32[2,1,16,512]{3,2,1,0:T(8,128)S(1)}, u32[]{:S(2)}, u32[]{:S(2)}) collective-permute-start(f32[2,1,16,512]{3,2,1,0:T(8,128)S(1)} %get-tuple-element.59), channel_id=1, source_target_pairs={{0,32},{32,64},{64,96},{96,128},{128,160},{160,192},{192,224},{1,3... | collective-permute-start | bytes 196616 | tf_op jit(solution)/shard_map/ppermute | solution.py:31
  34.2 7.0 collective-permute-start.5
  35.6 10.1 %collective-permute-start.11 = (f32[10,16,1]{2,1,0:T(8,128)S(1)}, f32[10,16,1]{2,1,0:T(8,128)S(1)}, u32[]{:S(2)}, u32[]{:S(2)}) collective-permute-start(f32[10,16,1]{2,1,0:T(8,128)S(1)} %get-tuple-element.69), channel_id=1, source_target_pairs={{1,0},{2,1},{3,2},{4,3},{5,4},{6,5},{7,6},{8,7},{9,8},{10,9},{11,1... | collective-permute-start | bytes 1928 | tf_op jit(solution)/shard_map/ppermute | solution.py:32
  37.5 8.1 collective-permute-start.10
  41.3 4.6 collective-permute-start.6
  43.2 6.6 collective-permute-start.7
  50.2 1.0 copy-start.11
  52.0 6.1 collective-permute-start.13
  56.8 6.5 collective-permute-start.12
  63.3 5.8 collective-permute-start.15
  65.3 5.1 collective-permute-start.14
  71.2 6.5 collective-permute-start.17
  76.4 5.7 collective-permute-start.16
  82.1 7.6 collective-permute-start.19
  84.1 6.9 collective-permute-start.18
  92.2 18.7 %copy-start.3 = (f32[8,16,512]{2,1,0:T(8,128)}, f32[8,16,512]{2,1,0:T(8,128)S(1)}, u32[]{:S(2)}) copy-start(f32[8,16,512]{2,1,0:T(8,128)S(1)} %fusion.91) | copy-start | bytes 786436
  92.2 5.9 collective-permute-start.21
  96.8 4.9 collective-permute-start.20
  101.8 7.6 collective-permute-start.23
  103.7 6.9 collective-permute-start.22
  112.2 5.6 collective-permute-start.24
  115.8 5.7 collective-permute-start.25
  121.6 7.8 collective-permute-start.26
  127.5 6.3 collective-permute-start.27
  134.5 93.7 %copy-start.7 = (f32[8,16,512]{2,1,0:T(8,128)S(1)}, f32[8,16,512]{2,1,0:T(8,128)}, u32[]{:S(2)}) copy-start(f32[8,16,512]{2,1,0:T(8,128)} %param.13) | copy-start | bytes 786436
  134.5 93.7 %copy-start.8 = (f32[8,16,512]{2,1,0:T(8,128)S(1)}, f32[8,16,512]{2,1,0:T(8,128)}, u32[]{:S(2)}) copy-start(f32[8,16,512]{2,1,0:T(8,128)} %param.11) | copy-start | bytes 786436
  134.5 93.7 %copy-start.9 = (f32[8,16,512]{2,1,0:T(8,128)S(1)}, f32[8,16,512]{2,1,0:T(8,128)}, u32[]{:S(2)}) copy-start(f32[8,16,512]{2,1,0:T(8,128)} %param.10) | copy-start | bytes 786436
  134.5 93.7 %copy-start.10 = (f32[8,16,512]{2,1,0:T(8,128)S(1)}, f32[8,16,512]{2,1,0:T(8,128)}, u32[]{:S(2)}) copy-start(f32[8,16,512]{2,1,0:T(8,128)} %param.12) | copy-start | bytes 786436
  230.1 621.3 %copy-start.1 = (f32[8,16,512]{2,1,0:T(8,128)}, f32[8,16,512]{2,1,0:T(8,128)S(1)}, u32[]{:S(2)}) copy-start(f32[8,16,512]{2,1,0:T(8,128)S(1)} %get-tuple-element.38) | copy-start | bytes 786436
  230.1 621.3 %copy-start.2 = (f32[8,16,512]{2,1,0:T(8,128)}, f32[8,16,512]{2,1,0:T(8,128)S(1)}, u32[]{:S(2)}) copy-start(f32[8,16,512]{2,1,0:T(8,128)S(1)} %get-tuple-element.39) | copy-start | bytes 786436
where the time goes:
time: 855 us; the launch traced here: 853 us
  blocking collectives  683 us (80%)
  starting transfers between devices  85.4 us (10%)
  waiting for transfers between devices  36.3 us (4%)
  other arithmetic  22.2 us (3%)
  between operations  22.2 us (3%)
    psum x8, blocking collectives, dual_reduce(): return lax.psum((slope_part, curve_part), ('thick', 'facade'))  591 us
    pmax x1, blocking collectives, on_device(): lax.pmax(jnp.max(jnp.where(layout_candidate, jnp.abs(grad), 0.0)), ('thic...  91.8 us
    ppermute x14, starting transfers between devices, with_halo(): before = lax.ppermute(last, axis, up)  62.4 us
    ppermute x14, waiting for transfers between devices, with_halo(): after = lax.ppermute(first, axis, down)  30.1 us
    ppermute x14, starting transfers between devices, with_halo(): after = lax.ppermute(first, axis, down)  23 us
  transfers between devices with their start and end apart: 28, of which 15 were waited for; matrix products, arithmetic and copies ran while one was open for 0% of the time, Pallas kernels for 0%

commit v1 on v0

--- a/solution.py
+++ b/solution.py
@@ -209,8 +209,18 @@
     return with_halo(values, (("thick", 0), ("facade", 2)), 1)
 
 
+def everyone(row):
+    axes = ("thick", "facade")
+    count = lax.axis_size("thick") * lax.axis_size("facade")
+    copies = jnp.broadcast_to(row, (count, row.shape[-1]))
+    return lax.all_to_all(copies, axes, 0, 0, tiled=True)
+
+
 def dual_reduce(slope_part, curve_part):
-    return lax.psum((slope_part, curve_part), ("thick", "facade"))
+    half = jnp.arange(128) < 64
+    rows = everyone(jnp.where(half, slope_part, curve_part)[None, :])
+    total = jnp.sum(rows, axis=0)
+    return total[0], total[64]
 
 
 def on_device(
@@ -274,7 +284,8 @@
     )
     weighted_ext = with_halo(weighted, (("thick", 0), ("facade", 2)), RADIUS)
     grad = smooth(weighted_ext, RADIUS)
-    scale = lax.pmax(jnp.max(jnp.where(layout_candidate, jnp.abs(grad), 0.0)), ("thick", "facade"))
+    scale_here = jnp.max(jnp.where(layout_candidate, jnp.abs(grad), 0.0))
+    scale = jnp.max(everyone(jnp.full((1, 128), scale_here)))
     normalised_element = grad / (scale + 1e-06)
     (
         below_limit_line,

time: 855 us -> 370 us (0.43)
  blocking collectives: 683 us -> 186 us
    psum x8 -> x0, blocking collectives: 591 us -> none  [dual_reduce(): return lax.psum((slope_part, curve_part), ('thick', 'facade'))]
    all_to_all x0 -> x9, blocking collectives: none -> 186 us  [everyone(): return lax.all_to_all(copies, axes, 0, 0, tiled=True)]
    pmax x1 -> x0, blocking collectives: 91.8 us -> none  [on_device(): lax.pmax(jnp.max(jnp.where(layout_candidate, jnp.abs(grad), 0.0)), ('thic...]
where the time goes in v1:
time: 370 us; the launch traced here: 369 us
  blocking collectives  186 us (50%)
  starting transfers between devices  85.4 us (23%)
  waiting for transfers between devices  36.3 us (10%)
  other arithmetic  28.5 us (8%)
  between operations  22.9 us (6%)
  local copies, waits for them, and re-layouts  9.99 us (3%)
    all_to_all x9, blocking collectives, everyone(): return lax.all_to_all(copies, axes, 0, 0, tiled=True)  186 us
    ppermute x14, starting transfers between devices, with_halo(): before = lax.ppermute(last, axis, up)  62.4 us
    ppermute x14, waiting for transfers between devices, with_halo(): after = lax.ppermute(first, axis, down)  30.1 us
    ppermute x14, starting transfers between devices, with_halo(): after = lax.ppermute(first, axis, down)  23 us
    reduce_sum x8, other arithmetic, on_device(): jnp.sum(jnp.where(layout_candidate, g_terms, 0.0))  12.4 us
  transfers between devices with their start and end apart: 28, of which 15 were waited for; matrix products, arithmetic and copies ran while one was open for 0% of the time, Pallas kernels for 0%

profile of v1, /device:TPU:1, one launch (start us, length us, event | category | flops | bytes accessed | tf_op | source)
XLA Modules:
  0.0 368.7 jit_solution(15525668702023299285)
XLA Ops:
  0.6 0.8 fusion.214
  1.4 1.3 collective-permute-start.8
  2.7 5.1 %collective-permute-start.9 = (f32[1,16,512]{2,1,0:T(8,128)S(1)}, f32[1,16,512]{2,1,0:T(8,128)S(1)}, u32[]{:S(2)}, u32[]{:S(2)}) collective-permute-start(f32[1,16,512]{2,1,0:T(8,128)S(1)} %get-tuple-element.64), channel_id=1, source_target_pairs={{0,32},{32,64},{64,96},{96,128},{128,160},{160,192},{192,224},{1,3... | collective-permute-start | bytes 98312 | tf_op jit(solution)/shard_map/ppermute | solution.py:31
  7.9 1.0 fusion.215
  8.8 1.3 collective-permute-start.1
  10.1 4.2 %collective-permute-start = (f32[4,16,512]{2,1,0:T(8,128)S(1)}, f32[4,16,512]{2,1,0:T(8,128)S(1)}, u32[]{:S(2)}, u32[]{:S(2)}) collective-permute-start(f32[4,16,512]{2,1,0:T(8,128)S(1)} %get-tuple-element.66), channel_id=1, source_target_pairs={{0,32},{32,64},{64,96},{96,128},{128,160},{160,192},{192,224},{1,3... | collective-permute-start | bytes 393224 | tf_op jit(solution)/shard_map/ppermute | solution.py:31
  14.5 1.7 collective-permute-done
  16.4 5.0 %collective-permute-start.2 = (f32[16,16,4]{2,1,0:T(8,128)S(1)}, f32[16,16,4]{2,1,0:T(8,128)S(1)}, u32[]{:S(2)}, u32[]{:S(2)}) collective-permute-start(f32[16,16,4]{2,1,0:T(8,128)S(1)} %get-tuple-element.45), channel_id=1, source_target_pairs={{0,1},{1,2},{2,3},{3,4},{4,5},{5,6},{6,7},{7,8},{8,9},{9,10},{10,1... | collective-permute-start | bytes 12296 | tf_op jit(solution)/shard_map/ppermute | solution.py:31
  21.4 1.9 collective-permute-start.3
  23.4 4.3 %collective-permute-done.3 = f32[16,16,4]{2,1,0:T(8,128)S(1)} collective-permute-done((f32[16,16,4]{2,1,0:T(8,128)S(1)}, f32[16,16,4]{2,1,0:T(8,128)S(1)}, u32[]{:S(2)}, u32[]{:S(2)}) %collective-permute-start.3) | collective-permute-done | bytes 4128 | tf_op jit(solution)/shard_map/ppermute | solution.py:32
  30.1 4.1 %collective-permute-start.4 = (f32[2,1,16,512]{3,2,1,0:T(8,128)S(1)}, f32[2,1,16,512]{3,2,1,0:T(8,128)S(1)}, u32[]{:S(2)}, u32[]{:S(2)}) collective-permute-start(f32[2,1,16,512]{3,2,1,0:T(8,128)S(1)} %get-tuple-element.43), channel_id=1, source_target_pairs={{0,32},{32,64},{64,96},{96,128},{128,160},{160,192},{192,224},{1,3... | collective-permute-start | bytes 196616 | tf_op jit(solution)/shard_map/ppermute | solution.py:31
  34.2 1.3 collective-permute-start.5
  35.6 1.9 collective-permute-start.11
  37.5 3.6 collective-permute-start.10
  41.3 1.9 collective-permute-start.6
  43.2 2.4 collective-permute-start.7
  45.9 3.9 %collective-permute-done.7 = f32[2,10,16,1]{3,2,1,0:T(8,128)S(1)} collective-permute-done((f32[2,10,16,1]{3,2,1,0:T(8,128)S(1)}, f32[2,10,16,1]{3,2,1,0:T(8,128)S(1)}, u32[]{:S(2)}, u32[]{:S(2)}) %collective-permute-start.7) | collective-permute-done | bytes 1312 | tf_op jit(solution)/shard_map/ppermute | solution.py:32
  50.2 0.9 copy-done.11
  51.1 0.9 broadcast_multiply_fusion.2
  52.0 4.8 %collective-permute-start.13 = (f32[1,16,512]{2,1,0:T(8,128)S(1)}, f32[1,16,512]{2,1,0:T(8,128)S(1)}, u32[]{:S(2)}, u32[]{:S(2)}) collective-permute-start(f32[1,16,512]{2,1,0:T(8,128)S(1)} %get-tuple-element.61), channel_id=1, source_target_pairs={{0,32},{32,64},{64,96},{96,128},{128,160},{160,192},{192,224},{1,3... | collective-permute-start | bytes 98312 | tf_op jit(solution)/shard_map/ppermute | solution.py:31
  56.8 1.3 collective-permute-start.12
  58.1 5.2 %collective-permute-done.12 = f32[1,16,512]{2,1,0:T(8,128)S(1)} collective-permute-done((f32[1,16,512]{2,1,0:T(8,128)S(1)}, f32[1,16,512]{2,1,0:T(8,128)S(1)}, u32[]{:S(2)}, u32[]{:S(2)}) %collective-permute-start.12) | collective-permute-done | bytes 32800 | tf_op jit(solution)/shard_map/ppermute | solution.py:32
  63.3 1.9 collective-permute-start.15
  65.3 3.6 collective-permute-start.14
  69.1 1.3 collective-permute-done.14
  71.2 5.1 %collective-permute-start.17 = (f32[1,16,512]{2,1,0:T(8,128)S(1)}, f32[1,16,512]{2,1,0:T(8,128)S(1)}, u32[]{:S(2)}, u32[]{:S(2)}) collective-permute-start(f32[1,16,512]{2,1,0:T(8,128)S(1)} %get-tuple-element.59), channel_id=1, source_target_pairs={{0,32},{32,64},{64,96},{96,128},{128,160},{160,192},{192,224},{1,3... | collective-permute-start | bytes 98312 | tf_op jit(solution)/shard_map/ppermute | solution.py:31
  76.4 1.3 collective-permute-start.16
  77.7 4.4 %collective-permute-done.16 = f32[1,16,512]{2,1,0:T(8,128)S(1)} collective-permute-done((f32[1,16,512]{2,1,0:T(8,128)S(1)}, f32[1,16,512]{2,1,0:T(8,128)S(1)}, u32[]{:S(2)}, u32[]{:S(2)}) %collective-permute-start.16) | collective-permute-done | bytes 32800 | tf_op jit(solution)/shard_map/ppermute | solution.py:32
  82.1 1.9 collective-permute-start.19
  84.1 5.4 %collective-permute-start.18 = (f32[10,16,1]{2,1,0:T(8,128)S(1)}, f32[10,16,1]{2,1,0:T(8,128)S(1)}, u32[]{:S(2)}, u32[]{:S(2)}) collective-permute-start(f32[10,16,1]{2,1,0:T(8,128)S(1)} %get-tuple-element.50), channel_id=1, source_target_pairs={{0,1},{1,2},{2,3},{3,4},{4,5},{5,6},{6,7},{7,8},{8,9},{9,10},{10,1... | collective-permute-start | bytes 1928 | tf_op jit(solution)/shard_map/ppermute | solution.py:31
  89.7 1.3 collective-permute-done.18
  91.2 0.9 fusion.91
  92.2 4.6 %collective-permute-start.21 = (f32[1,16,512]{2,1,0:T(8,128)S(1)}, f32[1,16,512]{2,1,0:T(8,128)S(1)}, u32[]{:S(2)}, u32[]{:S(2)}) collective-permute-start(f32[1,16,512]{2,1,0:T(8,128)S(1)} %get-tuple-element.57), channel_id=1, source_target_pairs={{0,32},{32,64},{64,96},{96,128},{128,160},{160,192},{192,224},{1,3... | collective-permute-start | bytes 98312 | tf_op jit(solution)/shard_map/ppermute | solution.py:31
  96.8 1.3 collective-permute-start.20
  98.1 3.6 collective-permute-done.20
  101.8 1.9 collective-permute-start.23
  103.7 5.4 %collective-permute-start.22 = (f32[10,16,1]{2,1,0:T(8,128)S(1)}, f32[10,16,1]{2,1,0:T(8,128)S(1)}, u32[]{:S(2)}, u32[]{:S(2)}) collective-permute-start(f32[10,16,1]{2,1,0:T(8,128)S(1)} %get-tuple-element.48), channel_id=1, source_target_pairs={{0,1},{1,2},{2,3},{3,4},{4,5},{5,6},{6,7},{7,8},{8,9},{9,10},{10,1... | collective-permute-start | bytes 1928 | tf_op jit(solution)/shard_map/ppermute | solution.py:31
  109.3 1.3 collective-permute-done.22
  110.9 1.2 multiply_divide_fusion
  112.2 3.6 collective-permute-start.24
  115.8 1.3 collective-permute-start.25
  117.7 3.8 %collective-permute-done.25 = f32[4,16,512]{2,1,0:T(8,128)S(1)} collective-permute-done((f32[4,16,512]{2,1,0:T(8,128)S(1)}, f32[4,16,512]{2,1,0:T(8,128)S(1)}, u32[]{:S(2)}, u32[]{:S(2)}) %collective-permute-start.25) | collective-permute-done | bytes 131104 | tf_op jit(solution)/shard_map/ppermute | solution.py:32
  121.6 5.8 %collective-permute-start.26 = (f32[16,16,4]{2,1,0:T(8,128)S(1)}, f32[16,16,4]{2,1,0:T(8,128)S(1)}, u32[]{:S(2)}, u32[]{:S(2)}) collective-permute-start(f32[16,16,4]{2,1,0:T(8,128)S(1)} %get-tuple-element.41), channel_id=1, source_target_pairs={{0,1},{1,2},{2,3},{3,4},{4,5},{5,6},{6,7},{7,8},{8,9},{9,10},{10,1... | collective-permute-start | bytes 12296 | tf_op jit(solution)/shard_map/ppermute | solution.py:31
  127.5 1.9 collective-permute-start.27
  129.4 4.3 %collective-permute-done.27 = f32[16,16,4]{2,1,0:T(8,128)S(1)} collective-permute-done((f32[16,16,4]{2,1,0:T(8,128)S(1)}, f32[16,16,4]{2,1,0:T(8,128)S(1)}, u32[]{:S(2)}, u32[]{:S(2)}) %collective-permute-start.27) | collective-permute-done | bytes 4128 | tf_op jit(solution)/shard_map/ppermute | solution.py:32
  134.5 1.2 select_reduce_fusion.17
  136.5 38.6 %all_to_all.54 = f32[256,1,128]{2,1,0:T(1,128)S(1)} all-to-all(f32[256,1,128]{2,1,0:T(1,128)S(1)} %broadcast_in_dim_broadcast_in_dim.3), channel_id=1, replica_groups=mesh['thick'=8,'facade'=32] {'thick','facade'}, dimensions={0} | all-to-all | bytes 262144 | tf_op jit(solution)/shard_map/all_to_all | solution.py:216
  176.5 1.8 select_reduce_fusion.15
  180.3 18.4 %all_to_all.55 = f32[256,1,128]{2,1,0:T(1,128)S(1)} all-to-all(f32[256,1,128]{2,1,0:T(1,128)S(1)} %broadcast_in_dim.150), channel_id=1, replica_groups=mesh['thick'=8,'facade'=32] {'thick','facade'}, dimensions={0} | all-to-all | bytes 262144 | tf_op jit(solution)/shard_map/all_to_all | solution.py:216
  200.5 1.5 select_reduce_fusion.13
  204.1 18.4 %all_to_all.56 = f32[256,1,128]{2,1,0:T(1,128)S(1)} all-to-all(f32[256,1,128]{2,1,0:T(1,128)S(1)} %broadcast_in_dim.153), channel_id=1, replica_groups=mesh['thick'=8,'facade'=32] {'thick','facade'}, dimensions={0} | all-to-all | bytes 262144 | tf_op jit(solution)/shard_map/all_to_all | solution.py:216
  224.3 1.5 select_reduce_fusion.11
  227.9 18.4 %all_to_all.57 = f32[256,1,128]{2,1,0:T(1,128)S(1)} all-to-all(f32[256,1,128]{2,1,0:T(1,128)S(1)} %broadcast_in_dim.156), channel_id=1, replica_groups=mesh['thick'=8,'facade'=32] {'thick','facade'}, dimensions={0} | all-to-all | bytes 262144 | tf_op jit(solution)/shard_map/all_to_all | solution.py:216
  248.2 1.5 select_reduce_fusion.9
  251.7 18.4 %all_to_all.58 = f32[256,1,128]{2,1,0:T(1,128)S(1)} all-to-all(f32[256,1,128]{2,1,0:T(1,128)S(1)} %broadcast_in_dim.159), channel_id=1, replica_groups=mesh['thick'=8,'facade'=32] {'thick','facade'}, dimensions={0} | all-to-all | bytes 262144 | tf_op jit(solution)/shard_map/all_to_all | solution.py:216
  272.0 1.5 select_reduce_fusion.7
  275.6 18.6 %all_to_all.59 = f32[256,1,128]{2,1,0:T(1,128)S(1)} all-to-all(f32[256,1,128]{2,1,0:T(1,128)S(1)} %broadcast_in_dim.162), channel_id=1, replica_groups=mesh['thick'=8,'facade'=32] {'thick','facade'}, dimensions={0} | all-to-all | bytes 262144 | tf_op jit(solution)/shard_map/all_to_all | solution.py:216
  296.0 1.5 select_reduce_fusion.5
  299.6 18.4 %all_to_all.60 = f32[256,1,128]{2,1,0:T(1,128)S(1)} all-to-all(f32[256,1,128]{2,1,0:T(1,128)S(1)} %broadcast_in_dim.165), channel_id=1, replica_groups=mesh['thick'=8,'facade'=32] {'thick','facade'}, dimensions={0} | all-to-all | bytes 262144 | tf_op jit(solution)/shard_map/all_to_all | solution.py:216
  319.9 1.5 select_reduce_fusion.3
  323.4 18.4 %all_to_all.61 = f32[256,1,128]{2,1,0:T(1,128)S(1)} all-to-all(f32[256,1,128]{2,1,0:T(1,128)S(1)} %broadcast_in_dim.168), channel_id=1, replica_groups=mesh['thick'=8,'facade'=32] {'thick','facade'}, dimensions={0} | all-to-all | bytes 262144 | tf_op jit(solution)/shard_map/all_to_all | solution.py:216
  343.7 1.5 select_reduce_fusion.1
  347.1 18.4 %all_to_all.62 = f32[256,1,128]{2,1,0:T(1,128)S(1)} all-to-all(f32[256,1,128]{2,1,0:T(1,128)S(1)} %broadcast_in_dim.171), channel_id=1, replica_groups=mesh['thick'=8,'facade'=32] {'thick','facade'}, dimensions={0} | all-to-all | bytes 262144 | tf_op jit(solution)/shard_map/all_to_all | solution.py:216
  367.5 1.2 minimum_select_fusion
  (110 shorter events, 19.2 us)
Async XLA Ops:
  1.4 22.0 %collective-permute-start.8 = (f32[1,16,512]{2,1,0:T(8,128)S(1)}, f32[1,16,512]{2,1,0:T(8,128)S(1)}, u32[]{:S(2)}, u32[]{:S(2)}) collective-permute-start(f32[1,16,512]{2,1,0:T(8,128)S(1)} %get-tuple-element.63), channel_id=1, source_target_pairs={{32,0},{64,32},{96,64},{128,96},{160,128},{192,160},{224,192},{33,... | collective-permute-start | bytes 98312 | tf_op jit(solution)/shard_map/ppermute | solution.py:32
  2.7 11.8 %copy-start.4 = (f32[8,16,512]{2,1,0:T(8,128)S(1)}, f32[8,16,512]{2,1,0:T(8,128)}, u32[]{:S(2)}) copy-start(f32[8,16,512]{2,1,0:T(8,128)} %param.16) | copy-start | bytes 786436
  2.7 11.8 %collective-permute-start.9 = (f32[1,16,512]{2,1,0:T(8,128)S(1)}, f32[1,16,512]{2,1,0:T(8,128)S(1)}, u32[]{:S(2)}, u32[]{:S(2)}) collective-permute-start(f32[1,16,512]{2,1,0:T(8,128)S(1)} %get-tuple-element.64), channel_id=1, source_target_pairs={{0,32},{32,64},{64,96},{96,128},{128,160},{160,192},{192,224},{1,3... | collective-permute-start | bytes 98312 | tf_op jit(solution)/shard_map/ppermute | solution.py:31
  8.8 7.5 %collective-permute-start.1 = (f32[4,16,512]{2,1,0:T(8,128)S(1)}, f32[4,16,512]{2,1,0:T(8,128)S(1)}, u32[]{:S(2)}, u32[]{:S(2)}) collective-permute-start(f32[4,16,512]{2,1,0:T(8,128)S(1)} %get-tuple-element.65), channel_id=1, source_target_pairs={{32,0},{64,32},{96,64},{128,96},{160,128},{192,160},{224,192},{33,... | collective-permute-start | bytes 393224 | tf_op jit(solution)/shard_map/ppermute | solution.py:32
  10.1 6.1 %collective-permute-start = (f32[4,16,512]{2,1,0:T(8,128)S(1)}, f32[4,16,512]{2,1,0:T(8,128)S(1)}, u32[]{:S(2)}, u32[]{:S(2)}) collective-permute-start(f32[4,16,512]{2,1,0:T(8,128)S(1)} %get-tuple-element.66), channel_id=1, source_target_pairs={{0,32},{32,64},{64,96},{96,128},{128,160},{160,192},{192,224},{1,3... | collective-permute-start | bytes 393224 | tf_op jit(solution)/shard_map/ppermute | solution.py:31
  14.5 1.8 copy-start
  16.4 7.0 %collective-permute-start.2 = (f32[16,16,4]{2,1,0:T(8,128)S(1)}, f32[16,16,4]{2,1,0:T(8,128)S(1)}, u32[]{:S(2)}, u32[]{:S(2)}) collective-permute-start(f32[16,16,4]{2,1,0:T(8,128)S(1)} %get-tuple-element.45), channel_id=1, source_target_pairs={{0,1},{1,2},{2,3},{3,4},{4,5},{5,6},{6,7},{7,8},{8,9},{9,10},{10,1... | collective-permute-start | bytes 12296 | tf_op jit(solution)/shard_map/ppermute | solution.py:31
  21.4 6.3 %collective-permute-start.3 = (f32[16,16,4]{2,1,0:T(8,128)S(1)}, f32[16,16,4]{2,1,0:T(8,128)S(1)}, u32[]{:S(2)}, u32[]{:S(2)}) collective-permute-start(f32[16,16,4]{2,1,0:T(8,128)S(1)} %get-tuple-element.46), channel_id=1, source_target_pairs={{1,0},{2,1},{3,2},{4,3},{5,4},{6,5},{7,6},{8,7},{9,8},{10,9},{11,1... | collective-permute-start | bytes 12296 | tf_op jit(solution)/shard_map/ppermute | solution.py:32
  28.2 1.0 copy-start.6
  29.1 0.9 copy-start.5
  30.1 11.0 %collective-permute-start.4 = (f32[2,1,16,512]{3,2,1,0:T(8,128)S(1)}, f32[2,1,16,512]{3,2,1,0:T(8,128)S(1)}, u32[]{:S(2)}, u32[]{:S(2)}) collective-permute-start(f32[2,1,16,512]{3,2,1,0:T(8,128)S(1)} %get-tuple-element.43), channel_id=1, source_target_pairs={{0,32},{32,64},{64,96},{96,128},{128,160},{160,192},{192,224},{1,3... | collective-permute-start | bytes 196616 | tf_op jit(solution)/shard_map/ppermute | solution.py:31
  34.2 7.0 %collective-permute-start.5 = (f32[2,1,16,512]{3,2,1,0:T(8,128)S(1)}, f32[2,1,16,512]{3,2,1,0:T(8,128)S(1)}, u32[]{:S(2)}, u32[]{:S(2)}) collective-permute-start(f32[2,1,16,512]{3,2,1,0:T(8,128)S(1)} %get-tuple-element.44), channel_id=1, source_target_pairs={{32,0},{64,32},{96,64},{128,96},{160,128},{192,160},{224,192},{33,... | collective-permute-start | bytes 196616 | tf_op jit(solution)/shard_map/ppermute | solution.py:32
  35.6 10.1 %collective-permute-start.11 = (f32[10,16,1]{2,1,0:T(8,128)S(1)}, f32[10,16,1]{2,1,0:T(8,128)S(1)}, u32[]{:S(2)}, u32[]{:S(2)}) collective-permute-start(f32[10,16,1]{2,1,0:T(8,128)S(1)} %get-tuple-element.53), channel_id=1, source_target_pairs={{1,0},{2,1},{3,2},{4,3},{5,4},{6,5},{7,6},{8,7},{9,8},{10,9},{11,1... | collective-permute-start | bytes 1928 | tf_op jit(solution)/shard_map/ppermute | solution.py:32
  37.5 8.1 %collective-permute-start.10 = (f32[10,16,1]{2,1,0:T(8,128)S(1)}, f32[10,16,1]{2,1,0:T(8,128)S(1)}, u32[]{:S(2)}, u32[]{:S(2)}) collective-permute-start(f32[10,16,1]{2,1,0:T(8,128)S(1)} %get-tuple-element.54), channel_id=1, source_target_pairs={{0,1},{1,2},{2,3},{3,4},{4,5},{5,6},{6,7},{7,8},{8,9},{9,10},{10,1... | collective-permute-start | bytes 1928 | tf_op jit(solution)/shard_map/ppermute | solution.py:31
  41.3 4.6 %collective-permute-start.6 = (f32[2,10,16,1]{3,2,1,0:T(8,128)S(1)}, f32[2,10,16,1]{3,2,1,0:T(8,128)S(1)}, u32[]{:S(2)}, u32[]{:S(2)}) collective-permute-start(f32[2,10,16,1]{3,2,1,0:T(8,128)S(1)} %get-tuple-element.39), channel_id=1, source_target_pairs={{0,1},{1,2},{2,3},{3,4},{4,5},{5,6},{6,7},{7,8},{8,9},{9,10},{10,1... | collective-permute-start | bytes 3848 | tf_op jit(solution)/shard_map/ppermute | solution.py:31
  43.2 6.6 %collective-permute-start.7 = (f32[2,10,16,1]{3,2,1,0:T(8,128)S(1)}, f32[2,10,16,1]{3,2,1,0:T(8,128)S(1)}, u32[]{:S(2)}, u32[]{:S(2)}) collective-permute-start(f32[2,10,16,1]{3,2,1,0:T(8,128)S(1)} %get-tuple-element.40), channel_id=1, source_target_pairs={{1,0},{2,1},{3,2},{4,3},{5,4},{6,5},{7,6},{8,7},{9,8},{10,9},{11,1... | collective-permute-start | bytes 3848 | tf_op jit(solution)/shard_map/ppermute | solution.py:32
  50.2 1.0 copy-start.11
  52.0 6.1 %collective-permute-start.13 = (f32[1,16,512]{2,1,0:T(8,128)S(1)}, f32[1,16,512]{2,1,0:T(8,128)S(1)}, u32[]{:S(2)}, u32[]{:S(2)}) collective-permute-start(f32[1,16,512]{2,1,0:T(8,128)S(1)} %get-tuple-element.61), channel_id=1, source_target_pairs={{0,32},{32,64},{64,96},{96,128},{128,160},{160,192},{192,224},{1,3... | collective-permute-start | bytes 98312 | tf_op jit(solution)/shard_map/ppermute | solution.py:31
  56.8 6.5 %collective-permute-start.12 = (f32[1,16,512]{2,1,0:T(8,128)S(1)}, f32[1,16,512]{2,1,0:T(8,128)S(1)}, u32[]{:S(2)}, u32[]{:S(2)}) collective-permute-start(f32[1,16,512]{2,1,0:T(8,128)S(1)} %get-tuple-element.62), channel_id=1, source_target_pairs={{32,0},{64,32},{96,64},{128,96},{160,128},{192,160},{224,192},{33,... | collective-permute-start | bytes 98312 | tf_op jit(solution)/shard_map/ppermute | solution.py:32
  63.3 5.8 %collective-permute-start.15 = (f32[10,16,1]{2,1,0:T(8,128)S(1)}, f32[10,16,1]{2,1,0:T(8,128)S(1)}, u32[]{:S(2)}, u32[]{:S(2)}) collective-permute-start(f32[10,16,1]{2,1,0:T(8,128)S(1)} %get-tuple-element.51), channel_id=1, source_target_pairs={{1,0},{2,1},{3,2},{4,3},{5,4},{6,5},{7,6},{8,7},{9,8},{10,9},{11,1... | collective-permute-start | bytes 1928 | tf_op jit(solution)/shard_map/ppermute | solution.py:32
  65.3 5.1 %collective-permute-start.14 = (f32[10,16,1]{2,1,0:T(8,128)S(1)}, f32[10,16,1]{2,1,0:T(8,128)S(1)}, u32[]{:S(2)}, u32[]{:S(2)}) collective-permute-start(f32[10,16,1]{2,1,0:T(8,128)S(1)} %get-tuple-element.52), channel_id=1, source_target_pairs={{0,1},{1,2},{2,3},{3,4},{4,5},{5,6},{6,7},{7,8},{8,9},{9,10},{10,1... | collective-permute-start | bytes 1928 | tf_op jit(solution)/shard_map/ppermute | solution.py:31
  71.2 6.5 %collective-permute-start.17 = (f32[1,16,512]{2,1,0:T(8,128)S(1)}, f32[1,16,512]{2,1,0:T(8,128)S(1)}, u32[]{:S(2)}, u32[]{:S(2)}) collective-permute-start(f32[1,16,512]{2,1,0:T(8,128)S(1)} %get-tuple-element.59), channel_id=1, source_target_pairs={{0,32},{32,64},{64,96},{96,128},{128,160},{160,192},{192,224},{1,3... | collective-permute-start | bytes 98312 | tf_op jit(solution)/shard_map/ppermute | solution.py:31
  76.4 5.7 %collective-permute-start.16 = (f32[1,16,512]{2,1,0:T(8,128)S(1)}, f32[1,16,512]{2,1,0:T(8,128)S(1)}, u32[]{:S(2)}, u32[]{:S(2)}) collective-permute-start(f32[1,16,512]{2,1,0:T(8,128)S(1)} %get-tuple-element.60), channel_id=1, source_target_pairs={{32,0},{64,32},{96,64},{128,96},{160,128},{192,160},{224,192},{33,... | collective-permute-start | bytes 98312 | tf_op jit(solution)/shard_map/ppermute | solution.py:32
  82.1 7.6 %collective-permute-start.19 = (f32[10,16,1]{2,1,0:T(8,128)S(1)}, f32[10,16,1]{2,1,0:T(8,128)S(1)}, u32[]{:S(2)}, u32[]{:S(2)}) collective-permute-start(f32[10,16,1]{2,1,0:T(8,128)S(1)} %get-tuple-element.49), channel_id=1, source_target_pairs={{1,0},{2,1},{3,2},{4,3},{5,4},{6,5},{7,6},{8,7},{9,8},{10,9},{11,1... | collective-permute-start | bytes 1928 | tf_op jit(solution)/shard_map/ppermute | solution.py:32
  84.1 6.9 %collective-permute-start.18 = (f32[10,16,1]{2,1,0:T(8,128)S(1)}, f32[10,16,1]{2,1,0:T(8,128)S(1)}, u32[]{:S(2)}, u32[]{:S(2)}) collective-permute-start(f32[10,16,1]{2,1,0:T(8,128)S(1)} %get-tuple-element.50), channel_id=1, source_target_pairs={{0,1},{1,2},{2,3},{3,4},{4,5},{5,6},{6,7},{7,8},{8,9},{9,10},{10,1... | collective-permute-start | bytes 1928 | tf_op jit(solution)/shard_map/ppermute | solution.py:31
  92.2 18.7 %copy-start.3 = (f32[8,16,512]{2,1,0:T(8,128)}, f32[8,16,512]{2,1,0:T(8,128)S(1)}, u32[]{:S(2)}) copy-start(f32[8,16,512]{2,1,0:T(8,128)S(1)} %fusion.91) | copy-start | bytes 786436
  92.2 5.9 %collective-permute-start.21 = (f32[1,16,512]{2,1,0:T(8,128)S(1)}, f32[1,16,512]{2,1,0:T(8,128)S(1)}, u32[]{:S(2)}, u32[]{:S(2)}) collective-permute-start(f32[1,16,512]{2,1,0:T(8,128)S(1)} %get-tuple-element.57), channel_id=1, source_target_pairs={{0,32},{32,64},{64,96},{96,128},{128,160},{160,192},{192,224},{1,3... | collective-permute-start | bytes 98312 | tf_op jit(solution)/shard_map/ppermute | solution.py:31
  96.8 4.9 %collective-permute-start.20 = (f32[1,16,512]{2,1,0:T(8,128)S(1)}, f32[1,16,512]{2,1,0:T(8,128)S(1)}, u32[]{:S(2)}, u32[]{:S(2)}) collective-permute-start(f32[1,16,512]{2,1,0:T(8,128)S(1)} %get-tuple-element.58), channel_id=1, source_target_pairs={{32,0},{64,32},{96,64},{128,96},{160,128},{192,160},{224,192},{33,... | collective-permute-start | bytes 98312 | tf_op jit(solution)/shard_map/ppermute | solution.py:32
  101.8 7.6 %collective-permute-start.23 = (f32[10,16,1]{2,1,0:T(8,128)S(1)}, f32[10,16,1]{2,1,0:T(8,128)S(1)}, u32[]{:S(2)}, u32[]{:S(2)}) collective-permute-start(f32[10,16,1]{2,1,0:T(8,128)S(1)} %get-tuple-element.47), channel_id=1, source_target_pairs={{1,0},{2,1},{3,2},{4,3},{5,4},{6,5},{7,6},{8,7},{9,8},{10,9},{11,1... | collective-permute-start | bytes 1928 | tf_op jit(solution)/shard_map/ppermute | solution.py:32
  103.7 6.9 %collective-permute-start.22 = (f32[10,16,1]{2,1,0:T(8,128)S(1)}, f32[10,16,1]{2,1,0:T(8,128)S(1)}, u32[]{:S(2)}, u32[]{:S(2)}) collective-permute-start(f32[10,16,1]{2,1,0:T(8,128)S(1)} %get-tuple-element.48), channel_id=1, source_target_pairs={{0,1},{1,2},{2,3},{3,4},{4,5},{5,6},{6,7},{7,8},{8,9},{9,10},{10,1... | collective-permute-start | bytes 1928 | tf_op jit(solution)/shard_map/ppermute | solution.py:31
  112.2 5.6 %collective-permute-start.24 = (f32[4,16,512]{2,1,0:T(8,128)S(1)}, f32[4,16,512]{2,1,0:T(8,128)S(1)}, u32[]{:S(2)}, u32[]{:S(2)}) collective-permute-start(f32[4,16,512]{2,1,0:T(8,128)S(1)} %get-tuple-element.55), channel_id=1, source_target_pairs={{0,32},{32,64},{64,96},{96,128},{128,160},{160,192},{192,224},{1,3... | collective-permute-start | bytes 393224 | tf_op jit(solution)/shard_map/ppermute | solution.py:31
  115.8 5.7 %collective-permute-start.25 = (f32[4,16,512]{2,1,0:T(8,128)S(1)}, f32[4,16,512]{2,1,0:T(8,128)S(1)}, u32[]{:S(2)}, u32[]{:S(2)}) collective-permute-start(f32[4,16,512]{2,1,0:T(8,128)S(1)} %get-tuple-element.56), channel_id=1, source_target_pairs={{32,0},{64,32},{96,64},{128,96},{160,128},{192,160},{224,192},{33,... | collective-permute-start | bytes 393224 | tf_op jit(solution)/shard_map/ppermute | solution.py:32
  121.6 7.8 %collective-permute-start.26 = (f32[16,16,4]{2,1,0:T(8,128)S(1)}, f32[16,16,4]{2,1,0:T(8,128)S(1)}, u32[]{:S(2)}, u32[]{:S(2)}) collective-permute-start(f32[16,16,4]{2,1,0:T(8,128)S(1)} %get-tuple-element.41), channel_id=1, source_target_pairs={{0,1},{1,2},{2,3},{3,4},{4,5},{5,6},{6,7},{7,8},{8,9},{9,10},{10,1... | collective-permute-start | bytes 12296 | tf_op jit(solution)/shard_map/ppermute | solution.py:31
  127.5 6.3 %collective-permute-start.27 = (f32[16,16,4]{2,1,0:T(8,128)S(1)}, f32[16,16,4]{2,1,0:T(8,128)S(1)}, u32[]{:S(2)}, u32[]{:S(2)}) collective-permute-start(f32[16,16,4]{2,1,0:T(8,128)S(1)} %get-tuple-element.42), channel_id=1, source_target_pairs={{1,0},{2,1},{3,2},{4,3},{5,4},{6,5},{7,6},{8,7},{9,8},{10,9},{11,1... | collective-permute-start | bytes 12296 | tf_op jit(solution)/shard_map/ppermute | solution.py:32
  134.5 41.9 %copy-start.9 = (f32[8,16,512]{2,1,0:T(8,128)S(1)}, f32[8,16,512]{2,1,0:T(8,128)}, u32[]{:S(2)}) copy-start(f32[8,16,512]{2,1,0:T(8,128)} %param.10) | copy-start | bytes 786436
  134.5 41.9 %copy-start.10 = (f32[8,16,512]{2,1,0:T(8,128)S(1)}, f32[8,16,512]{2,1,0:T(8,128)}, u32[]{:S(2)}) copy-start(f32[8,16,512]{2,1,0:T(8,128)} %param.12) | copy-start | bytes 786436
  135.7 40.7 %copy-start.7 = (f32[8,16,512]{2,1,0:T(8,128)S(1)}, f32[8,16,512]{2,1,0:T(8,128)}, u32[]{:S(2)}) copy-start(f32[8,16,512]{2,1,0:T(8,128)} %param.13) | copy-start | bytes 786436
  135.7 40.7 %copy-start.8 = (f32[8,16,512]{2,1,0:T(8,128)S(1)}, f32[8,16,512]{2,1,0:T(8,128)}, u32[]{:S(2)}) copy-start(f32[8,16,512]{2,1,0:T(8,128)} %param.11) | copy-start | bytes 786436
  178.3 189.3 %copy-start.1 = (f32[8,16,512]{2,1,0:T(8,128)}, f32[8,16,512]{2,1,0:T(8,128)S(1)}, u32[]{:S(2)}) copy-start(f32[8,16,512]{2,1,0:T(8,128)S(1)} %get-tuple-element.22) | copy-start | bytes 786436
  178.3 189.3 %copy-start.2 = (f32[8,16,512]{2,1,0:T(8,128)}, f32[8,16,512]{2,1,0:T(8,128)S(1)}, u32[]{:S(2)}) copy-start(f32[8,16,512]{2,1,0:T(8,128)S(1)} %get-tuple-element.23) | copy-start | bytes 786436

commit v2 on v0

v2 whole, which is shorter than its diff:
```python
import functools
import jax
import jax.numpy as jnp
from jax import lax
from jax.experimental import pallas as pl
from jax.experimental.pallas import tpu as pltpu
from jax.sharding import PartitionSpec as P

RADIUS = 4
SWEEPS = 3
NEWTON = 8

k_void = 0.03
k_frame = 160.0
k_glass = 1.0
k_anchor = 50.0
loss_rate = 0.05
spectrum_low = 0.05
spectrum_high = 2.0
solid_allowance = 0.35
curve_floor = 0.05
move_limit = 0.2
gamma_slope = 200.0

LANES = 128
STRIP = 16
above_weight = 1.001 + 1e-05
below_weight = 0.001 + 1e-05

f32 = jnp.float32
AXES = ("thick", "facade")
BOTH_SIDES = 16


def call(kernel, outs, args, scratch=()):
    vmem = pl.BlockSpec(memory_space=pltpu.VMEM)
    return pl.pallas_call(
        kernel,
        out_shape=[jax.ShapeDtypeStruct(shape, f32) for shape in outs],
        in_specs=[vmem] * len(args),
        out_specs=[vmem] * len(outs),
        scratch_shapes=[pltpu.VMEM(shape, f32) for shape in scratch],
        compiler_params=pltpu.CompilerParams(vmem_limit_bytes=40 * 1024 * 1024),
    )(*args)


def lane_iota(shape):
    return lax.broadcasted_iota(jnp.int32, shape, len(shape) - 1)


def sub_iota(shape):
    return lax.broadcasted_iota(jnp.int32, shape, len(shape) - 2)


def ahead(value, step, axis):
    return pltpu.roll(value, (value.shape[axis] - step) % value.shape[axis], axis)


def behind(value, step, axis):
    return pltpu.roll(value, step, axis)


def pack_kernel(*refs):
    firsts, lasts, to_left, to_right = refs[0:5], refs[5:10], refs[10], refs[11]
    rows, height, _ = to_left.shape
    group = lane_iota((height, LANES)) // STRIP
    for row in range(rows):
        for source, target, place in ((firsts, to_left, 0), (lasts, to_right, LANES - STRIP)):
            packed = jnp.zeros((height, LANES), f32)
            for index, ref in enumerate(source):
                value = ref[row]
                if value.dtype != f32:
                    value = value.astype(f32) + 1.0
                shift = (STRIP * index - place) % LANES
                if shift:
                    value = pltpu.roll(value, shift, 1)
                packed = jnp.where(group == index, value, packed)
            target[row] = packed


def halo_lanes(left, right, index):
    lane = lane_iota(left.shape)
    shift = (LANES - STRIP * index) % LANES
    after = pltpu.roll(right, shift, 1) if shift else right
    shift = (LANES - STRIP - STRIP * index) % LANES
    before = pltpu.roll(left, shift, 1) if shift else left
    return jnp.where(lane < STRIP, after, jnp.where(lane >= LANES - STRIP, before, 0.0))


def axis_weight(position, total):
    acc = jnp.zeros(position.shape, f32)
    for offset in range(-RADIUS, RADIUS + 1):
        weight = float(RADIUS + 1 - abs(offset))
        inside = (position + offset >= 0) & (position + offset < total)
        acc = acc + jnp.where(inside, weight, 0.0)
    return jnp.maximum(acc, 1.0)


def inverse_plane(height, own, cols_total, col_start):
    width = own + LANES
    lane = lane_iota((1, width))
    place = jnp.where(lane < own + LANES // 2, lane, lane - width) + col_start
    middle = axis_weight(sub_iota((height, 1)), height)
    return 1.0 / (middle * axis_weight(place, cols_total))


def row_weight(row, rows_total, row_start):
    return 1.0 / axis_weight(jnp.full((1, 1), row + row_start, jnp.int32), rows_total)


def boxes(values):
    pairs = [a + b for a, b in zip(values[:-1], values[1:])]
    fours = [a + b for a, b in zip(pairs[:-2], pairs[2:])]
    return [a + b for a, b in zip(fours, values[4:])]


def filter_depth(get, put, count):
    singles = [get(r) for r in range(count)]
    return boxes(boxes(singles))


def filter_height(value):
    height = value.shape[0]
    level = sub_iota((height, 1))
    total = float(RADIUS + 1) * value
    for offset in range(1, RADIUS + 1):
        weight = float(RADIUS + 1 - offset)
        up = jnp.where(level < height - offset, weight, 0.0)
        down = jnp.where(level >= offset, weight, 0.0)
        total = total + up * ahead(value, offset, 0) + down * behind(value, offset, 0)
    return total


def filter_lanes(value):
    def box(v):
        pair = v + ahead(v, 1, 1)
        return pair + ahead(pair, 2, 1) + behind(v, 1, 1)

    def box_back(v):
        pair = v + behind(v, 1, 1)
        return pair + behind(pair, 2, 1) + ahead(v, 1, 1)

    return box_back(box(value))


def depth_filter(source, middle, target):
    count = source.shape[0]
    for r in range(count - 4):
        middle[r] = (source[r] + source[r + 1]) + (source[r + 2] + source[r + 3]) + source[r + 4]
    for r in range(count - 8):
        target[r] = (middle[r] + middle[r + 1]) + (middle[r + 2] + middle[r + 3]) + middle[r + 4]


def rho_kernel(
    rows_total, cols_total, place,
    density, material, from_above, from_below, left, right, corner_above, corner_below,
    rho_out, cond_first, cond_last,
    ext, middle, summed,
):
    rows, height, own = density.shape
    for r in range(4):
        ext[r, :, :own] = from_above[r]
        ext[r, :, own:] = halo_lanes(corner_above[r], corner_above[4 + r], 0)
        ext[rows + 4 + r, :, :own] = from_below[r]
        ext[rows + 4 + r, :, own:] = halo_lanes(corner_below[r], corner_below[4 + r], 0)
    for r in range(rows):
        ext[4 + r, :, :own] = density[r]
        ext[4 + r, :, own:] = halo_lanes(left[r], right[r], 0)
    depth_filter(ext, middle, summed)
    row_start = place[0]
    plane = inverse_plane(height, own, cols_total, place[1])
    for r in range(rows):
        rho = filter_lanes(filter_height(summed[r])) * (
            plane * row_weight(r, rows_total, row_start)
        )
        code = jnp.concatenate(
            [material[r].astype(f32) + 1.0, halo_lanes(left[r], right[r], 1)], axis=1
        )
        frame = k_void + (k_frame - k_void) * rho * rho * rho
        cond = jnp.where(code == 2.0, frame, jnp.where(code == 1.0, k_glass, k_anchor))
        cond = jnp.where(code == 0.0, 0.0, cond)
        rho_out[r] = rho
        if r < 4:
            cond_first[r] = cond
        else:
            cond_last[r - 4] = cond


def sweep_kernel(
    rows_total, cols_total, place,
    cond_above, cond_first, cond_last, cond_below, rho, material,
    prior, source, temp, rows_above, rows_below, left, right, corner_above, corner_below,
    dual_out, weighted_first, weighted_last,
    cond, field, load, heat, depth_face, height_face, lane_face, inverse, residual, next_field, dual,
):
    rows, height, own = prior.shape
    width = own + LANES
    last_level = sub_iota((height, 1)) == height - 1
    for r in range(4):
        cond[r] = cond_above[r]
        cond[4 + r] = cond_first[r]
        cond[8 + r] = cond_last[r]
        cond[12 + r] = cond_below[r]
    for r in range(4):
        field[r, :, :own] = rows_above[r]
        field[r, :, own:] = halo_lanes(corner_above[r], corner_above[4 + r], 3)
        field[12 + r, :, :own] = rows_below[r]
        field[12 + r, :, own:] = halo_lanes(corner_below[r], corner_below[4 + r], 3)
    for r in range(3):
        load[1 + r, :, :own] = rows_above[4 + r]
        load[1 + r, :, own:] = halo_lanes(corner_above[1 + r], corner_above[5 + r], 2)
        load[12 + r, :, :own] = rows_below[4 + r]
        load[12 + r, :, own:] = halo_lanes(corner_below[r], corner_below[4 + r], 2)
    heat[0, :, :own] = rows_above[7]
    heat[0, :, own:] = halo_lanes(corner_above[3], corner_above[7], 4)
    heat[9, :, :own] = rows_below[7]
    heat[9, :, own:] = halo_lanes(corner_below[0], corner_below[4], 4)
    for r in range(rows):
        field[4 + r, :, :own] = prior[r]
        field[4 + r, :, own:] = halo_lanes(left[r], right[r], 3)
        load[4 + r, :, :own] = source[r]
        load[4 + r, :, own:] = halo_lanes(left[r], right[r], 2)
        heat[1 + r, :, :own] = temp[r]
        heat[1 + r, :, own:] = halo_lanes(left[r], right[r], 4)

    def face(one, other):
        return 2.0 * one * other / jnp.maximum(one + other, 1e-3)

    depth_face[0] = face(cond[0], cond[1])

    def make_faces(r, carry):
        here = cond[r]
        deep = face(here, cond[r + 1])
        tall = jnp.where(last_level, 0.0, face(here, ahead(here, 1, 0)))
        wide = face(here, ahead(here, 1, 1))
        depth_face[r] = deep
        height_face[r] = tall
        lane_face[r] = wide
        diagonal = (
            loss_rate + (deep + depth_face[r - 1]) + (tall + behind(tall, 1, 0))
            + (wide + behind(wide, 1, 1))
        )
        inverse[r] = 1.0 / diagonal
        return carry

    lax.fori_loop(1, 15, make_faces, 0)

    def product(ref, r):
        here = ref[r]
        deep = depth_face[r] * (here - ref[r + 1]) + depth_face[r - 1] * (here - ref[r - 1])
        tall = height_face[r] * (here - ahead(here, 1, 0))
        wide = lane_face[r] * (here - ahead(here, 1, 1))
        return (
            loss_rate * here + deep + (tall - behind(tall, 1, 0)) + (wide - behind(wide, 1, 1))
        )

    centre = 0.5 * (spectrum_high + spectrum_low)
    half = 0.5 * (spectrum_high - spectrum_low)
    ratio = centre / half

    def begin(r, carry):
        left_over = load[r] - product(field, r)
        residual[r] = left_over
        direction = left_over * inverse[r] * (1.0 / centre)
        next_field[r] = direction
        dual[r] = field[r] + direction
        return carry

    lax.fori_loop(1, 15, begin, 0)
    factor = 1.0 / ratio
    now, then = next_field, field
    for sweep in range(SWEEPS - 1):
        factor_next = 1.0 / (2.0 * ratio - factor)
        keep, add = factor_next * factor, 2.0 * factor_next / half

        def step(r, carry, now=now, then=then, keep=keep, add=add):
            left_over = residual[r] - product(now, r)
            residual[r] = left_over
            direction = keep * now[r] + add * (left_over * inverse[r])
            then[r] = direction
            dual[r] = dual[r] + direction
            return carry

        lax.fori_loop(2 + sweep, 14 - sweep, step, 0)
        factor = factor_next
        now, then = then, now

    row_start = place[0]
    plane = inverse_plane(height, own, cols_total, place[1])
    for r in range(rows):
        dual_out[r] = dual[4 + r, :, :own]

    def sens(r, deep_before):
        c, a, t = cond[r], dual[r], heat[r - 3]

        def shared(c_q, a_q, t_q):
            inv = 1.0 / jnp.maximum(c + c_q, 1e-3)
            return (a - a_q) * (t - t_q) * (inv * inv)

        c_q = cond[r + 1]
        deep = shared(c_q, dual[r + 1], heat[r - 2])
        c_sq = c * c
        total = deep * (c_q * c_q)
        deep_next = deep * c_sq
        c_q = ahead(c, 1, 0)
        tall = jnp.where(last_level, 0.0, shared(c_q, ahead(a, 1, 0), ahead(t, 1, 0)))
        total = total + tall * (c_q * c_q) + behind(tall * c_sq, 1, 0)
        c_q = ahead(c, 1, 1)
        wide = shared(c_q, ahead(a, 1, 1), ahead(t, 1, 1))
        total = total + wide * (c_q * c_q) + behind(wide * c_sq, 1, 1)
        return -2.0 * (total + deep_before), deep_next

    c, c_q = cond[3], cond[4]
    inv = 1.0 / jnp.maximum(c + c_q, 1e-3)
    deep_before = (dual[3] - dual[4]) * (heat[0] - heat[1]) * (inv * inv) * (c * c)
    for r in range(rows):
        value, deep_before = sens(4 + r, deep_before)
        code = jnp.concatenate(
            [material[r].astype(f32) + 1.0, halo_lanes(left[r], right[r], 1)], axis=1
        )
        squared = rho[r] * rho[r]
        value = value * (3.0 * (k_frame - k_void)) * squared * (
            plane * row_weight(r, rows_total, row_start)
        )
        value = jnp.where(code == 2.0, value, 0.0)
        if r < 4:
            weighted_first[r] = value
        else:
            weighted_last[r - 4] = value


def grad_kernel(from_above, first, last, from_below, material, grad_out, message, ext, middle, summed):
    rows, height, own = grad_out.shape
    for r in range(4):
        ext[r] = from_above[r]
        ext[4 + r] = first[r]
        ext[8 + r] = last[r]
        ext[12 + r] = from_below[r]
    depth_filter(ext, middle, summed)
    largest = jnp.zeros((height, LANES), f32)
    for r in range(rows):
        grad = filter_lanes(filter_height(summed[r]))[:, :own]
        grad_out[r] = grad
        size = jnp.where(material[r] == 1, jnp.abs(grad), 0.0)
        for block in range(own // LANES):
            largest = jnp.maximum(largest, size[:, block * LANES:(block + 1) * LANES])
    message[...] = jnp.broadcast_to(jnp.max(largest, axis=0, keepdims=True), message.shape)


def lines_kernel(
    solid, newer, older, below_spacing, above_spacing, material,
    below_out, above_out, up_out, low_out, least_out, most_out, upper_out, lower_out, bend_out,
    tallies,
):
    rows, height, own = solid.shape
    base = jnp.zeros((height, LANES), f32)
    count = jnp.zeros((height, LANES), f32)
    for r in range(rows):
        x = solid[r]
        design = material[r] == 1
        gamma = 0.95 + 0.25 * jnp.tanh(gamma_slope * newer[r] * older[r])
        below = x - gamma * below_spacing[r]
        above = x + gamma * above_spacing[r]
        below_out[r] = below
        above_out[r] = above
        up = above - x
        low = x - below
        floor = jnp.maximum(jnp.maximum(0.0, below + 0.1 * low), x - move_limit)
        ceiling = jnp.minimum(jnp.minimum(1.0, above - 0.1 * up), x + move_limit)
        up_out[r] = up
        low_out[r] = low
        least_out[r] = floor - below
        most_out[r] = ceiling - below
        upper_out[r] = jnp.where(design, above_weight * up * up, 0.0)
        lower_out[r] = jnp.where(design, below_weight * low * low, 0.0)
        bend_out[r] = jnp.where(design, up * low / (2.0 * (up + low)), 0.0)
        term = jnp.where(
            design, x - solid_allowance - above_weight * up - below_weight * low, 0.0
        )
        one = jnp.where(design, curve_floor, 0.0)
        for block in range(own // LANES):
            base = base + term[:, block * LANES:(block + 1) * LANES]
            count = count + one[:, block * LANES:(block + 1) * LANES]
    tallies[0] = base
    tallies[1] = count


def reached(rate_above, rate_below, y, up, low, least, most):
    root_above = rate_above + y * above_weight
    root_below = rate_below + y * below_weight
    inv_above, inv_below = lax.rsqrt(root_above), lax.rsqrt(root_below)
    root_above, root_below = root_above * inv_above, root_below * inv_below
    width = up + low
    pull = low * root_below
    trial = width * pull / (up * root_above + pull)
    return trial, jnp.clip(trial, least, most), width, root_above, root_below, inv_above, inv_below


def sums_to_message(slope, curve, message):
    slope = jnp.sum(slope, axis=0, keepdims=True)
    curve = jnp.sum(curve, axis=0, keepdims=True)
    slope = slope + pltpu.roll(slope, LANES // 2, 1)
    curve = curve + pltpu.roll(curve, LANES // 2, 1)
    lane = lane_iota((1, LANES))
    message[...] = jnp.broadcast_to(jnp.where(lane < LANES // 2, slope, curve), message.shape)


def evaluate(y, rate_above, rate_below, up, low, least, most, upper, lower, bend, tallies, message):
    rows, height, own = up.shape
    slope_sum, curve_sum = tallies[0], tallies[1]
    for r in range(rows):
        trial, chosen, width, root_above, root_below, inv_above, inv_below = reached(
            rate_above(r), rate_below(r), y, up[r], low[r], least[r], most[r]
        )
        rest = width - chosen
        slope = (upper[r] * chosen + lower[r] * rest) / (rest * chosen)
        split = above_weight * (inv_above * inv_above) - below_weight * (inv_below * inv_below)
        curve = bend[r] * (root_above * root_below) * (split * split)
        free = (trial > least[r]) & (trial < most[r])
        curve = jnp.where(free, curve, 0.0)
        for block in range(own // LANES):
            slope_sum = slope_sum + slope[:, block * LANES:(block + 1) * LANES]
            curve_sum = curve_sum + curve[:, block * LANES:(block + 1) * LANES]
    sums_to_message(slope_sum, curve_sum, message)


def first_kernel(
    arrived, grad, up, low, least, most, upper, lower, bend, tallies,
    message, rate_above_out, rate_below_out,
):
    scale = jnp.max(jnp.max(arrived[...], axis=0, keepdims=True), axis=1, keepdims=True)
    inverse = 1.0 / (scale + 1e-06)

    def above(r):
        element = grad[r] * inverse
        value = jnp.maximum(1.001 * element, -0.001 * element) + 1e-05
        rate_above_out[r] = value
        return value

    def below(r):
        element = grad[r] * inverse
        value = jnp.maximum(0.001 * element, -1.001 * element) + 1e-05
        rate_below_out[r] = value
        return value

    evaluate(
        jnp.ones((1, 1), f32), above, below, up, low, least, most, upper, lower, bend, tallies, message
    )


def advance(arrived, y):
    total = jnp.sum(arrived[...], axis=0, keepdims=True)
    lane = lane_iota(total.shape)
    slope = jnp.sum(jnp.where(lane < LANES // 2, total, 0.0), axis=1, keepdims=True)
    curve = jnp.sum(jnp.where(lane < LANES // 2, 0.0, total), axis=1, keepdims=True)
    return jnp.maximum(0.0, y + slope / curve)


def step_kernel(
    arrived, y_ref, rate_above, rate_below, up, low, least, most, upper, lower, bend, tallies,
    message, y_out,
):
    y = advance(arrived, y_ref[0:1, 0:1])
    y_out[...] = jnp.broadcast_to(y, y_out.shape)
    evaluate(
        y, lambda r: rate_above[r], lambda r: rate_below[r],
        up, low, least, most, upper, lower, bend, tallies, message,
    )


def last_kernel(
    arrived, y_ref, rate_above, rate_below, up, low, least, most, below, solid, material, out
):
    y = advance(arrived, y_ref[0:1, 0:1])
    for r in range(out.shape[0]):
        chosen = reached(rate_above[r], rate_below[r], y, up[r], low[r], least[r], most[r])[1]
        out[r] = jnp.where(material[r] == 1, below[r] + chosen, solid[r])


def with_place(kernel, rows_total, cols_total):
    def body(place_ref, *refs):
        kernel(rows_total, cols_total, (place_ref[0], place_ref[1]), *refs)

    return body


def placed_call(kernel, place, outs, args, scratch, totals):
    vmem = pl.BlockSpec(memory_space=pltpu.VMEM)
    return pl.pallas_call(
        with_place(kernel, *totals),
        out_shape=[jax.ShapeDtypeStruct(shape, f32) for shape in outs],
        in_specs=[pl.BlockSpec(memory_space=pltpu.SMEM)] + [vmem] * len(args),
        out_specs=[vmem] * len(outs),
        scratch_shapes=[pltpu.VMEM(shape, f32) for shape in scratch],
        compiler_params=pltpu.CompilerParams(vmem_limit_bytes=40 * 1024 * 1024),
    )(place, *args)


def pack_strips(arrays):
    rows, height, own = arrays[0].shape
    end = own // LANES - 1
    block = (rows, height, LANES)
    first = pl.BlockSpec(block, lambda i: (0, 0, 0))
    last = pl.BlockSpec(block, lambda i: (0, 0, end))
    out = pl.BlockSpec(block, lambda i: (0, 0, 0))
    return pl.pallas_call(
        pack_kernel,
        grid=(1,),
        out_shape=[jax.ShapeDtypeStruct(block, f32)] * 2,
        in_specs=[first] * 5 + [last] * 5,
        out_specs=[out] * 2,
    )(*arrays, *arrays)


def on_device(
    solid_occupancy,
    newer_occupancy_shift,
    older_occupancy_shift,
    below_limit_spacing,
    above_limit_spacing,
    thermal_state,
    loss_state_derivative,
    prior_dual_state,
    cell_material,
):
    rows, height, own = solid_occupancy.shape
    deep, long = lax.axis_size("thick"), lax.axis_size("facade")
    totals = (rows * deep, own * long)
    place = jnp.stack(
        [lax.axis_index("thick") * rows, lax.axis_index("facade") * own]
    ).astype(jnp.int32)
    width = own + LANES
    whole = (rows, height, own)

    def shift(axis, size, step):
        pairs = [(i, i + step) for i in range(size) if 0 <= i + step < size]
        return lambda value: lax.ppermute(value, axis, pairs)

    to_right, to_left = shift("facade", long, 1), shift("facade", long, -1)
    to_deeper, to_nearer = shift("thick", deep, 1), shift("thick", deep, -1)

    first_strips, last_strips = pack_strips(
        (solid_occupancy, cell_material, loss_state_derivative, prior_dual_state, thermal_state)
    )
    right, left = to_left(first_strips), to_right(last_strips)
    density_above, density_below = (
        to_deeper(solid_occupancy[rows - 4:]),
        to_nearer(solid_occupancy[:4]),
    )
    rows_above = to_deeper(
        jnp.concatenate(
            [prior_dual_state[rows - 4:], loss_state_derivative[rows - 3:], thermal_state[rows - 1:]]
        )
    )
    rows_below = to_nearer(
        jnp.concatenate([prior_dual_state[:4], loss_state_derivative[:3], thermal_state[:1]])
    )
    corner_above = to_deeper(jnp.concatenate([left[rows - 4:], right[rows - 4:]]))
    corner_below = to_nearer(jnp.concatenate([left[:4], right[:4]]))

    (below, above, up, low, least, most, upper, lower, bend, tallies) = call(
        lines_kernel,
        [whole] * 9 + [(2, height, LANES)],
        (
            solid_occupancy, newer_occupancy_shift, older_occupancy_shift,
            below_limit_spacing, above_limit_spacing, cell_material,
        ),
    )

    four = (4, height, width)
    rho, cond_first, cond_last = placed_call(
        rho_kernel, place,
        [(rows, height, width), four, four],
        (
            solid_occupancy, cell_material, density_above, density_below, left, right,
            corner_above, corner_below,
        ),
        [(BOTH_SIDES, height, width), (BOTH_SIDES - 4, height, width), (rows, height, width)],
        totals,
    )
    cond_above, cond_below = to_deeper(cond_last), to_nearer(cond_first)
    tall = (BOTH_SIDES, height, width)
    dual_state, weighted_first, weighted_last = placed_call(
        sweep_kernel, place,
        [whole, four, four],
        (
            cond_above, cond_first, cond_last, cond_below, rho, cell_material,
            prior_dual_state, loss_state_derivative, thermal_state, rows_above, rows_below,
            left, right, corner_above, corner_below,
        ),
        [tall, tall, tall, (10, height, width)] + [tall] * 7,
        totals,
    )
    weighted_above, weighted_below = to_deeper(weighted_last), to_nearer(weighted_first)
    count = deep * long
    note = (count, LANES)
    grad, message = call(
        grad_kernel,
        [whole, note],
        (weighted_above, weighted_first, weighted_last, weighted_below, cell_material),
        [tall, (BOTH_SIDES - 4, height, width), (rows, height, width)],
    )

    def everyone(rows_out):
        return lax.all_to_all(rows_out, AXES, 0, 0, tiled=True)

    fixed = (up, low, least, most, upper, lower, bend, tallies)
    message, rate_above, rate_below = call(
        first_kernel, [note, whole, whole], (everyone(message), grad) + fixed
    )
    y = jnp.ones((8, LANES), f32)
    for _ in range(NEWTON - 1):
        message, y = call(
            step_kernel, [note, (8, LANES)],
            (everyone(message), y, rate_above, rate_below) + fixed,
        )
    (density_new,) = call(
        last_kernel, [whole],
        (
            everyone(message), y, rate_above, rate_below, up, low, least, most, below,
            solid_occupancy, cell_material,
        ),
    )
    return (density_new, below, above, dual_state)


def solution(mesh):
    spec = P("thick", None, "facade")
    return jax.shard_map(
        on_device,
        mesh=mesh,
        in_specs=(spec,) * 9,
        out_specs=(spec,) * 4,
        check_vma=False,
    )
```

time: 855 us -> 256 us (0.30)
  blocking collectives: 683 us -> 147 us
  starting transfers between devices: 85.4 us -> 51.9 us
  Pallas kernels: 0 us -> 23.3 us
  other arithmetic: 22.2 us -> 0.13 us
  between operations: 22.2 us -> 1 us
    psum x8 -> x0, blocking collectives: 591 us -> none  [dual_reduce(): return lax.psum((slope_part, curve_part), ('thick', 'facade'))]
    all_to_all x0 -> x8, blocking collectives: none -> 147 us  [everyone(): return lax.all_to_all(rows_out, AXES, 0, 0, tiled=True)]
    pmax x1 -> x0, blocking collectives: 91.8 us -> none  [on_device(): lax.pmax(jnp.max(jnp.where(layout_candidate, jnp.abs(grad), 0.0)), ('thic...]
    ppermute x28 -> x12, starting transfers between devices: 85.4 us -> 34.8 us  [shift(): return lambda value: lax.ppermute(value, axis, pairs)]
    pallas_call x0 -> x14, Pallas kernels: none -> 23.3 us  [the longest x2 12.6 us: placed_call(): pl.pallas_call(with_place(kernel, *totals), out_shape=[jax.ShapeDtypeStru...]
    ppermute x28 -> x12, waiting for transfers between devices: 36.3 us -> 18.4 us  [shift(): return lambda value: lax.ppermute(value, axis, pairs)]
    all_to_all x0 -> x1, starting transfers between devices: none -> 17.1 us  [everyone(): return lax.all_to_all(rows_out, AXES, 0, 0, tiled=True)]
    reduce_sum x8 -> x0, other arithmetic: 12.1 us -> none  [on_device(): jnp.sum(jnp.where(layout_candidate, h_terms, 0.0))]
  transfers between devices with their start and end apart: 28 -> 13, of which waited for: 15 -> 7; matrix products, arithmetic and copies ran while one was open for 0% -> 0% of each run, Pallas kernels for 0% -> 1%
where the time goes in v2:
time: 256 us; the launch traced here: 255 us
  blocking collectives  147 us (57%)
  starting transfers between devices  51.9 us (20%)
  waiting for transfers between devices  29.4 us (11%)
  Pallas kernels  23.3 us (9%)
    all_to_all x8, blocking collectives, everyone(): return lax.all_to_all(rows_out, AXES, 0, 0, tiled=True)  147 us
    ppermute x12, starting transfers between devices, shift(): return lambda value: lax.ppermute(value, axis, pairs)  34.8 us
    ppermute x12, waiting for transfers between devices, shift(): return lambda value: lax.ppermute(value, axis, pairs)  18.4 us
    all_to_all x1, starting transfers between devices, everyone(): return lax.all_to_all(rows_out, AXES, 0, 0, tiled=True)  17.1 us
    pallas_call x2, Pallas kernels, placed_call(): pl.pallas_call(with_place(kernel, *totals), out_shape=[jax.ShapeDtypeStru...  12.6 us
    all_to_all x1, waiting for transfers between devices, everyone(): return lax.all_to_all(rows_out, AXES, 0, 0, tiled=True)  11 us
    pallas_call x11, Pallas kernels, call(): pl.pallas_call(kernel, out_shape=[jax.ShapeDtypeStruct(shape, f32) for sh...  8.64 us
  transfers between devices with their start and end apart: 13, of which 7 were waited for; matrix products, arithmetic and copies ran while one was open for 0% of the time, Pallas kernels for 1%

profile of v2, /device:TPU:1, one launch (start us, length us, event | category | flops | bytes accessed | tf_op | source)
XLA Modules:
  0.0 254.9 jit_solution(17237964872761183216)
XLA Ops:
  0.6 0.0 copy-start.1
  0.6 2.0 shard_map.120
  2.7 4.5 %collective-permute-start.2 = (f32[8,16,128]{2,1,0:T(8,128)}, f32[8,16,128]{2,1,0:T(8,128)S(1)}, u32[]{:S(2)}, u32[]{:S(2)}) collective-permute-start(f32[8,16,128]{2,1,0:T(8,128)} %get-tuple-element.41), channel_id=1, source_target_pairs={{0,1},{1,2},{2,3},{3,4},{4,5},{5,6},{6,7},{7,8},{8,9},{9,10},{10,1... | collective-permute-start | bytes 196616 | tf_op jit(solution)/shard_map/ppermute | solution.py:537
  7.2 0.0 copy-start.2
  7.2 2.1 collective-permute-start.3
  9.3 0.0 copy-done.1
  9.3 3.5 %collective-permute-start = (f32[4,16,512]{2,1,0:T(8,128)S(1)}, f32[4,16,512]{2,1,0:T(8,128)S(1)}, u32[]{:S(2)}, u32[]{:S(2)}) collective-permute-start(f32[4,16,512]{2,1,0:T(8,128)S(1)} %get-tuple-element.85), channel_id=1, source_target_pairs={{0,32},{32,64},{64,96},{96,128},{128,160},{160,192},{192,224},{1,3... | collective-permute-start | bytes 393224 | tf_op jit(solution)/shard_map/ppermute | solution.py:537
  12.9 0.0 copy-start.3
  12.9 1.4 collective-permute-start.1
  14.3 0.0 copy-done.2
  14.3 0.0 copy-done.3
  14.3 0.0 copy-start.4
  14.4 0.9 copy-done.4
  15.3 4.2 %collective-permute-start.8 = (f32[8,16,512]{2,1,0:T(8,128)S(1)}, f32[8,16,512]{2,1,0:T(8,128)S(1)}, u32[]{:S(2)}, u32[]{:S(2)}) collective-permute-start(f32[8,16,512]{2,1,0:T(8,128)S(1)} %pad_maximum_fusion), channel_id=1, source_target_pairs={{0,32},{32,64},{64,96},{96,128},{128,160},{160,192},{192,224},{1,3... | collective-permute-start | bytes 786440 | tf_op jit(solution)/shard_map/ppermute | solution.py:537
  19.5 0.0 copy-start
  19.6 0.0 collective-permute-done.2.refs_4_.refs_11_
  19.6 1.4 collective-permute-start.9
  21.0 0.0 collective-permute-done.3.refs_5_.refs_12_
  21.1 4.2 %collective-permute-start.4 = (f32[8,16,128]{2,1,0:T(8,128)S(1)}, f32[8,16,128]{2,1,0:T(8,128)S(1)}, u32[]{:S(2)}, u32[]{:S(2)}) collective-permute-start(f32[8,16,128]{2,1,0:T(8,128)S(1)} %pad_maximum_fusion.2), channel_id=1, source_target_pairs={{0,32},{32,64},{64,96},{96,128},{128,160},{160,192},{192,224},{1,3... | collective-permute-start | bytes 196616 | tf_op jit(solution)/shard_map/ppermute | solution.py:537
  25.2 1.3 collective-permute-done.4.refs_6_.refs_13_
  26.5 1.3 collective-permute-start.5
  27.8 0.1 pad_add_fusion.place_ref
  27.9 5.4 %collective-permute-done.5.refs_7_.refs_14_ = f32[8,16,128]{2,1,0:T(8,128)S(1)} collective-permute-done((f32[8,16,128]{2,1,0:T(8,128)S(1)}, f32[8,16,128]{2,1,0:T(8,128)S(1)}, u32[]{:S(2)}, u32[]{:S(2)}) %collective-permute-start.5) | collective-permute-done | bytes 65568 | tf_op jit(solution)/shard_map/ppermute | solution.py:537
  33.3 0.0 collective-permute-done.refs_2_
  33.3 0.0 collective-permute-done.1.refs_3_
  33.3 0.0 copy-done
  33.3 2.2 shard_map.121
  35.5 5.1 %collective-permute-start.6 = (f32[4,16,640]{2,1,0:T(8,128)S(1)}, f32[4,16,640]{2,1,0:T(8,128)S(1)}, u32[]{:S(2)}, u32[]{:S(2)}) collective-permute-start(f32[4,16,640]{2,1,0:T(8,128)S(1)} %get-tuple-element.43.refs_2_), channel_id=1, source_target_pairs={{0,32},{32,64},{64,96},{96,128},{128,160},{160,192},{192,224},{1,3... | collective-permute-start | bytes 491528 | tf_op jit(solution)/shard_map/ppermute | solution.py:537
  40.7 1.3 collective-permute-start.7
  42.0 0.0 collective-permute-done.8.refs_9_
  42.0 0.0 collective-permute-done.9.refs_10_
  42.0 1.8 collective-permute-done.6.refs_0_
  43.8 5.1 %collective-permute-done.7.refs_3_ = f32[4,16,640]{2,1,0:T(8,128)S(1)} collective-permute-done((f32[4,16,640]{2,1,0:T(8,128)S(1)}, f32[4,16,640]{2,1,0:T(8,128)S(1)}, u32[]{:S(2)}, u32[]{:S(2)}) %collective-permute-start.7) | collective-permute-done | bytes 163872 | tf_op jit(solution)/shard_map/ppermute | solution.py:537
  48.9 10.5 %shard_map.122 = (f32[8,16,512]{2,1,0:T(8,128)}, f32[4,16,640]{2,1,0:T(8,128)S(1)}, f32[4,16,640]{2,1,0:T(8,128)S(1)}) custom-call(s32[2]{0:T(128)S(1)} %pad_add_fusion.place_ref, f32[4,16,640]{2,1,0:T(8,128)S(1)} %collective-permute-done.6.refs_0_, f32[4,16,640]{2,1,0:T(8,128)S(1)} %get-tuple-element.44.refs_1_, ...), custom_call_target="tpu_custom_call" | custom-call | tf_op jit(solution)/shard_map/pallas_call | solution.py:489
  59.4 4.5 %collective-permute-start.10 = (f32[4,16,640]{2,1,0:T(8,128)S(1)}, f32[4,16,640]{2,1,0:T(8,128)S(1)}, u32[]{:S(2)}, u32[]{:S(2)}) collective-permute-start(f32[4,16,640]{2,1,0:T(8,128)S(1)} %get-tuple-element.46.last), channel_id=1, source_target_pairs={{0,32},{32,64},{64,96},{96,128},{128,160},{160,192},{192,224},{1,3... | collective-permute-start | bytes 491528 | tf_op jit(solution)/shard_map/ppermute | solution.py:537
  63.9 1.3 collective-permute-start.11
  65.2 0.9 collective-permute-done.10.from_above
  66.1 3.8 %collective-permute-done.11.from_below = f32[4,16,640]{2,1,0:T(8,128)S(1)} collective-permute-done((f32[4,16,640]{2,1,0:T(8,128)S(1)}, f32[4,16,640]{2,1,0:T(8,128)S(1)}, u32[]{:S(2)}, u32[]{:S(2)}) %collective-permute-start.11) | collective-permute-done | bytes 163872 | tf_op jit(solution)/shard_map/ppermute | solution.py:537
  70.0 2.1 shard_map.123
  72.0 17.1 %all-to-all-start = ((f32[256,1,128]{2,1,0:T(1,128)}), f32[256,1,128]{2,1,0:T(1,128)S(1)}, u32[]{:S(2)}, u32[]{:S(2)}) async-start(f32[256,1,128]{2,1,0:T(1,128)} %bitcast.3), calls=%async_computation | async-start | bytes 262144 | tf_op jit(solution)/shard_map/all_to_all | solution.py:605
  89.1 0.0 copy-done.6
  89.1 0.0 copy-done.7
  89.2 0.0 copy-start.8
  89.2 0.9 copy-done.8
  90.1 0.9 shard_map.124
  91.0 11.0 %all-to-all-done = f32[256,1,128]{2,1,0:T(1,128)S(1)} async-done(((f32[256,1,128]{2,1,0:T(1,128)}), f32[256,1,128]{2,1,0:T(1,128)S(1)}, u32[]{:S(2)}, u32[]{:S(2)}) %all-to-all-start) | async-done | bytes 131104 | tf_op jit(solution)/shard_map/all_to_all | solution.py:605
  102.0 0.6 shard_map.125
  102.7 18.4 %all_to_all.99 = f32[256,1,128]{2,1,0:T(1,128)S(1)} all-to-all(f32[256,1,128]{2,1,0:T(1,128)S(1)} %bitcast.48), channel_id=1, replica_groups=mesh['thick'=8,'facade'=32] {'thick','facade'}, dimensions={0} | all-to-all | bytes 262144 | tf_op jit(solution)/shard_map/all_to_all | solution.py:605
  121.0 0.6 shard_map.126
  121.6 18.4 %all_to_all.100 = f32[256,1,128]{2,1,0:T(1,128)S(1)} all-to-all(f32[256,1,128]{2,1,0:T(1,128)S(1)} %bitcast.49), channel_id=1, replica_groups=mesh['thick'=8,'facade'=32] {'thick','facade'}, dimensions={0} | all-to-all | bytes 262144 | tf_op jit(solution)/shard_map/all_to_all | solution.py:605
  140.0 0.6 shard_map.127
  140.5 18.5 %all_to_all.101 = f32[256,1,128]{2,1,0:T(1,128)S(1)} all-to-all(f32[256,1,128]{2,1,0:T(1,128)S(1)} %bitcast.50), channel_id=1, replica_groups=mesh['thick'=8,'facade'=32] {'thick','facade'}, dimensions={0} | all-to-all | bytes 262144 | tf_op jit(solution)/shard_map/all_to_all | solution.py:605
  159.1 0.6 shard_map.128
  159.7 18.4 %all_to_all.102 = f32[256,1,128]{2,1,0:T(1,128)S(1)} all-to-all(f32[256,1,128]{2,1,0:T(1,128)S(1)} %bitcast.51), channel_id=1, replica_groups=mesh['thick'=8,'facade'=32] {'thick','facade'}, dimensions={0} | all-to-all | bytes 262144 | tf_op jit(solution)/shard_map/all_to_all | solution.py:605
  178.0 0.6 shard_map.129
  178.6 18.4 %all_to_all.103 = f32[256,1,128]{2,1,0:T(1,128)S(1)} all-to-all(f32[256,1,128]{2,1,0:T(1,128)S(1)} %bitcast.52), channel_id=1, replica_groups=mesh['thick'=8,'facade'=32] {'thick','facade'}, dimensions={0} | all-to-all | bytes 262144 | tf_op jit(solution)/shard_map/all_to_all | solution.py:605
  197.0 0.6 shard_map.130
  197.5 18.4 %all_to_all.104 = f32[256,1,128]{2,1,0:T(1,128)S(1)} all-to-all(f32[256,1,128]{2,1,0:T(1,128)S(1)} %bitcast.53), channel_id=1, replica_groups=mesh['thick'=8,'facade'=32] {'thick','facade'}, dimensions={0} | all-to-all | bytes 262144 | tf_op jit(solution)/shard_map/all_to_all | solution.py:605
  215.9 0.6 shard_map.131
  216.5 18.4 %all_to_all.105 = f32[256,1,128]{2,1,0:T(1,128)S(1)} all-to-all(f32[256,1,128]{2,1,0:T(1,128)S(1)} %bitcast.54), channel_id=1, replica_groups=mesh['thick'=8,'facade'=32] {'thick','facade'}, dimensions={0} | all-to-all | bytes 262144 | tf_op jit(solution)/shard_map/all_to_all | solution.py:605
  234.8 0.6 shard_map.132
  235.4 0.0 copy-start.9
  235.4 18.5 %all_to_all.106 = f32[256,1,128]{2,1,0:T(1,128)S(1)} all-to-all(f32[256,1,128]{2,1,0:T(1,128)S(1)} %bitcast.47), channel_id=1, replica_groups=mesh['thick'=8,'facade'=32] {'thick','facade'}, dimensions={0} | all-to-all | bytes 262144 | tf_op jit(solution)/shard_map/all_to_all | solution.py:605
  253.9 1.0 shard_map.133
  (16 shorter events, 0.1 us)
Async XLA Ops:
  0.6 8.6 %copy-start.1 = (f32[8,16,512]{2,1,0:T(8,128)S(1)}, f32[8,16,512]{2,1,0:T(8,128)}, u32[]{:S(2)}) copy-start(f32[8,16,512]{2,1,0:T(8,128)} %solid.3) | copy-start | bytes 786436
  2.7 16.9 %collective-permute-start.2 = (f32[8,16,128]{2,1,0:T(8,128)}, f32[8,16,128]{2,1,0:T(8,128)S(1)}, u32[]{:S(2)}, u32[]{:S(2)}) collective-permute-start(f32[8,16,128]{2,1,0:T(8,128)} %get-tuple-element.41), channel_id=1, source_target_pairs={{0,1},{1,2},{2,3},{3,4},{4,5},{5,6},{6,7},{7,8},{8,9},{9,10},{10,1... | collective-permute-start | bytes 196616 | tf_op jit(solution)/shard_map/ppermute | solution.py:537
  7.2 7.1 %copy-start.2 = (f32[8,16,512]{2,1,0:T(8,128)S(1)}, f32[8,16,512]{2,1,0:T(8,128)}, u32[]{:S(2)}) copy-start(f32[8,16,512]{2,1,0:T(8,128)} %refs_6_.3) | copy-start | bytes 786436
  7.2 13.8 %collective-permute-start.3 = (f32[8,16,128]{2,1,0:T(8,128)}, f32[8,16,128]{2,1,0:T(8,128)S(1)}, u32[]{:S(2)}, u32[]{:S(2)}) collective-permute-start(f32[8,16,128]{2,1,0:T(8,128)} %get-tuple-element.42), channel_id=1, source_target_pairs={{1,0},{2,1},{3,2},{4,3},{5,4},{6,5},{7,6},{8,7},{9,8},{10,9},{11,1... | collective-permute-start | bytes 196616 | tf_op jit(solution)/shard_map/ppermute | solution.py:537
  9.3 24.0 %collective-permute-start = (f32[4,16,512]{2,1,0:T(8,128)S(1)}, f32[4,16,512]{2,1,0:T(8,128)S(1)}, u32[]{:S(2)}, u32[]{:S(2)}) collective-permute-start(f32[4,16,512]{2,1,0:T(8,128)S(1)} %get-tuple-element.85), channel_id=1, source_target_pairs={{0,32},{32,64},{64,96},{96,128},{128,160},{160,192},{192,224},{1,3... | collective-permute-start | bytes 393224 | tf_op jit(solution)/shard_map/ppermute | solution.py:537
  12.9 1.5 copy-start.3
  12.9 20.5 %collective-permute-start.1 = (f32[4,16,512]{2,1,0:T(8,128)S(1)}, f32[4,16,512]{2,1,0:T(8,128)S(1)}, u32[]{:S(2)}, u32[]{:S(2)}) collective-permute-start(f32[4,16,512]{2,1,0:T(8,128)S(1)} %get-tuple-element.84), channel_id=1, source_target_pairs={{32,0},{64,32},{96,64},{128,96},{160,128},{192,160},{224,192},{33,... | collective-permute-start | bytes 393224 | tf_op jit(solution)/shard_map/ppermute | solution.py:537
  14.3 1.0 copy-start.4
  15.3 26.7 %collective-permute-start.8 = (f32[8,16,512]{2,1,0:T(8,128)S(1)}, f32[8,16,512]{2,1,0:T(8,128)S(1)}, u32[]{:S(2)}, u32[]{:S(2)}) collective-permute-start(f32[8,16,512]{2,1,0:T(8,128)S(1)} %pad_maximum_fusion), channel_id=1, source_target_pairs={{0,32},{32,64},{64,96},{96,128},{128,160},{160,192},{192,224},{1,3... | collective-permute-start | bytes 786440 | tf_op jit(solution)/shard_map/ppermute | solution.py:537
  19.5 13.8 %copy-start = (s32[8,16,512]{2,1,0:T(8,128)S(1)}, s32[8,16,512]{2,1,0:T(8,128)}, u32[]{:S(2)}) copy-start(s32[8,16,512]{2,1,0:T(8,128)} %material.5) | copy-start | bytes 786436
  19.6 22.4 %collective-permute-start.9 = (f32[8,16,512]{2,1,0:T(8,128)S(1)}, f32[8,16,512]{2,1,0:T(8,128)S(1)}, u32[]{:S(2)}, u32[]{:S(2)}) collective-permute-start(f32[8,16,512]{2,1,0:T(8,128)S(1)} %pad_maximum_fusion.1), channel_id=1, source_target_pairs={{32,0},{64,32},{96,64},{128,96},{160,128},{192,160},{224,192},{33,... | collective-permute-start | bytes 786440 | tf_op jit(solution)/shard_map/ppermute | solution.py:537
  21.1 5.5 %collective-permute-start.4 = (f32[8,16,128]{2,1,0:T(8,128)S(1)}, f32[8,16,128]{2,1,0:T(8,128)S(1)}, u32[]{:S(2)}, u32[]{:S(2)}) collective-permute-start(f32[8,16,128]{2,1,0:T(8,128)S(1)} %pad_maximum_fusion.2), channel_id=1, source_target_pairs={{0,32},{32,64},{64,96},{96,128},{128,160},{160,192},{192,224},{1,3... | collective-permute-start | bytes 196616 | tf_op jit(solution)/shard_map/ppermute | solution.py:537
  26.5 6.8 %collective-permute-start.5 = (f32[8,16,128]{2,1,0:T(8,128)S(1)}, f32[8,16,128]{2,1,0:T(8,128)S(1)}, u32[]{:S(2)}, u32[]{:S(2)}) collective-permute-start(f32[8,16,128]{2,1,0:T(8,128)S(1)} %pad_maximum_fusion.3), channel_id=1, source_target_pairs={{32,0},{64,32},{96,64},{128,96},{160,128},{192,160},{224,192},{33,... | collective-permute-start | bytes 196616 | tf_op jit(solution)/shard_map/ppermute | solution.py:537
  35.5 8.3 %collective-permute-start.6 = (f32[4,16,640]{2,1,0:T(8,128)S(1)}, f32[4,16,640]{2,1,0:T(8,128)S(1)}, u32[]{:S(2)}, u32[]{:S(2)}) collective-permute-start(f32[4,16,640]{2,1,0:T(8,128)S(1)} %get-tuple-element.43.refs_2_), channel_id=1, source_target_pairs={{0,32},{32,64},{64,96},{96,128},{128,160},{160,192},{192,224},{1,3... | collective-permute-start | bytes 491528 | tf_op jit(solution)/shard_map/ppermute | solution.py:537
  40.7 8.2 %collective-permute-start.7 = (f32[4,16,640]{2,1,0:T(8,128)S(1)}, f32[4,16,640]{2,1,0:T(8,128)S(1)}, u32[]{:S(2)}, u32[]{:S(2)}) collective-permute-start(f32[4,16,640]{2,1,0:T(8,128)S(1)} %get-tuple-element.44.refs_1_), channel_id=1, source_target_pairs={{32,0},{64,32},{96,64},{128,96},{160,128},{192,160},{224,192},{33,... | collective-permute-start | bytes 491528 | tf_op jit(solution)/shard_map/ppermute | solution.py:537
  59.4 6.8 %collective-permute-start.10 = (f32[4,16,640]{2,1,0:T(8,128)S(1)}, f32[4,16,640]{2,1,0:T(8,128)S(1)}, u32[]{:S(2)}, u32[]{:S(2)}) collective-permute-start(f32[4,16,640]{2,1,0:T(8,128)S(1)} %get-tuple-element.46.last), channel_id=1, source_target_pairs={{0,32},{32,64},{64,96},{96,128},{128,160},{160,192},{192,224},{1,3... | collective-permute-start | bytes 491528 | tf_op jit(solution)/shard_map/ppermute | solution.py:537
  63.9 6.1 %collective-permute-start.11 = (f32[4,16,640]{2,1,0:T(8,128)S(1)}, f32[4,16,640]{2,1,0:T(8,128)S(1)}, u32[]{:S(2)}, u32[]{:S(2)}) collective-permute-start(f32[4,16,640]{2,1,0:T(8,128)S(1)} %get-tuple-element.47.first), channel_id=1, source_target_pairs={{32,0},{64,32},{96,64},{128,96},{160,128},{192,160},{224,192},{33,... | collective-permute-start | bytes 491528 | tf_op jit(solution)/shard_map/ppermute | solution.py:537
  70.0 19.2 %copy-start.6 = (f32[8,16,512]{2,1,0:T(8,128)S(1)}, f32[8,16,512]{2,1,0:T(8,128)}, u32[]{:S(2)}) copy-start(f32[8,16,512]{2,1,0:T(8,128)} %older.1) | copy-start | bytes 786436
  70.0 19.2 %copy-start.7 = (f32[8,16,512]{2,1,0:T(8,128)S(1)}, f32[8,16,512]{2,1,0:T(8,128)}, u32[]{:S(2)}) copy-start(f32[8,16,512]{2,1,0:T(8,128)} %below_spacing.1) | copy-start | bytes 786436
  72.0 17.1 %copy-start.5 = (f32[8,16,512]{2,1,0:T(8,128)S(1)}, f32[8,16,512]{2,1,0:T(8,128)}, u32[]{:S(2)}) copy-start(f32[8,16,512]{2,1,0:T(8,128)} %newer.1) | copy-start | bytes 786436
  72.0 30.0 %all-to-all-start = ((f32[256,1,128]{2,1,0:T(1,128)}), f32[256,1,128]{2,1,0:T(1,128)S(1)}, u32[]{:S(2)}, u32[]{:S(2)}) async-start(f32[256,1,128]{2,1,0:T(1,128)} %bitcast.3), calls=%async_computation | async-start | bytes 262144 | tf_op jit(solution)/shard_map/all_to_all | solution.py:605
  89.2 1.0 copy-start.8
  235.4 18.5 %copy-start.9 = (f32[8,16,512]{2,1,0:T(8,128)S(1)}, f32[8,16,512]{2,1,0:T(8,128)}, u32[]{:S(2)}) copy-start(f32[8,16,512]{2,1,0:T(8,128)} %get-tuple-element.38.below) | copy-start | bytes 786436

commit v3 on v2

--- a/solution.py
+++ b/solution.py
@@ -108,17 +108,6 @@
     return 1.0 / axis_weight(jnp.full((1, 1), row + row_start, jnp.int32), rows_total)
 
 
-def boxes(values):
-    pairs = [a + b for a, b in zip(values[:-1], values[1:])]
-    fours = [a + b for a, b in zip(pairs[:-2], pairs[2:])]
-    return [a + b for a, b in zip(fours, values[4:])]
-
-
-def filter_depth(get, put, count):
-    singles = [get(r) for r in range(count)]
-    return boxes(boxes(singles))
-
-
 def filter_height(value):
     height = value.shape[0]
     level = sub_iota((height, 1))
@@ -151,30 +140,51 @@
         target[r] = (middle[r] + middle[r + 1]) + (middle[r + 2] + middle[r + 3]) + middle[r + 4]
 
 
+def present(place, rows, own, rows_total, cols_total):
+    row_start, col_start = place
+
+    def flag(condition):
+        return jnp.where(condition, 1.0, 0.0).astype(f32)
+
+    return (
+        flag(row_start > 0), flag(row_start + rows < rows_total),
+        flag(col_start > 0), flag(col_start + own < cols_total),
+    )
+
+
+def corner(message, row):
+    lanes = slice(row * LANES, (row + 1) * LANES)
+    return message[12, :, lanes], message[13, :, lanes]
+
+
 def rho_kernel(
     rows_total, cols_total, place,
-    density, material, from_above, from_below, left, right, corner_above, corner_below,
+    density, material, from_above, from_below, left, right,
     rho_out, cond_first, cond_last,
     ext, middle, summed,
 ):
     rows, height, own = density.shape
+    has_above, has_below, has_left, has_right = present(place, rows, own, rows_total, cols_total)
+
+    def halo(strips, index):
+        return halo_lanes(strips[0] * has_left, strips[1] * has_right, index)
+
     for r in range(4):
-        ext[r, :, :own] = from_above[r]
-        ext[r, :, own:] = halo_lanes(corner_above[r], corner_above[4 + r], 0)
-        ext[rows + 4 + r, :, :own] = from_below[r]
-        ext[rows + 4 + r, :, own:] = halo_lanes(corner_below[r], corner_below[4 + r], 0)
+        ext[r, :, :own] = from_above[r] * has_above
+        ext[r, :, own:] = halo(corner(from_above, r), 0) * has_above
+        ext[rows + 4 + r, :, :own] = from_below[r] * has_below
+        ext[rows + 4 + r, :, own:] = halo(corner(from_below, r), 0) * has_below
     for r in range(rows):
         ext[4 + r, :, :own] = density[r]
-        ext[4 + r, :, own:] = halo_lanes(left[r], right[r], 0)
+        ext[4 + r, :, own:] = halo((left[r], right[r]), 0)
     depth_filter(ext, middle, summed)
-    row_start = place[0]
     plane = inverse_plane(height, own, cols_total, place[1])
     for r in range(rows):
         rho = filter_lanes(filter_height(summed[r])) * (
-            plane * row_weight(r, rows_total, row_start)
+            plane * row_weight(r, rows_total, place[0])
         )
         code = jnp.concatenate(
-            [material[r].astype(f32) + 1.0, halo_lanes(left[r], right[r], 1)], axis=1
+            [material[r].astype(f32) + 1.0, halo((left[r], right[r]), 1)], axis=1
         )
         frame = k_void + (k_frame - k_void) * rho * rho * rho
         cond = jnp.where(code == 2.0, frame, jnp.where(code == 1.0, k_glass, k_anchor))
@@ -189,153 +199,158 @@
 def sweep_kernel(
     rows_total, cols_total, place,
     cond_above, cond_first, cond_last, cond_below, rho, material,
-    prior, source, temp, rows_above, rows_below, left, right, corner_above, corner_below,
+    prior, source, temp, from_above, from_below, left, right, tallies,
     dual_out, weighted_first, weighted_last,
     cond, field, load, heat, depth_face, height_face, lane_face, inverse, residual, next_field, dual,
+    depth_here, depth_there, height_here, height_there, lane_here, lane_there,
 ):
     rows, height, own = prior.shape
-    width = own + LANES
+    has_above, has_below, has_left, has_right = present(place, rows, own, rows_total, cols_total)
     last_level = sub_iota((height, 1)) == height - 1
     for r in range(4):
-        cond[r] = cond_above[r]
+        cond[r] = cond_above[r] * has_above
         cond[4 + r] = cond_first[r]
         cond[8 + r] = cond_last[r]
-        cond[12 + r] = cond_below[r]
+        cond[12 + r] = cond_below[r] * has_below
+
+    def place_row(target, row, main, strips, index):
+        target[row, :, :own] = main
+        target[row, :, own:] = halo_lanes(strips[0], strips[1], index)
+
     for r in range(4):
-        field[r, :, :own] = rows_above[r]
-        field[r, :, own:] = halo_lanes(corner_above[r], corner_above[4 + r], 3)
-        field[12 + r, :, :own] = rows_below[r]
-        field[12 + r, :, own:] = halo_lanes(corner_below[r], corner_below[4 + r], 3)
+        place_row(field, r, from_above[4 + r], corner(from_above, r), 3)
+        place_row(field, 12 + r, from_below[4 + r], corner(from_below, r), 3)
     for r in range(3):
-        load[1 + r, :, :own] = rows_above[4 + r]
-        load[1 + r, :, own:] = halo_lanes(corner_above[1 + r], corner_above[5 + r], 2)
-        load[12 + r, :, :own] = rows_below[4 + r]
-        load[12 + r, :, own:] = halo_lanes(corner_below[r], corner_below[4 + r], 2)
-    heat[0, :, :own] = rows_above[7]
-    heat[0, :, own:] = halo_lanes(corner_above[3], corner_above[7], 4)
-    heat[9, :, :own] = rows_below[7]
-    heat[9, :, own:] = halo_lanes(corner_below[0], corner_below[4], 4)
+        place_row(load, 1 + r, from_above[8 + r], corner(from_above, 1 + r), 2)
+        place_row(load, 12 + r, from_below[8 + r], corner(from_below, r), 2)
+    place_row(heat, 0, from_above[11], corner(from_above, 3), 4)
+    place_row(heat, 9, from_below[11], corner(from_below, 0), 4)
     for r in range(rows):
-        field[4 + r, :, :own] = prior[r]
-        field[4 + r, :, own:] = halo_lanes(left[r], right[r], 3)
-        load[4 + r, :, :own] = source[r]
-        load[4 + r, :, own:] = halo_lanes(left[r], right[r], 2)
-        heat[1 + r, :, :own] = temp[r]
-        heat[1 + r, :, own:] = halo_lanes(left[r], right[r], 4)
-
-    def face(one, other):
-        return 2.0 * one * other / jnp.maximum(one + other, 1e-3)
-
-    depth_face[0] = face(cond[0], cond[1])
-
-    def make_faces(r, carry):
-        here = cond[r]
-        deep = face(here, cond[r + 1])
-        tall = jnp.where(last_level, 0.0, face(here, ahead(here, 1, 0)))
-        wide = face(here, ahead(here, 1, 1))
+        strips = (left[r], right[r])
+        place_row(field, 4 + r, prior[r], strips, 3)
+        place_row(load, 4 + r, source[r], strips, 2)
+        place_row(heat, 1 + r, temp[r], strips, 4)
+
+    centre = 0.5 * (spectrum_high + spectrum_low)
+    half = 0.5 * (spectrum_high - spectrum_low)
+    ratio = centre / half
+
+    def face(one, other, keep, row, here, there):
+        inv = 1.0 / jnp.maximum(one + other, 1e-3)
+        part = one * inv
+        if keep:
+            rest = other * inv
+            there[row] = part * part
+            here[row] = rest * rest
+        return 2.0 * part * other
+
+    here = cond[0]
+    following = cond[1]
+    deep_before = face(here, following, False, 0, depth_here, depth_there)
+    depth_face[0] = deep_before
+    flux_before = deep_before * (field[0] - field[1])
+    for r in range(1, 15):
+        here, following = following, cond[r + 1]
+        deep = face(here, following, 3 <= r < 12, r, depth_here, depth_there)
+        tall = face(here, ahead(here, 1, 0), 4 <= r < 12, r, height_here, height_there)
+        tall = jnp.where(last_level, 0.0, tall)
+        wide = face(here, ahead(here, 1, 1), 4 <= r < 12, r, lane_here, lane_there)
         depth_face[r] = deep
         height_face[r] = tall
         lane_face[r] = wide
-        diagonal = (
-            loss_rate + (deep + depth_face[r - 1]) + (tall + behind(tall, 1, 0))
+        inv_diagonal = 1.0 / (
+            loss_rate + (deep + deep_before) + (tall + behind(tall, 1, 0))
             + (wide + behind(wide, 1, 1))
         )
-        inverse[r] = 1.0 / diagonal
-        return carry
-
-    lax.fori_loop(1, 15, make_faces, 0)
-
-    def product(ref, r):
-        here = ref[r]
-        deep = depth_face[r] * (here - ref[r + 1]) + depth_face[r - 1] * (here - ref[r - 1])
-        tall = height_face[r] * (here - ahead(here, 1, 0))
-        wide = lane_face[r] * (here - ahead(here, 1, 1))
-        return (
-            loss_rate * here + deep + (tall - behind(tall, 1, 0)) + (wide - behind(wide, 1, 1))
-        )
-
-    centre = 0.5 * (spectrum_high + spectrum_low)
-    half = 0.5 * (spectrum_high - spectrum_low)
-    ratio = centre / half
-
-    def begin(r, carry):
-        left_over = load[r] - product(field, r)
+        inverse[r] = inv_diagonal
+        value = field[r]
+        flux = deep * (value - field[r + 1])
+        high = tall * (value - ahead(value, 1, 0))
+        along = wide * (value - ahead(value, 1, 1))
+        product = (
+            loss_rate * value + (flux - flux_before) + (high - behind(high, 1, 0))
+            + (along - behind(along, 1, 1))
+        )
+        left_over = load[r] - product
         residual[r] = left_over
-        direction = left_over * inverse[r] * (1.0 / centre)
+        direction = left_over * inv_diagonal * (1.0 / centre)
         next_field[r] = direction
-        dual[r] = field[r] + direction
-        return carry
-
-    lax.fori_loop(1, 15, begin, 0)
+        if 3 <= r < 13:
+            dual[r] = value + direction
+        deep_before, flux_before = deep, flux
+
     factor = 1.0 / ratio
     now, then = next_field, field
     for sweep in range(SWEEPS - 1):
         factor_next = 1.0 / (2.0 * ratio - factor)
         keep, add = factor_next * factor, 2.0 * factor_next / half
-
-        def step(r, carry, now=now, then=then, keep=keep, add=add):
-            left_over = residual[r] - product(now, r)
-            residual[r] = left_over
-            direction = keep * now[r] + add * (left_over * inverse[r])
+        start, stop = 2 + sweep, 14 - sweep
+        following = now[start]
+        flux_before = depth_face[start - 1] * (now[start - 1] - following)
+        for r in range(start, stop):
+            value, following = following, now[r + 1]
+            flux = depth_face[r] * (value - following)
+            high = height_face[r] * (value - ahead(value, 1, 0))
+            along = lane_face[r] * (value - ahead(value, 1, 1))
+            product = (
+                loss_rate * value + (flux - flux_before) + (high - behind(high, 1, 0))
+                + (along - behind(along, 1, 1))
+            )
+            left_over = residual[r] - product
+            if sweep < SWEEPS - 2:
+                residual[r] = left_over
+            direction = keep * value + add * (left_over * inverse[r])
             then[r] = direction
-            dual[r] = dual[r] + direction
-            return carry
-
-        lax.fori_loop(2 + sweep, 14 - sweep, step, 0)
+            if 3 <= r < 13:
+                dual[r] = dual[r] + direction
+            flux_before = flux
         factor = factor_next
         now, then = then, now
 
-    row_start = place[0]
     plane = inverse_plane(height, own, cols_total, place[1])
     for r in range(rows):
         dual_out[r] = dual[4 + r, :, :own]
-
-    def sens(r, deep_before):
-        c, a, t = cond[r], dual[r], heat[r - 3]
-
-        def shared(c_q, a_q, t_q):
-            inv = 1.0 / jnp.maximum(c + c_q, 1e-3)
-            return (a - a_q) * (t - t_q) * (inv * inv)
-
-        c_q = cond[r + 1]
-        deep = shared(c_q, dual[r + 1], heat[r - 2])
-        c_sq = c * c
-        total = deep * (c_q * c_q)
-        deep_next = deep * c_sq
-        c_q = ahead(c, 1, 0)
-        tall = jnp.where(last_level, 0.0, shared(c_q, ahead(a, 1, 0), ahead(t, 1, 0)))
-        total = total + tall * (c_q * c_q) + behind(tall * c_sq, 1, 0)
-        c_q = ahead(c, 1, 1)
-        wide = shared(c_q, ahead(a, 1, 1), ahead(t, 1, 1))
-        total = total + wide * (c_q * c_q) + behind(wide * c_sq, 1, 1)
-        return -2.0 * (total + deep_before), deep_next
-
-    c, c_q = cond[3], cond[4]
-    inv = 1.0 / jnp.maximum(c + c_q, 1e-3)
-    deep_before = (dual[3] - dual[4]) * (heat[0] - heat[1]) * (inv * inv) * (c * c)
-    for r in range(rows):
-        value, deep_before = sens(4 + r, deep_before)
-        code = jnp.concatenate(
-            [material[r].astype(f32) + 1.0, halo_lanes(left[r], right[r], 1)], axis=1
-        )
-        squared = rho[r] * rho[r]
-        value = value * (3.0 * (k_frame - k_void)) * squared * (
-            plane * row_weight(r, rows_total, row_start)
+    a, t = dual[3], heat[0]
+    a_next, t_next = dual[4], heat[1]
+    deep_before = (a - a_next) * (t - t_next) * depth_there[3]
+    for r in range(4, 4 + rows):
+        a, t = a_next, t_next
+        a_next, t_next = dual[r + 1], heat[r - 2]
+        deep = (a - a_next) * (t - t_next)
+        tall = (a - ahead(a, 1, 0)) * (t - ahead(t, 1, 0))
+        tall = jnp.where(last_level, 0.0, tall)
+        wide = (a - ahead(a, 1, 1)) * (t - ahead(t, 1, 1))
+        total = (
+            (deep * depth_here[r] + deep_before)
+            + (tall * height_here[r] + behind(tall * height_there[r], 1, 0))
+            + (wide * lane_here[r] + behind(wide * lane_there[r], 1, 1))
+        )
+        deep_before = deep * depth_there[r]
+        row = r - 4
+        strips = halo_lanes(left[row] * has_left, right[row] * has_right, 1)
+        code = jnp.concatenate([material[row].astype(f32) + 1.0, strips], axis=1)
+        thick_rho = rho[row]
+        value = total * (thick_rho * thick_rho) * (
+            plane * (row_weight(row, rows_total, place[0]) * (-6.0 * (k_frame - k_void)))
         )
         value = jnp.where(code == 2.0, value, 0.0)
-        if r < 4:
-            weighted_first[r] = value
+        if row < 4:
+            weighted_first[row] = value
         else:
-            weighted_last[r - 4] = value
-
-
-def grad_kernel(from_above, first, last, from_below, material, grad_out, message, ext, middle, summed):
+            weighted_last[row - 4] = value
+
+
+def grad_kernel(
+    rows_total, cols_total, place,
+    from_above, first, last, from_below, material, grad_out, message, ext, middle, summed,
+):
     rows, height, own = grad_out.shape
+    has_above, has_below, _, _ = present(place, rows, own, rows_total, cols_total)
     for r in range(4):
-        ext[r] = from_above[r]
+        ext[r] = from_above[r] * has_above
         ext[4 + r] = first[r]
         ext[8 + r] = last[r]
-        ext[12 + r] = from_below[r]
+        ext[12 + r] = from_below[r] * has_below
     depth_filter(ext, middle, summed)
     largest = jnp.zeros((height, LANES), f32)
     for r in range(rows):
@@ -532,31 +547,35 @@
     width = own + LANES
     whole = (rows, height, own)
 
-    def shift(axis, size, step):
-        pairs = [(i, i + step) for i in range(size) if 0 <= i + step < size]
+    def turn(axis, size, step):
+        pairs = [(i, (i + step) % size) for i in range(size)]
         return lambda value: lax.ppermute(value, axis, pairs)
 
-    to_right, to_left = shift("facade", long, 1), shift("facade", long, -1)
-    to_deeper, to_nearer = shift("thick", deep, 1), shift("thick", deep, -1)
+    to_right, to_left = turn("facade", long, 1), turn("facade", long, -1)
+    to_deeper, to_nearer = turn("thick", deep, 1), turn("thick", deep, -1)
 
     first_strips, last_strips = pack_strips(
         (solid_occupancy, cell_material, loss_state_derivative, prior_dual_state, thermal_state)
     )
     right, left = to_left(first_strips), to_right(last_strips)
-    density_above, density_below = (
-        to_deeper(solid_occupancy[rows - 4:]),
-        to_nearer(solid_occupancy[:4]),
-    )
-    rows_above = to_deeper(
-        jnp.concatenate(
-            [prior_dual_state[rows - 4:], loss_state_derivative[rows - 3:], thermal_state[rows - 1:]]
-        )
-    )
-    rows_below = to_nearer(
-        jnp.concatenate([prior_dual_state[:4], loss_state_derivative[:3], thermal_state[:1]])
-    )
-    corner_above = to_deeper(jnp.concatenate([left[rows - 4:], right[rows - 4:]]))
-    corner_below = to_nearer(jnp.concatenate([left[:4], right[:4]]))
+
+    def side_by_side(strips, start):
+        return jnp.concatenate([strips[start + r] for r in range(4)], axis=1)[None]
+
+    def depth_message(last):
+        def end(value, count):
+            return value[rows - count:] if last else value[:count]
+
+        start = rows - 4 if last else 0
+        return jnp.concatenate(
+            [
+                end(solid_occupancy, 4), end(prior_dual_state, 4),
+                end(loss_state_derivative, 3), end(thermal_state, 1),
+                side_by_side(left, start), side_by_side(right, start),
+            ]
+        )
+
+    from_above, from_below = to_deeper(depth_message(True)), to_nearer(depth_message(False))
 
     (below, above, up, low, least, most, upper, lower, bend, tallies) = call(
         lines_kernel,
@@ -572,8 +591,7 @@
         rho_kernel, place,
         [(rows, height, width), four, four],
         (
-            solid_occupancy, cell_material, density_above, density_below, left, right,
-            corner_above, corner_below,
+            solid_occupancy, cell_material, from_above, from_below, left, right,
         ),
         [(BOTH_SIDES, height, width), (BOTH_SIDES - 4, height, width), (rows, height, width)],
         totals,
@@ -585,20 +603,21 @@
         [whole, four, four],
         (
             cond_above, cond_first, cond_last, cond_below, rho, cell_material,
-            prior_dual_state, loss_state_derivative, thermal_state, rows_above, rows_below,
-            left, right, corner_above, corner_below,
+            prior_dual_state, loss_state_derivative, thermal_state, from_above, from_below,
+            left, right, tallies,
         ),
-        [tall, tall, tall, (10, height, width)] + [tall] * 7,
+        [tall, tall, tall, (10, height, width)] + [tall] * 13,
         totals,
     )
     weighted_above, weighted_below = to_deeper(weighted_last), to_nearer(weighted_first)
     count = deep * long
     note = (count, LANES)
-    grad, message = call(
-        grad_kernel,
+    grad, message = placed_call(
+        grad_kernel, place,
         [whole, note],
         (weighted_above, weighted_first, weighted_last, weighted_below, cell_material),
         [tall, (BOTH_SIDES - 4, height, width), (rows, height, width)],
+        totals,
     )
 
     def everyone(rows_out):

time: 256 us -> 230 us (0.90)
  starting transfers between devices: 51.9 us -> 14.7 us
  blocking collectives: 147 us -> 176 us
  waiting for transfers between devices: 29.4 us -> 17.2 us
  Pallas kernels: 23.3 us -> 19.7 us
    all_to_all x8 -> x9, blocking collectives: 147 us -> 176 us  [everyone(): return lax.all_to_all(rows_out, AXES, 0, 0, tiled=True)]
    ppermute x12 -> x8, starting transfers between devices: 34.8 us -> 14.7 us  [turn(): return lambda value: lax.ppermute(value, axis, pairs)]
    all_to_all x1 -> x0, starting transfers between devices: 17.1 us -> none  [everyone(): return lax.all_to_all(rows_out, AXES, 0, 0, tiled=True)]
    all_to_all x1 -> x0, waiting for transfers between devices: 11 us -> none  [everyone(): return lax.all_to_all(rows_out, AXES, 0, 0, tiled=True)]
    pallas_call x2 -> x3, Pallas kernels: 12.6 us -> 10.5 us  [placed_call(): pl.pallas_call(with_place(kernel, *totals), out_shape=[jax.ShapeDtypeStru...]
    pallas_call x11 -> x10, Pallas kernels: 8.64 us -> 7.1 us  [call(): pl.pallas_call(kernel, out_shape=[jax.ShapeDtypeStruct(shape, f32) for sh...]
    ppermute x12 -> x8, waiting for transfers between devices: 18.4 us -> 17.2 us  [turn(): return lambda value: lax.ppermute(value, axis, pairs)]
  transfers between devices with their start and end apart: 13 -> 8, of which waited for: 7 -> 5; matrix products, arithmetic and copies ran while one was open for 0% -> 0% of each run, Pallas kernels for 1% -> 0%
where the time goes in v3:
time: 230 us
  blocking collectives  176 us (77%)
  Pallas kernels  19.7 us (9%)
  waiting for transfers between devices  17.2 us (7%)
  starting transfers between devices  14.7 us (6%)
    all_to_all x9, blocking collectives, everyone(): return lax.all_to_all(rows_out, AXES, 0, 0, tiled=True)  176 us
    ppermute x8, waiting for transfers between devices, turn(): return lambda value: lax.ppermute(value, axis, pairs)  17.2 us
    ppermute x8, starting transfers between devices, turn(): return lambda value: lax.ppermute(value, axis, pairs)  14.7 us
    pallas_call x3, Pallas kernels, placed_call(): pl.pallas_call(with_place(kernel, *totals), out_shape=[jax.ShapeDtypeStru...  10.5 us
    pallas_call x10, Pallas kernels, call(): pl.pallas_call(kernel, out_shape=[jax.ShapeDtypeStruct(shape, f32) for sh...  7.1 us
  transfers between devices with their start and end apart: 8, of which 5 were waited for; matrix products, arithmetic and copies ran while one was open for 0% of the time, Pallas kernels for 0%

profile of v3, /device:TPU:1, one launch (start us, length us, event | category | flops | bytes accessed | tf_op | source)
XLA Modules:
  0.0 229.7 jit_solution(14811917773370813114)
XLA Ops:
  0.6 0.0 copy-start.1
  0.6 2.0 shard_map.120
  2.7 2.6 %collective-permute-start = (f32[8,16,128]{2,1,0:T(8,128)}, f32[8,16,128]{2,1,0:T(8,128)S(1)}, u32[]{:S(2)}, u32[]{:S(2)}) collective-permute-start(f32[8,16,128]{2,1,0:T(8,128)} %get-tuple-element.41), channel_id=1, source_target_pairs={{0,1},{1,2},{2,3},{3,4},{4,5},{5,6},{6,7},{7,8},{8,9},{9,10},{10,1... | collective-permute-start | bytes 196616 | tf_op jit(solution)/shard_map/ppermute | solution.py:552
  5.3 0.0 copy-start.2
  5.3 0.7 collective-permute-start.1
  6.0 0.0 copy-done.1
  6.0 0.2 copy-done.2
  6.2 0.0 copy-start.3
  6.3 0.0 copy-start.4
  6.3 0.9 copy-done.3
  7.2 0.1 copy-done.4
  7.3 0.0 copy-start
  7.3 0.0 collective-permute-done.refs_4_.refs_11_
  7.3 1.9 collective-permute-done.1.refs_5_.refs_12_
  9.2 5.9 %collective-permute-start.3 = (f32[14,16,512]{2,1,0:T(8,128)S(1)}, f32[14,16,512]{2,1,0:T(8,128)S(1)}, u32[]{:S(2)}, u32[]{:S(2)}) collective-permute-start(f32[14,16,512]{2,1,0:T(8,128)S(1)} %fusion.3), channel_id=1, source_target_pairs={{0,224},{32,0},{64,32},{96,64},{128,96},{160,128},{192,160},{224,1... | collective-permute-start | bytes 1376264 | tf_op jit(solution)/shard_map/ppermute | solution.py:552
  15.2 0.0 collective-permute-start.2
  15.2 0.1 pad_add_fusion.place_ref
  15.2 0.0 copy-start.5
  15.2 0.0 copy-start.6
  15.3 0.0 copy-start.7
  15.3 0.0 copy-start.8
  15.3 7.7 %collective-permute-done.3.refs_3_.refs_10_ = f32[14,16,512]{2,1,0:T(8,128)S(1)} collective-permute-done((f32[14,16,512]{2,1,0:T(8,128)S(1)}, f32[14,16,512]{2,1,0:T(8,128)S(1)}, u32[]{:S(2)}, u32[]{:S(2)}) %collective-permute-start.3) | collective-permute-done | bytes 458784 | tf_op jit(solution)/shard_map/ppermute | solution.py:552
  23.0 3.1 %collective-permute-done.2.refs_2_.refs_9_ = f32[14,16,512]{2,1,0:T(8,128)S(1)} collective-permute-done((f32[14,16,512]{2,1,0:T(8,128)S(1)}, f32[14,16,512]{2,1,0:T(8,128)S(1)}, u32[]{:S(2)}, u32[]{:S(2)}) %collective-permute-start.2) | collective-permute-done | bytes 458784 | tf_op jit(solution)/shard_map/ppermute | solution.py:552
  26.1 0.0 copy-done
  26.1 2.2 shard_map.121
  28.3 0.1 collective-permute-start.4
  28.4 2.7 %collective-permute-start.5 = (f32[4,16,640]{2,1,0:T(8,128)S(1)}, f32[4,16,640]{2,1,0:T(8,128)S(1)}, u32[]{:S(2)}, u32[]{:S(2)}) collective-permute-start(f32[4,16,640]{2,1,0:T(8,128)S(1)} %get-tuple-element.44.refs_1_), channel_id=1, source_target_pairs={{0,224},{32,0},{64,32},{96,64},{128,96},{160,128},{192,160},{224,1... | collective-permute-start | bytes 491528 | tf_op jit(solution)/shard_map/ppermute | solution.py:552
  31.1 0.0 copy-done.5
  31.1 0.0 copy-done.6
  31.1 0.0 copy-done.7
  31.1 0.0 copy-done.8
  31.1 0.9 shard_map.122
  32.0 1.8 collective-permute-done.4.refs_0_
  33.8 0.0 collective-permute-done.5.refs_3_
  33.8 6.5 %shard_map.123 = (f32[8,16,512]{2,1,0:T(8,128)}, f32[4,16,640]{2,1,0:T(8,128)S(1)}, f32[4,16,640]{2,1,0:T(8,128)S(1)}) custom-call(s32[2]{0:T(128)S(1)} %pad_add_fusion.place_ref, f32[4,16,640]{2,1,0:T(8,128)S(1)} %collective-permute-done.4.refs_0_, f32[4,16,640]{2,1,0:T(8,128)S(1)} %get-tuple-element.44.refs_1_, ...), custom_call_target="tpu_custom_call" | custom-call | tf_op jit(solution)/shard_map/pallas_call | solution.py:504
  40.2 0.0 collective-permute-start.6
  40.2 2.7 %collective-permute-start.7 = (f32[4,16,640]{2,1,0:T(8,128)S(1)}, f32[4,16,640]{2,1,0:T(8,128)S(1)}, u32[]{:S(2)}, u32[]{:S(2)}) collective-permute-start(f32[4,16,640]{2,1,0:T(8,128)S(1)} %get-tuple-element.48.refs_1_), channel_id=1, source_target_pairs={{0,224},{32,0},{64,32},{96,64},{128,96},{160,128},{192,160},{224,1... | collective-permute-start | bytes 491528 | tf_op jit(solution)/shard_map/ppermute | solution.py:552
  42.9 2.7 %collective-permute-done.6.refs_0_ = f32[4,16,640]{2,1,0:T(8,128)S(1)} collective-permute-done((f32[4,16,640]{2,1,0:T(8,128)S(1)}, f32[4,16,640]{2,1,0:T(8,128)S(1)}, u32[]{:S(2)}, u32[]{:S(2)}) %collective-permute-start.6) | collective-permute-done | bytes 163872 | tf_op jit(solution)/shard_map/ppermute | solution.py:552
  45.6 0.0 collective-permute-done.7.refs_3_
  45.6 1.9 shard_map.124
  47.5 28.8 %all_to_all.99 = f32[256,1,128]{2,1,0:T(1,128)S(1)} all-to-all(f32[256,1,128]{2,1,0:T(1,128)S(1)} %bitcast.96), channel_id=1, replica_groups=mesh['thick'=8,'facade'=32] {'thick','facade'}, dimensions={0} | all-to-all | bytes 262144 | tf_op jit(solution)/shard_map/all_to_all | solution.py:624
  76.3 0.7 shard_map.125
  77.0 18.4 %all_to_all.100 = f32[256,1,128]{2,1,0:T(1,128)S(1)} all-to-all(f32[256,1,128]{2,1,0:T(1,128)S(1)} %bitcast.97), channel_id=1, replica_groups=mesh['thick'=8,'facade'=32] {'thick','facade'}, dimensions={0} | all-to-all | bytes 262144 | tf_op jit(solution)/shard_map/all_to_all | solution.py:624
  95.3 0.6 shard_map.126
  96.0 18.4 %all_to_all.101 = f32[256,1,128]{2,1,0:T(1,128)S(1)} all-to-all(f32[256,1,128]{2,1,0:T(1,128)S(1)} %bitcast.98), channel_id=1, replica_groups=mesh['thick'=8,'facade'=32] {'thick','facade'}, dimensions={0} | all-to-all | bytes 262144 | tf_op jit(solution)/shard_map/all_to_all | solution.py:624
  114.3 0.6 shard_map.127
  115.0 18.4 %all_to_all.102 = f32[256,1,128]{2,1,0:T(1,128)S(1)} all-to-all(f32[256,1,128]{2,1,0:T(1,128)S(1)} %bitcast.99), channel_id=1, replica_groups=mesh['thick'=8,'facade'=32] {'thick','facade'}, dimensions={0} | all-to-all | bytes 262144 | tf_op jit(solution)/shard_map/all_to_all | solution.py:624
  133.3 0.6 shard_map.128
  134.0 18.4 %all_to_all.103 = f32[256,1,128]{2,1,0:T(1,128)S(1)} all-to-all(f32[256,1,128]{2,1,0:T(1,128)S(1)} %bitcast.100), channel_id=1, replica_groups=mesh['thick'=8,'facade'=32] {'thick','facade'}, dimensions={0} | all-to-all | bytes 262144 | tf_op jit(solution)/shard_map/all_to_all | solution.py:624
  152.3 0.6 shard_map.129
  153.0 18.4 %all_to_all.104 = f32[256,1,128]{2,1,0:T(1,128)S(1)} all-to-all(f32[256,1,128]{2,1,0:T(1,128)S(1)} %bitcast.101), channel_id=1, replica_groups=mesh['thick'=8,'facade'=32] {'thick','facade'}, dimensions={0} | all-to-all | bytes 262144 | tf_op jit(solution)/shard_map/all_to_all | solution.py:624
  171.3 0.6 shard_map.130
  172.0 18.6 %all_to_all.105 = f32[256,1,128]{2,1,0:T(1,128)S(1)} all-to-all(f32[256,1,128]{2,1,0:T(1,128)S(1)} %bitcast.102), channel_id=1, replica_groups=mesh['thick'=8,'facade'=32] {'thick','facade'}, dimensions={0} | all-to-all | bytes 262144 | tf_op jit(solution)/shard_map/all_to_all | solution.py:624
  190.5 0.6 shard_map.131
  191.2 18.4 %all_to_all.106 = f32[256,1,128]{2,1,0:T(1,128)S(1)} all-to-all(f32[256,1,128]{2,1,0:T(1,128)S(1)} %bitcast.103), channel_id=1, replica_groups=mesh['thick'=8,'facade'=32] {'thick','facade'}, dimensions={0} | all-to-all | bytes 262144 | tf_op jit(solution)/shard_map/all_to_all | solution.py:624
  209.5 0.6 shard_map.132
  210.2 0.0 copy-start.9
  210.2 18.5 %all_to_all.107 = f32[256,1,128]{2,1,0:T(1,128)S(1)} all-to-all(f32[256,1,128]{2,1,0:T(1,128)S(1)} %bitcast.95), channel_id=1, replica_groups=mesh['thick'=8,'facade'=32] {'thick','facade'}, dimensions={0} | all-to-all | bytes 262144 | tf_op jit(solution)/shard_map/all_to_all | solution.py:624
  228.7 0.0 copy-done.9
  228.7 1.0 shard_map.133
  (11 shorter events, 0.1 us)
Async XLA Ops:
  0.6 5.4 %copy-start.1 = (f32[8,16,512]{2,1,0:T(8,128)S(1)}, f32[8,16,512]{2,1,0:T(8,128)}, u32[]{:S(2)}) copy-start(f32[8,16,512]{2,1,0:T(8,128)} %solid.3) | copy-start | bytes 786436
  2.7 4.6 %collective-permute-start = (f32[8,16,128]{2,1,0:T(8,128)}, f32[8,16,128]{2,1,0:T(8,128)S(1)}, u32[]{:S(2)}, u32[]{:S(2)}) collective-permute-start(f32[8,16,128]{2,1,0:T(8,128)} %get-tuple-element.41), channel_id=1, source_target_pairs={{0,1},{1,2},{2,3},{3,4},{4,5},{5,6},{6,7},{7,8},{8,9},{9,10},{10,1... | collective-permute-start | bytes 196616 | tf_op jit(solution)/shard_map/ppermute | solution.py:552
  5.3 0.9 copy-start.2
  5.3 3.9 %collective-permute-start.1 = (f32[8,16,128]{2,1,0:T(8,128)}, f32[8,16,128]{2,1,0:T(8,128)S(1)}, u32[]{:S(2)}, u32[]{:S(2)}) collective-permute-start(f32[8,16,128]{2,1,0:T(8,128)} %get-tuple-element.42), channel_id=1, source_target_pairs={{0,31},{1,0},{2,1},{3,2},{4,3},{5,4},{6,5},{7,6},{8,7},{9,8},{10,9... | collective-permute-start | bytes 196616 | tf_op jit(solution)/shard_map/ppermute | solution.py:552
  6.2 0.9 copy-start.3
  6.3 1.0 copy-start.4
  7.3 18.8 %copy-start = (s32[8,16,512]{2,1,0:T(8,128)S(1)}, s32[8,16,512]{2,1,0:T(8,128)}, u32[]{:S(2)}) copy-start(s32[8,16,512]{2,1,0:T(8,128)} %material.3) | copy-start | bytes 786436
  9.2 13.8 %collective-permute-start.3 = (f32[14,16,512]{2,1,0:T(8,128)S(1)}, f32[14,16,512]{2,1,0:T(8,128)S(1)}, u32[]{:S(2)}, u32[]{:S(2)}) collective-permute-start(f32[14,16,512]{2,1,0:T(8,128)S(1)} %fusion.3), channel_id=1, source_target_pairs={{0,224},{32,0},{64,32},{96,64},{128,96},{160,128},{192,160},{224,1... | collective-permute-start | bytes 1376264 | tf_op jit(solution)/shard_map/ppermute | solution.py:552
  15.2 10.9 %collective-permute-start.2 = (f32[14,16,512]{2,1,0:T(8,128)S(1)}, f32[14,16,512]{2,1,0:T(8,128)S(1)}, u32[]{:S(2)}, u32[]{:S(2)}) collective-permute-start(f32[14,16,512]{2,1,0:T(8,128)S(1)} %fusion.1), channel_id=1, source_target_pairs={{0,32},{32,64},{64,96},{96,128},{128,160},{160,192},{192,224},{224... | collective-permute-start | bytes 1376264 | tf_op jit(solution)/shard_map/ppermute | solution.py:552
  15.2 15.8 %copy-start.5 = (f32[8,16,512]{2,1,0:T(8,128)S(1)}, f32[8,16,512]{2,1,0:T(8,128)}, u32[]{:S(2)}) copy-start(f32[8,16,512]{2,1,0:T(8,128)} %newer.1) | copy-start | bytes 786436
  15.2 15.8 %copy-start.6 = (f32[8,16,512]{2,1,0:T(8,128)S(1)}, f32[8,16,512]{2,1,0:T(8,128)}, u32[]{:S(2)}) copy-start(f32[8,16,512]{2,1,0:T(8,128)} %older.1) | copy-start | bytes 786436
  15.3 15.8 %copy-start.7 = (f32[8,16,512]{2,1,0:T(8,128)S(1)}, f32[8,16,512]{2,1,0:T(8,128)}, u32[]{:S(2)}) copy-start(f32[8,16,512]{2,1,0:T(8,128)} %below_spacing.1) | copy-start | bytes 786436
  15.3 15.8 %copy-start.8 = (f32[8,16,512]{2,1,0:T(8,128)S(1)}, f32[8,16,512]{2,1,0:T(8,128)}, u32[]{:S(2)}) copy-start(f32[8,16,512]{2,1,0:T(8,128)} %above_spacing.1) | copy-start | bytes 786436
  28.3 5.5 %collective-permute-start.4 = (f32[4,16,640]{2,1,0:T(8,128)S(1)}, f32[4,16,640]{2,1,0:T(8,128)S(1)}, u32[]{:S(2)}, u32[]{:S(2)}) collective-permute-start(f32[4,16,640]{2,1,0:T(8,128)S(1)} %get-tuple-element.43.refs_2_), channel_id=1, source_target_pairs={{0,32},{32,64},{64,96},{96,128},{128,160},{160,192},{192,224},{224... | collective-permute-start | bytes 491528 | tf_op jit(solution)/shard_map/ppermute | solution.py:552
  28.4 5.4 %collective-permute-start.5 = (f32[4,16,640]{2,1,0:T(8,128)S(1)}, f32[4,16,640]{2,1,0:T(8,128)S(1)}, u32[]{:S(2)}, u32[]{:S(2)}) collective-permute-start(f32[4,16,640]{2,1,0:T(8,128)S(1)} %get-tuple-element.44.refs_1_), channel_id=1, source_target_pairs={{0,224},{32,0},{64,32},{96,64},{128,96},{160,128},{192,160},{224,1... | collective-permute-start | bytes 491528 | tf_op jit(solution)/shard_map/ppermute | solution.py:552
  40.2 5.4 %collective-permute-start.6 = (f32[4,16,640]{2,1,0:T(8,128)S(1)}, f32[4,16,640]{2,1,0:T(8,128)S(1)}, u32[]{:S(2)}, u32[]{:S(2)}) collective-permute-start(f32[4,16,640]{2,1,0:T(8,128)S(1)} %get-tuple-element.47.refs_2_), channel_id=1, source_target_pairs={{0,32},{32,64},{64,96},{96,128},{128,160},{160,192},{192,224},{224... | collective-permute-start | bytes 491528 | tf_op jit(solution)/shard_map/ppermute | solution.py:552
  40.2 5.4 %collective-permute-start.7 = (f32[4,16,640]{2,1,0:T(8,128)S(1)}, f32[4,16,640]{2,1,0:T(8,128)S(1)}, u32[]{:S(2)}, u32[]{:S(2)}) collective-permute-start(f32[4,16,640]{2,1,0:T(8,128)S(1)} %get-tuple-element.48.refs_1_), channel_id=1, source_target_pairs={{0,224},{32,0},{64,32},{96,64},{128,96},{160,128},{192,160},{224,1... | collective-permute-start | bytes 491528 | tf_op jit(solution)/shard_map/ppermute | solution.py:552
  210.2 18.5 %copy-start.9 = (f32[8,16,512]{2,1,0:T(8,128)S(1)}, f32[8,16,512]{2,1,0:T(8,128)}, u32[]{:S(2)}) copy-start(f32[8,16,512]{2,1,0:T(8,128)} %get-tuple-element.38.below) | copy-start | bytes 786436

commit v4 on v3

--- a/solution.py
+++ b/solution.py
@@ -153,13 +153,12 @@
 
 
 def corner(message, row):
-    lanes = slice(row * LANES, (row + 1) * LANES)
-    return message[12, :, lanes], message[13, :, lanes]
+    return message[row], message[4 + row]
 
 
 def rho_kernel(
     rows_total, cols_total, place,
-    density, material, from_above, from_below, left, right,
+    density, material, from_above, from_below, corner_above, corner_below, left, right,
     rho_out, cond_first, cond_last,
     ext, middle, summed,
 ):
@@ -171,9 +170,9 @@
 
     for r in range(4):
         ext[r, :, :own] = from_above[r] * has_above
-        ext[r, :, own:] = halo(corner(from_above, r), 0) * has_above
+        ext[r, :, own:] = halo(corner(corner_above, r), 0) * has_above
         ext[rows + 4 + r, :, :own] = from_below[r] * has_below
-        ext[rows + 4 + r, :, own:] = halo(corner(from_below, r), 0) * has_below
+        ext[rows + 4 + r, :, own:] = halo(corner(corner_below, r), 0) * has_below
     for r in range(rows):
         ext[4 + r, :, :own] = density[r]
         ext[4 + r, :, own:] = halo((left[r], right[r]), 0)
@@ -196,117 +195,186 @@
             cond_last[r - 4] = cond
 
 
-def sweep_kernel(
-    rows_total, cols_total, place,
-    cond_above, cond_first, cond_last, cond_below, rho, material,
-    prior, source, temp, from_above, from_below, left, right, tallies,
-    dual_out, weighted_first, weighted_last,
-    cond, field, load, heat, depth_face, height_face, lane_face, inverse, residual, next_field, dual,
+centre_value = 0.5 * (spectrum_high + spectrum_low)
+half_width = 0.5 * (spectrum_high - spectrum_low)
+ratio_value = centre_value / half_width
+INNER = range(5, 11)
+
+
+class Rows:
+    def __init__(self, ready, first, stop, rest):
+        self.ready, self.first, self.stop, self.rest = ready, first, stop, rest
+
+    def __getitem__(self, row):
+        if self.first <= row < self.stop:
+            return self.ready[row - self.first]
+        return self.rest[row]
+
+
+def face(one, other, store=None):
+    inv = 1.0 / jnp.maximum(one + other, 1e-3)
+    part = one * inv
+    if store is not None:
+        here, there, row = store
+        rest = other * inv
+        there[row] = part * part
+        here[row] = rest * rest
+    return 2.0 * part * other
+
+
+def first_residual(value, before, after, load, deep_before, deep, tall, wide):
+    inverse = 1.0 / (
+        loss_rate + (deep + deep_before) + (tall + behind(tall, 1, 0)) + (wide + behind(wide, 1, 1))
+    )
+    left_over = load - operate(value, deep_before * (before - value), deep * (value - after), tall, wide)
+    direction = left_over * inverse * (1.0 / centre_value)
+    return inverse, left_over, direction
+
+
+def operate(value, flux_before, flux, tall, wide):
+    high = tall * (value - ahead(value, 1, 0))
+    along = wide * (value - ahead(value, 1, 1))
+    return (
+        loss_rate * value + (flux - flux_before) + (high - behind(high, 1, 0))
+        + (along - behind(along, 1, 1))
+    )
+
+
+def prepare_kernel(
+    cond_first, cond_last, prior, source, temp,
+    from_above, from_below, corner_above, corner_below, left, right,
+    field, load, heat, depth_face, height_face, lane_face,
     depth_here, depth_there, height_here, height_there, lane_here, lane_there,
+    inverse, residual, direction, dual,
 ):
     rows, height, own = prior.shape
-    has_above, has_below, has_left, has_right = present(place, rows, own, rows_total, cols_total)
     last_level = sub_iota((height, 1)) == height - 1
-    for r in range(4):
-        cond[r] = cond_above[r] * has_above
-        cond[4 + r] = cond_first[r]
-        cond[8 + r] = cond_last[r]
-        cond[12 + r] = cond_below[r] * has_below
 
     def place_row(target, row, main, strips, index):
         target[row, :, :own] = main
         target[row, :, own:] = halo_lanes(strips[0], strips[1], index)
 
     for r in range(4):
-        place_row(field, r, from_above[4 + r], corner(from_above, r), 3)
-        place_row(field, 12 + r, from_below[4 + r], corner(from_below, r), 3)
+        place_row(field, r, from_above[4 + r], corner(corner_above, r), 3)
+        place_row(field, 12 + r, from_below[4 + r], corner(corner_below, r), 3)
     for r in range(3):
-        place_row(load, 1 + r, from_above[8 + r], corner(from_above, 1 + r), 2)
-        place_row(load, 12 + r, from_below[8 + r], corner(from_below, r), 2)
-    place_row(heat, 0, from_above[11], corner(from_above, 3), 4)
-    place_row(heat, 9, from_below[11], corner(from_below, 0), 4)
+        place_row(load, 1 + r, from_above[8 + r], corner(corner_above, 1 + r), 2)
+        place_row(load, 12 + r, from_below[8 + r], corner(corner_below, r), 2)
+    load[0] = jnp.zeros(load.shape[1:], f32)
+    load[15] = jnp.zeros(load.shape[1:], f32)
+    place_row(heat, 0, from_above[11], corner(corner_above, 3), 4)
+    place_row(heat, 9, from_below[11], corner(corner_below, 0), 4)
     for r in range(rows):
         strips = (left[r], right[r])
         place_row(field, 4 + r, prior[r], strips, 3)
         place_row(load, 4 + r, source[r], strips, 2)
         place_row(heat, 1 + r, temp[r], strips, 4)
 
-    centre = 0.5 * (spectrum_high + spectrum_low)
-    half = 0.5 * (spectrum_high - spectrum_low)
-    ratio = centre / half
-
-    def face(one, other, keep, row, here, there):
-        inv = 1.0 / jnp.maximum(one + other, 1e-3)
-        part = one * inv
-        if keep:
-            rest = other * inv
-            there[row] = part * part
-            here[row] = rest * rest
-        return 2.0 * part * other
-
-    here = cond[0]
-    following = cond[1]
-    deep_before = face(here, following, False, 0, depth_here, depth_there)
-    depth_face[0] = deep_before
-    flux_before = deep_before * (field[0] - field[1])
+    deep_before = None
+    following = cond_first[0]
+    for r in range(4, 12):
+        i = r - 4
+        here = following
+        tall = jnp.where(
+            last_level, 0.0, face(here, ahead(here, 1, 0), (height_here, height_there, i))
+        )
+        wide = face(here, ahead(here, 1, 1), (lane_here, lane_there, i))
+        height_face[i] = tall
+        lane_face[i] = wide
+        if r < 11:
+            following = cond_first[i + 1] if i < 3 else cond_last[i - 3]
+            deep = face(here, following, (depth_here, depth_there, i))
+            depth_face[i] = deep
+        if r in INNER:
+            value = field[r]
+            one, two, three = first_residual(
+                value, field[r - 1], field[r + 1], load[r], deep_before, deep, tall, wide
+            )
+            k = r - INNER.start
+            inverse[k], residual[k], direction[k] = one, two, three
+            dual[k] = value + three
+        deep_before = deep
+
+
+def sweep_kernel(
+    rows_total, cols_total, place,
+    cond_above, cond_first, cond_last, cond_below, rho, material,
+    field, load, heat, own_depth_face, own_height_face, own_lane_face,
+    own_depth_here, own_depth_there, height_here, height_there, lane_here, lane_there,
+    own_inverse, own_residual, own_direction, own_dual, left, right, tallies,
+    dual_out, weighted_first, weighted_last,
+    depth_face, height_face, lane_face, inverse, residual, first_direction, next_direction, dual,
+    edge_here, edge_there,
+):
+    rows, height, own = rho.shape[0], rho.shape[1], dual_out.shape[2]
+    has_above, has_below, has_left, has_right = present(place, rows, own, rows_total, cols_total)
+    last_level = sub_iota((height, 1)) == height - 1
+
+    def cond(r):
+        if r < 4:
+            return cond_above[r] * has_above
+        if r >= 12:
+            return cond_below[r - 12] * has_below
+        return cond_first[r - 4] if r < 8 else cond_last[r - 8]
+
+    depth_faces = Rows(own_depth_face, 4, 11, depth_face)
+    height_faces = Rows(own_height_face, 4, 12, height_face)
+    lane_faces = Rows(own_lane_face, 4, 12, lane_face)
+    inverses = Rows(own_inverse, INNER.start, INNER.stop, inverse)
+    residuals = Rows(own_residual, INNER.start, INNER.stop, residual)
+    directions = Rows(own_direction, INNER.start, INNER.stop, first_direction)
+    duals = Rows(own_dual, INNER.start, INNER.stop, dual)
+
+    following = cond(0)
+    for r in range(15):
+        if 4 <= r < 11:
+            following = None
+            continue
+        here = cond(r) if following is None else following
+        following = cond(r + 1)
+        store = (edge_here, edge_there, 0 if r == 3 else 1) if r in (3, 11) else None
+        depth_face[r] = face(here, following, store)
+        if r in (1, 2, 3, 12, 13, 14):
+            height_face[r] = jnp.where(last_level, 0.0, face(here, ahead(here, 1, 0)))
+            lane_face[r] = face(here, ahead(here, 1, 1))
     for r in range(1, 15):
-        here, following = following, cond[r + 1]
-        deep = face(here, following, 3 <= r < 12, r, depth_here, depth_there)
-        tall = face(here, ahead(here, 1, 0), 4 <= r < 12, r, height_here, height_there)
-        tall = jnp.where(last_level, 0.0, tall)
-        wide = face(here, ahead(here, 1, 1), 4 <= r < 12, r, lane_here, lane_there)
-        depth_face[r] = deep
-        height_face[r] = tall
-        lane_face[r] = wide
-        inv_diagonal = 1.0 / (
-            loss_rate + (deep + deep_before) + (tall + behind(tall, 1, 0))
-            + (wide + behind(wide, 1, 1))
-        )
-        inverse[r] = inv_diagonal
+        if r in INNER:
+            continue
         value = field[r]
-        flux = deep * (value - field[r + 1])
-        high = tall * (value - ahead(value, 1, 0))
-        along = wide * (value - ahead(value, 1, 1))
-        product = (
-            loss_rate * value + (flux - flux_before) + (high - behind(high, 1, 0))
-            + (along - behind(along, 1, 1))
-        )
-        left_over = load[r] - product
-        residual[r] = left_over
-        direction = left_over * inv_diagonal * (1.0 / centre)
-        next_field[r] = direction
+        one, two, three = first_residual(
+            value, field[r - 1], field[r + 1], load[r],
+            depth_faces[r - 1], depth_faces[r], height_faces[r], lane_faces[r],
+        )
+        inverse[r], residual[r], first_direction[r] = one, two, three
         if 3 <= r < 13:
-            dual[r] = value + direction
-        deep_before, flux_before = deep, flux
-
-    factor = 1.0 / ratio
-    now, then = next_field, field
+            dual[r] = value + three
+
+    factor = 1.0 / ratio_value
+    now = directions
     for sweep in range(SWEEPS - 1):
-        factor_next = 1.0 / (2.0 * ratio - factor)
-        keep, add = factor_next * factor, 2.0 * factor_next / half
+        factor_next = 1.0 / (2.0 * ratio_value - factor)
+        keep, add = factor_next * factor, 2.0 * factor_next / half_width
         start, stop = 2 + sweep, 14 - sweep
         following = now[start]
-        flux_before = depth_face[start - 1] * (now[start - 1] - following)
+        flux_before = depth_faces[start - 1] * (now[start - 1] - following)
         for r in range(start, stop):
             value, following = following, now[r + 1]
-            flux = depth_face[r] * (value - following)
-            high = height_face[r] * (value - ahead(value, 1, 0))
-            along = lane_face[r] * (value - ahead(value, 1, 1))
-            product = (
-                loss_rate * value + (flux - flux_before) + (high - behind(high, 1, 0))
-                + (along - behind(along, 1, 1))
+            flux = depth_faces[r] * (value - following)
+            left_over = residuals[r] - operate(
+                value, flux_before, flux, height_faces[r], lane_faces[r]
             )
-            left_over = residual[r] - product
+            direction = keep * value + add * (left_over * inverses[r])
             if sweep < SWEEPS - 2:
                 residual[r] = left_over
-            direction = keep * value + add * (left_over * inverse[r])
-            then[r] = direction
+                next_direction[r] = direction
             if 3 <= r < 13:
-                dual[r] = dual[r] + direction
+                dual[r] = duals[r] + direction
             flux_before = flux
         factor = factor_next
-        now, then = then, now
-
+        now, residuals, duals = next_direction, residual, dual
+
+    depth_here = Rows(own_depth_here, 4, 11, {11: edge_here[1]})
+    depth_there = Rows(own_depth_there, 4, 11, {3: edge_there[0], 11: edge_there[1]})
     plane = inverse_plane(height, own, cols_total, place[1])
     for r in range(rows):
         dual_out[r] = dual[4 + r, :, :own]
@@ -314,6 +382,7 @@
     a_next, t_next = dual[4], heat[1]
     deep_before = (a - a_next) * (t - t_next) * depth_there[3]
     for r in range(4, 4 + rows):
+        row = r - 4
         a, t = a_next, t_next
         a_next, t_next = dual[r + 1], heat[r - 2]
         deep = (a - a_next) * (t - t_next)
@@ -322,11 +391,10 @@
         wide = (a - ahead(a, 1, 1)) * (t - ahead(t, 1, 1))
         total = (
             (deep * depth_here[r] + deep_before)
-            + (tall * height_here[r] + behind(tall * height_there[r], 1, 0))
-            + (wide * lane_here[r] + behind(wide * lane_there[r], 1, 1))
+            + (tall * height_here[row] + behind(tall * height_there[row], 1, 0))
+            + (wide * lane_here[row] + behind(wide * lane_there[row], 1, 1))
         )
         deep_before = deep * depth_there[r]
-        row = r - 4
         strips = halo_lanes(left[row] * has_left, right[row] * has_right, 1)
         code = jnp.concatenate([material[row].astype(f32) + 1.0, strips], axis=1)
         thick_rho = rho[row]
@@ -559,23 +627,24 @@
     )
     right, left = to_left(first_strips), to_right(last_strips)
 
-    def side_by_side(strips, start):
-        return jnp.concatenate([strips[start + r] for r in range(4)], axis=1)[None]
-
-    def depth_message(last):
-        def end(value, count):
-            return value[rows - count:] if last else value[:count]
-
-        start = rows - 4 if last else 0
-        return jnp.concatenate(
+    from_above = to_deeper(
+        jnp.concatenate(
             [
-                end(solid_occupancy, 4), end(prior_dual_state, 4),
-                end(loss_state_derivative, 3), end(thermal_state, 1),
-                side_by_side(left, start), side_by_side(right, start),
+                solid_occupancy[rows - 4:], prior_dual_state[rows - 4:],
+                loss_state_derivative[rows - 3:], thermal_state[rows - 1:],
             ]
         )
-
-    from_above, from_below = to_deeper(depth_message(True)), to_nearer(depth_message(False))
+    )
+    from_below = to_nearer(
+        jnp.concatenate(
+            [
+                solid_occupancy[:4], prior_dual_state[:4],
+                loss_state_derivative[:3], thermal_state[:1],
+            ]
+        )
+    )
+    corner_above = to_deeper(jnp.concatenate([left[rows - 4:], right[rows - 4:]]))
+    corner_below = to_nearer(jnp.concatenate([left[:4], right[:4]]))
 
     (below, above, up, low, least, most, upper, lower, bend, tallies) = call(
         lines_kernel,
@@ -591,22 +660,32 @@
         rho_kernel, place,
         [(rows, height, width), four, four],
         (
-            solid_occupancy, cell_material, from_above, from_below, left, right,
+            solid_occupancy, cell_material, from_above, from_below, corner_above, corner_below,
+            left, right,
         ),
         [(BOTH_SIDES, height, width), (BOTH_SIDES - 4, height, width), (rows, height, width)],
         totals,
     )
     cond_above, cond_below = to_deeper(cond_last), to_nearer(cond_first)
-    tall = (BOTH_SIDES, height, width)
+    tall, own_wide, inner = (
+        (BOTH_SIDES, height, width), (rows, height, width), (len(INNER), height, width),
+    )
+    prepared = call(
+        prepare_kernel,
+        [tall, tall, (rows + 2, height, width)] + [own_wide] * 9 + [inner] * 4,
+        (
+            cond_first, cond_last, prior_dual_state, loss_state_derivative, thermal_state,
+            from_above, from_below, corner_above, corner_below, left, right,
+        ),
+    )
     dual_state, weighted_first, weighted_last = placed_call(
         sweep_kernel, place,
         [whole, four, four],
         (
-            cond_above, cond_first, cond_last, cond_below, rho, cell_material,
-            prior_dual_state, loss_state_derivative, thermal_state, from_above, from_below,
+            cond_above, cond_first, cond_last, cond_below, rho, cell_material, *prepared,
             left, right, tallies,
         ),
-        [tall, tall, tall, (10, height, width)] + [tall] * 13,
+        [tall] * 8 + [(2, height, width)] * 2,
         totals,
     )
     weighted_above, weighted_below = to_deeper(weighted_last), to_nearer(weighted_first)

time: 230 us -> 225 us (0.978)
  waiting for transfers between devices: 17.2 us -> 10.2 us
  starting transfers between devices: 14.7 us -> 17.3 us
    ppermute x8 -> x10, waiting for transfers between devices: 17.2 us -> 10.2 us  [turn(): return lambda value: lax.ppermute(value, axis, pairs)]
    ppermute x8 -> x10, starting transfers between devices: 14.7 us -> 17.3 us  [turn(): return lambda value: lax.ppermute(value, axis, pairs)]
    pallas_call x10 -> x11, Pallas kernels: 7.1 us -> 7.79 us  [call(): pl.pallas_call(kernel, out_shape=[jax.ShapeDtypeStruct(shape, f32) for sh...]
  transfers between devices with their start and end apart: 8 -> 10, of which waited for: 5 -> 3; matrix products, arithmetic and copies ran while one was open for 0% -> 0% of each run, Pallas kernels for 0% -> 1%
where the time goes in v4:
time: 225 us
  blocking collectives  177 us (79%)
  Pallas kernels  18.6 us (8%)
  starting transfers between devices  17.3 us (8%)
  waiting for transfers between devices  10.2 us (5%)
    all_to_all x9, blocking collectives, everyone(): return lax.all_to_all(rows_out, AXES, 0, 0, tiled=True)  177 us
    ppermute x10, starting transfers between devices, turn(): return lambda value: lax.ppermute(value, axis, pairs)  17.3 us
    ppermute x10, waiting for transfers between devices, turn(): return lambda value: lax.ppermute(value, axis, pairs)  10.2 us
    pallas_call x3, Pallas kernels, placed_call(): pl.pallas_call(with_place(kernel, *totals), out_shape=[jax.ShapeDtypeStru...  8.75 us
    pallas_call x11, Pallas kernels, call(): pl.pallas_call(kernel, out_shape=[jax.ShapeDtypeStruct(shape, f32) for sh...  7.79 us
  transfers between devices with their start and end apart: 10, of which 3 were waited for; matrix products, arithmetic and copies ran while one was open for 0% of the time, Pallas kernels for 1%

profile of v4, /device:TPU:1, one launch (start us, length us, event | category | flops | bytes accessed | tf_op | source)
XLA Modules:
  0.0 225.0 jit_solution(14579736977453952295)
XLA Ops:
  0.6 0.0 copy-start.2
  0.6 0.0 copy-start.1
  0.7 2.1 shard_map.120
  2.7 2.6 %collective-permute-start.2 = (f32[8,16,128]{2,1,0:T(8,128)}, f32[8,16,128]{2,1,0:T(8,128)S(1)}, u32[]{:S(2)}, u32[]{:S(2)}) collective-permute-start(f32[8,16,128]{2,1,0:T(8,128)} %get-tuple-element.57), channel_id=1, source_target_pairs={{0,1},{1,2},{2,3},{3,4},{4,5},{5,6},{6,7},{7,8},{8,9},{9,10},{10,1... | collective-permute-start | bytes 196616 | tf_op jit(solution)/shard_map/ppermute | solution.py:620
  5.3 0.0 copy-start.3
  5.3 0.7 collective-permute-start.3
  6.0 0.0 copy-done.2
  6.0 0.0 copy-done.1
  6.1 0.2 copy-done.3
  6.3 0.0 copy-start.4
  6.3 0.9 copy-done.4
  7.2 5.7 %collective-permute-start.1 = (f32[12,16,512]{2,1,0:T(8,128)S(1)}, f32[12,16,512]{2,1,0:T(8,128)S(1)}, u32[]{:S(2)}, u32[]{:S(2)}) collective-permute-start(f32[12,16,512]{2,1,0:T(8,128)S(1)} %pad_maximum_fusion.1), channel_id=1, source_target_pairs={{0,224},{32,0},{64,32},{96,64},{128,96},{160,128},{192,160},{224,1... | collective-permute-start | bytes 1179656 | tf_op jit(solution)/shard_map/ppermute | solution.py:620
  12.9 0.1 collective-permute-start
  13.0 0.0 copy-start
  13.0 0.0 collective-permute-done.2.refs_6_.left.refs_22_
  13.1 0.0 collective-permute-done.3.refs_7_.right.refs_23_
  13.1 0.1 collective-permute-start.4
  13.2 2.7 %collective-permute-start.5 = (f32[8,16,128]{2,1,0:T(8,128)S(1)}, f32[8,16,128]{2,1,0:T(8,128)S(1)}, u32[]{:S(2)}, u32[]{:S(2)}) collective-permute-start(f32[8,16,128]{2,1,0:T(8,128)S(1)} %pad_maximum_fusion.3), channel_id=1, source_target_pairs={{0,224},{32,0},{64,32},{96,64},{128,96},{160,128},{192,160},{224,1... | collective-permute-start | bytes 196616 | tf_op jit(solution)/shard_map/ppermute | solution.py:620
  15.9 0.1 pad_add_fusion.place_ref
  16.0 0.0 copy-start.5
  16.0 0.0 copy-start.6
  16.0 0.0 copy-start.7
  16.0 6.9 %collective-permute-done.4.refs_4_.corner_above = f32[8,16,128]{2,1,0:T(8,128)S(1)} collective-permute-done((f32[8,16,128]{2,1,0:T(8,128)S(1)}, f32[8,16,128]{2,1,0:T(8,128)S(1)}, u32[]{:S(2)}, u32[]{:S(2)}) %collective-permute-start.4) | collective-permute-done | bytes 65568 | tf_op jit(solution)/shard_map/ppermute | solution.py:620
  22.9 0.0 collective-permute-done.5.refs_5_.corner_below
  22.9 0.0 collective-permute-done.1.refs_3_.from_below
  22.9 0.0 collective-permute-done.refs_2_.from_above
  22.9 0.0 copy-done
  22.9 2.2 shard_map.121
  25.1 0.1 collective-permute-start.6
  25.2 2.7 %collective-permute-start.7 = (f32[4,16,640]{2,1,0:T(8,128)S(1)}, f32[4,16,640]{2,1,0:T(8,128)S(1)}, u32[]{:S(2)}, u32[]{:S(2)}) collective-permute-start(f32[4,16,640]{2,1,0:T(8,128)S(1)} %get-tuple-element.60.cond_first.refs_1_), channel_id=1, source_target_pairs={{0,224},{32,0},{64,32},{96,64},{128,96},{160,128},{192,160},{224,1... | collective-permute-start | bytes 491528 | tf_op jit(solution)/shard_map/ppermute | solution.py:620
  27.8 0.0 copy-done.5
  27.8 0.0 copy-done.6
  27.8 0.0 copy-done.7
  27.8 0.0 copy-done.8
  27.8 0.9 shard_map.123
  28.8 1.2 shard_map.122
  29.9 0.6 collective-permute-done.6.refs_0_
  30.5 0.0 collective-permute-done.7.refs_3_
  30.5 4.7 %shard_map.124 = (f32[8,16,512]{2,1,0:T(8,128)}, f32[4,16,640]{2,1,0:T(8,128)S(1)}, f32[4,16,640]{2,1,0:T(8,128)S(1)}) custom-call(s32[2]{0:T(128)S(1)} %pad_add_fusion.place_ref, f32[4,16,640]{2,1,0:T(8,128)S(1)} %collective-permute-done.6.refs_0_, f32[4,16,640]{2,1,0:T(8,128)S(1)} %get-tuple-element.60.cond_first.refs_1_, ...), custom_call_target="tpu_custom_call" | custom-call | tf_op jit(solution)/shard_map/pallas_call | solution.py:572
  35.2 0.0 collective-permute-start.8
  35.2 2.7 %collective-permute-start.9 = (f32[4,16,640]{2,1,0:T(8,128)S(1)}, f32[4,16,640]{2,1,0:T(8,128)S(1)}, u32[]{:S(2)}, u32[]{:S(2)}) collective-permute-start(f32[4,16,640]{2,1,0:T(8,128)S(1)} %get-tuple-element.80.refs_1_), channel_id=1, source_target_pairs={{0,224},{32,0},{64,32},{96,64},{128,96},{160,128},{192,160},{224,1... | collective-permute-start | bytes 491528 | tf_op jit(solution)/shard_map/ppermute | solution.py:620
  37.9 2.7 %collective-permute-done.8.refs_0_ = f32[4,16,640]{2,1,0:T(8,128)S(1)} collective-permute-done((f32[4,16,640]{2,1,0:T(8,128)S(1)}, f32[4,16,640]{2,1,0:T(8,128)S(1)}, u32[]{:S(2)}, u32[]{:S(2)}) %collective-permute-start.8) | collective-permute-done | bytes 163872 | tf_op jit(solution)/shard_map/ppermute | solution.py:620
  40.6 0.0 collective-permute-done.9.refs_3_
  40.6 1.9 shard_map.125
  42.5 29.5 %all_to_all.99 = f32[256,1,128]{2,1,0:T(1,128)S(1)} all-to-all(f32[256,1,128]{2,1,0:T(1,128)S(1)} %bitcast.48), channel_id=1, replica_groups=mesh['thick'=8,'facade'=32] {'thick','facade'}, dimensions={0} | all-to-all | bytes 262144 | tf_op jit(solution)/shard_map/all_to_all | solution.py:703
  72.0 0.6 shard_map.126
  72.7 18.4 %all_to_all.100 = f32[256,1,128]{2,1,0:T(1,128)S(1)} all-to-all(f32[256,1,128]{2,1,0:T(1,128)S(1)} %bitcast.49), channel_id=1, replica_groups=mesh['thick'=8,'facade'=32] {'thick','facade'}, dimensions={0} | all-to-all | bytes 262144 | tf_op jit(solution)/shard_map/all_to_all | solution.py:703
  91.0 0.6 shard_map.127
  91.6 18.4 %all_to_all.101 = f32[256,1,128]{2,1,0:T(1,128)S(1)} all-to-all(f32[256,1,128]{2,1,0:T(1,128)S(1)} %bitcast.50), channel_id=1, replica_groups=mesh['thick'=8,'facade'=32] {'thick','facade'}, dimensions={0} | all-to-all | bytes 262144 | tf_op jit(solution)/shard_map/all_to_all | solution.py:703
  110.0 0.6 shard_map.128
  110.6 18.4 %all_to_all.102 = f32[256,1,128]{2,1,0:T(1,128)S(1)} all-to-all(f32[256,1,128]{2,1,0:T(1,128)S(1)} %bitcast.51), channel_id=1, replica_groups=mesh['thick'=8,'facade'=32] {'thick','facade'}, dimensions={0} | all-to-all | bytes 262144 | tf_op jit(solution)/shard_map/all_to_all | solution.py:703
  128.9 0.6 shard_map.129
  129.5 18.4 %all_to_all.103 = f32[256,1,128]{2,1,0:T(1,128)S(1)} all-to-all(f32[256,1,128]{2,1,0:T(1,128)S(1)} %bitcast.52), channel_id=1, replica_groups=mesh['thick'=8,'facade'=32] {'thick','facade'}, dimensions={0} | all-to-all | bytes 262144 | tf_op jit(solution)/shard_map/all_to_all | solution.py:703
  147.8 0.6 shard_map.130
  148.4 18.6 %all_to_all.104 = f32[256,1,128]{2,1,0:T(1,128)S(1)} all-to-all(f32[256,1,128]{2,1,0:T(1,128)S(1)} %bitcast.53), channel_id=1, replica_groups=mesh['thick'=8,'facade'=32] {'thick','facade'}, dimensions={0} | all-to-all | bytes 262144 | tf_op jit(solution)/shard_map/all_to_all | solution.py:703
  167.0 0.6 shard_map.131
  167.6 18.4 %all_to_all.105 = f32[256,1,128]{2,1,0:T(1,128)S(1)} all-to-all(f32[256,1,128]{2,1,0:T(1,128)S(1)} %bitcast.54), channel_id=1, replica_groups=mesh['thick'=8,'facade'=32] {'thick','facade'}, dimensions={0} | all-to-all | bytes 262144 | tf_op jit(solution)/shard_map/all_to_all | solution.py:703
  185.9 0.6 shard_map.132
  186.5 18.4 %all_to_all.106 = f32[256,1,128]{2,1,0:T(1,128)S(1)} all-to-all(f32[256,1,128]{2,1,0:T(1,128)S(1)} %bitcast.55), channel_id=1, replica_groups=mesh['thick'=8,'facade'=32] {'thick','facade'}, dimensions={0} | all-to-all | bytes 262144 | tf_op jit(solution)/shard_map/all_to_all | solution.py:703
  204.9 0.6 shard_map.133
  205.5 0.0 copy-start.9
  205.5 18.5 %all_to_all.107 = f32[256,1,128]{2,1,0:T(1,128)S(1)} all-to-all(f32[256,1,128]{2,1,0:T(1,128)S(1)} %bitcast.47), channel_id=1, replica_groups=mesh['thick'=8,'facade'=32] {'thick','facade'}, dimensions={0} | all-to-all | bytes 262144 | tf_op jit(solution)/shard_map/all_to_all | solution.py:703
  223.9 0.0 copy-done.9
  224.0 1.0 shard_map.134
  (11 shorter events, 0.1 us)
Async XLA Ops:
  0.6 5.4 %copy-start.2 = (f32[8,16,512]{2,1,0:T(8,128)S(1)}, f32[8,16,512]{2,1,0:T(8,128)}, u32[]{:S(2)}) copy-start(f32[8,16,512]{2,1,0:T(8,128)} %prior.1) | copy-start | bytes 786436
  0.6 5.4 %copy-start.1 = (f32[8,16,512]{2,1,0:T(8,128)S(1)}, f32[8,16,512]{2,1,0:T(8,128)}, u32[]{:S(2)}) copy-start(f32[8,16,512]{2,1,0:T(8,128)} %solid.3) | copy-start | bytes 786436
  2.7 10.3 %collective-permute-start.2 = (f32[8,16,128]{2,1,0:T(8,128)}, f32[8,16,128]{2,1,0:T(8,128)S(1)}, u32[]{:S(2)}, u32[]{:S(2)}) collective-permute-start(f32[8,16,128]{2,1,0:T(8,128)} %get-tuple-element.57), channel_id=1, source_target_pairs={{0,1},{1,2},{2,3},{3,4},{4,5},{5,6},{6,7},{7,8},{8,9},{9,10},{10,1... | collective-permute-start | bytes 196616 | tf_op jit(solution)/shard_map/ppermute | solution.py:620
  5.3 0.9 copy-start.3
  5.3 7.8 %collective-permute-start.3 = (f32[8,16,128]{2,1,0:T(8,128)}, f32[8,16,128]{2,1,0:T(8,128)S(1)}, u32[]{:S(2)}, u32[]{:S(2)}) collective-permute-start(f32[8,16,128]{2,1,0:T(8,128)} %get-tuple-element.58), channel_id=1, source_target_pairs={{0,31},{1,0},{2,1},{3,2},{4,3},{5,4},{6,5},{7,6},{8,7},{9,8},{10,9... | collective-permute-start | bytes 196616 | tf_op jit(solution)/shard_map/ppermute | solution.py:620
  6.3 0.9 copy-start.4
  7.2 15.6 %collective-permute-start.1 = (f32[12,16,512]{2,1,0:T(8,128)S(1)}, f32[12,16,512]{2,1,0:T(8,128)S(1)}, u32[]{:S(2)}, u32[]{:S(2)}) collective-permute-start(f32[12,16,512]{2,1,0:T(8,128)S(1)} %pad_maximum_fusion.1), channel_id=1, source_target_pairs={{0,224},{32,0},{64,32},{96,64},{128,96},{160,128},{192,160},{224,1... | collective-permute-start | bytes 1179656 | tf_op jit(solution)/shard_map/ppermute | solution.py:620
  12.9 9.9 %collective-permute-start = (f32[12,16,512]{2,1,0:T(8,128)S(1)}, f32[12,16,512]{2,1,0:T(8,128)S(1)}, u32[]{:S(2)}, u32[]{:S(2)}) collective-permute-start(f32[12,16,512]{2,1,0:T(8,128)S(1)} %pad_maximum_fusion), channel_id=1, source_target_pairs={{0,32},{32,64},{64,96},{96,128},{128,160},{160,192},{192,224},{224... | collective-permute-start | bytes 1179656 | tf_op jit(solution)/shard_map/ppermute | solution.py:620
  13.0 9.9 %copy-start = (s32[8,16,512]{2,1,0:T(8,128)S(1)}, s32[8,16,512]{2,1,0:T(8,128)}, u32[]{:S(2)}) copy-start(s32[8,16,512]{2,1,0:T(8,128)} %material.3) | copy-start | bytes 786436
  13.1 9.8 %collective-permute-start.4 = (f32[8,16,128]{2,1,0:T(8,128)S(1)}, f32[8,16,128]{2,1,0:T(8,128)S(1)}, u32[]{:S(2)}, u32[]{:S(2)}) collective-permute-start(f32[8,16,128]{2,1,0:T(8,128)S(1)} %pad_maximum_fusion.2), channel_id=1, source_target_pairs={{0,32},{32,64},{64,96},{96,128},{128,160},{160,192},{192,224},{224... | collective-permute-start | bytes 196616 | tf_op jit(solution)/shard_map/ppermute | solution.py:620
  13.2 9.7 %collective-permute-start.5 = (f32[8,16,128]{2,1,0:T(8,128)S(1)}, f32[8,16,128]{2,1,0:T(8,128)S(1)}, u32[]{:S(2)}, u32[]{:S(2)}) collective-permute-start(f32[8,16,128]{2,1,0:T(8,128)S(1)} %pad_maximum_fusion.3), channel_id=1, source_target_pairs={{0,224},{32,0},{64,32},{96,64},{128,96},{160,128},{192,160},{224,1... | collective-permute-start | bytes 196616 | tf_op jit(solution)/shard_map/ppermute | solution.py:620
  16.0 11.8 %copy-start.5 = (f32[8,16,512]{2,1,0:T(8,128)S(1)}, f32[8,16,512]{2,1,0:T(8,128)}, u32[]{:S(2)}) copy-start(f32[8,16,512]{2,1,0:T(8,128)} %newer.1) | copy-start | bytes 786436
  16.0 11.8 %copy-start.6 = (f32[8,16,512]{2,1,0:T(8,128)S(1)}, f32[8,16,512]{2,1,0:T(8,128)}, u32[]{:S(2)}) copy-start(f32[8,16,512]{2,1,0:T(8,128)} %older.1) | copy-start | bytes 786436
  16.0 11.8 %copy-start.7 = (f32[8,16,512]{2,1,0:T(8,128)S(1)}, f32[8,16,512]{2,1,0:T(8,128)}, u32[]{:S(2)}) copy-start(f32[8,16,512]{2,1,0:T(8,128)} %below_spacing.1) | copy-start | bytes 786436
  16.0 11.8 %copy-start.8 = (f32[8,16,512]{2,1,0:T(8,128)S(1)}, f32[8,16,512]{2,1,0:T(8,128)}, u32[]{:S(2)}) copy-start(f32[8,16,512]{2,1,0:T(8,128)} %above_spacing.1) | copy-start | bytes 786436
  25.1 5.5 %collective-permute-start.6 = (f32[4,16,640]{2,1,0:T(8,128)S(1)}, f32[4,16,640]{2,1,0:T(8,128)S(1)}, u32[]{:S(2)}, u32[]{:S(2)}) collective-permute-start(f32[4,16,640]{2,1,0:T(8,128)S(1)} %get-tuple-element.59.cond_last.refs_2_), channel_id=1, source_target_pairs={{0,32},{32,64},{64,96},{96,128},{128,160},{160,192},{192,224},{224... | collective-permute-start | bytes 491528 | tf_op jit(solution)/shard_map/ppermute | solution.py:620
  25.2 5.4 %collective-permute-start.7 = (f32[4,16,640]{2,1,0:T(8,128)S(1)}, f32[4,16,640]{2,1,0:T(8,128)S(1)}, u32[]{:S(2)}, u32[]{:S(2)}) collective-permute-start(f32[4,16,640]{2,1,0:T(8,128)S(1)} %get-tuple-element.60.cond_first.refs_1_), channel_id=1, source_target_pairs={{0,224},{32,0},{64,32},{96,64},{128,96},{160,128},{192,160},{224,1... | collective-permute-start | bytes 491528 | tf_op jit(solution)/shard_map/ppermute | solution.py:620
  35.2 5.4 %collective-permute-start.8 = (f32[4,16,640]{2,1,0:T(8,128)S(1)}, f32[4,16,640]{2,1,0:T(8,128)S(1)}, u32[]{:S(2)}, u32[]{:S(2)}) collective-permute-start(f32[4,16,640]{2,1,0:T(8,128)S(1)} %get-tuple-element.79.refs_2_), channel_id=1, source_target_pairs={{0,32},{32,64},{64,96},{96,128},{128,160},{160,192},{192,224},{224... | collective-permute-start | bytes 491528 | tf_op jit(solution)/shard_map/ppermute | solution.py:620
  35.2 5.4 %collective-permute-start.9 = (f32[4,16,640]{2,1,0:T(8,128)S(1)}, f32[4,16,640]{2,1,0:T(8,128)S(1)}, u32[]{:S(2)}, u32[]{:S(2)}) collective-permute-start(f32[4,16,640]{2,1,0:T(8,128)S(1)} %get-tuple-element.80.refs_1_), channel_id=1, source_target_pairs={{0,224},{32,0},{64,32},{96,64},{128,96},{160,128},{192,160},{224,1... | collective-permute-start | bytes 491528 | tf_op jit(solution)/shard_map/ppermute | solution.py:620
  205.5 18.5 %copy-start.9 = (f32[8,16,512]{2,1,0:T(8,128)S(1)}, f32[8,16,512]{2,1,0:T(8,128)}, u32[]{:S(2)}) copy-start(f32[8,16,512]{2,1,0:T(8,128)} %get-tuple-element.54.below) | copy-start | bytes 786436

commit v5 on v4

--- a/solution.py
+++ b/solution.py
@@ -60,8 +60,9 @@
     return pltpu.roll(value, step, axis)
 
 
-def pack_kernel(*refs):
-    firsts, lasts, to_left, to_right = refs[0:5], refs[5:10], refs[10], refs[11]
+def launch_kernel(*refs):
+    firsts, lasts, nears, fars = refs[0:5], refs[5:10], refs[10:14], refs[14:18]
+    to_left, to_right, rows_up, rows_down = refs[18:]
     rows, height, _ = to_left.shape
     group = lane_iota((height, LANES)) // STRIP
     for row in range(rows):
@@ -76,6 +77,12 @@
                     value = pltpu.roll(value, shift, 1)
                 packed = jnp.where(group == index, value, packed)
             target[row] = packed
+    start = 0
+    for near, far, count in zip(nears, fars, (4, 4, 3, 1)):
+        for r in range(count):
+            rows_down[start + r] = near[r]
+            rows_up[start + r] = far[far.shape[0] - count + r]
+        start += count
 
 
 def halo_lanes(left, right, index):
@@ -579,20 +586,26 @@
     )(place, *args)
 
 
-def pack_strips(arrays):
-    rows, height, own = arrays[0].shape
+def launch_messages(density, material, source, prior, temp):
+    rows, height, own = density.shape
     end = own // LANES - 1
-    block = (rows, height, LANES)
+    block, message = (rows, height, LANES), (12, height, own)
     first = pl.BlockSpec(block, lambda i: (0, 0, 0))
     last = pl.BlockSpec(block, lambda i: (0, 0, end))
-    out = pl.BlockSpec(block, lambda i: (0, 0, 0))
+
+    def layers(count, index):
+        return pl.BlockSpec((count, height, own), lambda i: (index, 0, 0))
+
+    strips = (density, material, source, prior, temp)
+    layered = (density, prior, source, temp)
     return pl.pallas_call(
-        pack_kernel,
+        launch_kernel,
         grid=(1,),
-        out_shape=[jax.ShapeDtypeStruct(block, f32)] * 2,
-        in_specs=[first] * 5 + [last] * 5,
-        out_specs=[out] * 2,
-    )(*arrays, *arrays)
+        out_shape=[jax.ShapeDtypeStruct(s, f32) for s in (block, block, message, message)],
+        in_specs=[first] * 5 + [last] * 5
+        + [layers(4, 0)] * 3 + [layers(1, 0)] + [layers(4, rows // 4 - 1)] * 3 + [layers(1, rows - 1)],
+        out_specs=[pl.BlockSpec(s, lambda i: (0, 0, 0)) for s in (block, block, message, message)],
+    )(*strips, *strips, *layered, *layered)
 
 
 def on_device(
@@ -622,27 +635,11 @@
     to_right, to_left = turn("facade", long, 1), turn("facade", long, -1)
     to_deeper, to_nearer = turn("thick", deep, 1), turn("thick", deep, -1)
 
-    first_strips, last_strips = pack_strips(
-        (solid_occupancy, cell_material, loss_state_derivative, prior_dual_state, thermal_state)
+    first_strips, last_strips, rows_up, rows_down = launch_messages(
+        solid_occupancy, cell_material, loss_state_derivative, prior_dual_state, thermal_state
     )
     right, left = to_left(first_strips), to_right(last_strips)
-
-    from_above = to_deeper(
-        jnp.concatenate(
-            [
-                solid_occupancy[rows - 4:], prior_dual_state[rows - 4:],
-                loss_state_derivative[rows - 3:], thermal_state[rows - 1:],
-            ]
-        )
-    )
-    from_below = to_nearer(
-        jnp.concatenate(
-            [
-                solid_occupancy[:4], prior_dual_state[:4],
-                loss_state_derivative[:3], thermal_state[:1],
-            ]
-        )
-    )
+    from_above, from_below = to_deeper(rows_up), to_nearer(rows_down)
     corner_above = to_deeper(jnp.concatenate([left[rows - 4:], right[rows - 4:]]))
     corner_below = to_nearer(jnp.concatenate([left[:4], right[:4]]))
 
@@ -660,8 +657,8 @@
         rho_kernel, place,
         [(rows, height, width), four, four],
         (
-            solid_occupancy, cell_material, from_above, from_below, corner_above, corner_below,
-            left, right,
+            solid_occupancy, cell_material, from_above, from_below,
+            corner_above, corner_below, left, right,
         ),
         [(BOTH_SIDES, height, width), (BOTH_SIDES - 4, height, width), (rows, height, width)],
         totals,

time: 225 us -> 223 us (level)
  transfers between devices with their start and end apart: 10 -> 10, of which waited for: 3 -> 4; matrix products, arithmetic and copies ran while one was open for 0% -> 0% of each run, Pallas kernels for 1% -> 1%
where the time goes in v5:
time: 223 us; the launch traced here: 222 us
  blocking collectives  176 us (79%)
  Pallas kernels  19.2 us (9%)
  starting transfers between devices  17.9 us (8%)
  waiting for transfers between devices  8.58 us (4%)
    all_to_all x9, blocking collectives, everyone(): return lax.all_to_all(rows_out, AXES, 0, 0, tiled=True)  176 us
    ppermute x10, starting transfers between devices, turn(): return lambda value: lax.ppermute(value, axis, pairs)  17.9 us
    pallas_call x3, Pallas kernels, placed_call(): pl.pallas_call(with_place(kernel, *totals), out_shape=[jax.ShapeDtypeStru...  8.78 us
    ppermute x10, waiting for transfers between devices, turn(): return lambda value: lax.ppermute(value, axis, pairs)  8.58 us
    pallas_call x11, Pallas kernels, call(): pl.pallas_call(kernel, out_shape=[jax.ShapeDtypeStruct(shape, f32) for sh...  7.79 us
  transfers between devices with their start and end apart: 10, of which 4 were waited for; matrix products, arithmetic and copies ran while one was open for 0% of the time, Pallas kernels for 1%

profile of v5, /device:TPU:1, one launch (start us, length us, event | category | flops | bytes accessed | tf_op | source)
XLA Modules:
  0.0 222.4 jit_solution(5626437687211191934)
XLA Ops:
  0.6 2.6 %shard_map.120 = (f32[8,16,128]{2,1,0:T(8,128)}, f32[8,16,128]{2,1,0:T(8,128)}, f32[12,16,512]{2,1,0:T(8,128)}, f32[12,16,512]{2,1,0:T(8,128)}) custom-call(f32[8,16,512]{2,1,0:T(8,128)} %solid.3, s32[8,16,512]{2,1,0:T(8,128)} %material.3, f32[8,16,512]{2,1,0:T(8,128)} %source.1, f32[8,16,512]{2,1,0:T(8,128)} %prior.1, f32[8,16,512]{2,1,0:T(8,128)} %temp.1, ...), custom_call_target="tpu_custom_call" | custom-call | tf_op jit(solution)/shard_map/pallas_call | solution.py:601
  3.2 2.7 %collective-permute-start.2 = (f32[8,16,128]{2,1,0:T(8,128)}, f32[8,16,128]{2,1,0:T(8,128)S(1)}, u32[]{:S(2)}, u32[]{:S(2)}) collective-permute-start(f32[8,16,128]{2,1,0:T(8,128)} %get-tuple-element.61), channel_id=1, source_target_pairs={{0,1},{1,2},{2,3},{3,4},{4,5},{5,6},{6,7},{7,8},{8,9},{9,10},{10,1... | collective-permute-start | bytes 196616 | tf_op jit(solution)/shard_map/ppermute | solution.py:633
  5.9 0.7 collective-permute-start.3
  6.6 0.9 collective-permute-start
  7.5 3.9 %collective-permute-start.1 = (f32[12,16,512]{2,1,0:T(8,128)}, f32[12,16,512]{2,1,0:T(8,128)S(1)}, u32[]{:S(2)}, u32[]{:S(2)}) collective-permute-start(f32[12,16,512]{2,1,0:T(8,128)} %get-tuple-element.60), channel_id=1, source_target_pairs={{0,224},{32,0},{64,32},{96,64},{128,96},{160,128},{192,160},{224,1... | collective-permute-start | bytes 1179656 | tf_op jit(solution)/shard_map/ppermute | solution.py:633
  11.5 0.0 copy-start
  11.5 0.0 copy-start.1
  11.5 0.0 collective-permute-done.2.refs_6_.left.refs_22_
  11.5 0.0 collective-permute-done.3.refs_7_.right.refs_23_
  11.5 4.2 %collective-permute-start.5 = (f32[8,16,128]{2,1,0:T(8,128)S(1)}, f32[8,16,128]{2,1,0:T(8,128)S(1)}, u32[]{:S(2)}, u32[]{:S(2)}) collective-permute-start(f32[8,16,128]{2,1,0:T(8,128)S(1)} %pad_maximum_fusion.1), channel_id=1, source_target_pairs={{0,224},{32,0},{64,32},{96,64},{128,96},{160,128},{192,160},{224,1... | collective-permute-start | bytes 196616 | tf_op jit(solution)/shard_map/ppermute | solution.py:633
  15.8 0.0 collective-permute-start.4
  15.8 0.1 pad_add_fusion.place_ref
  15.8 0.0 copy-start.5
  15.8 0.0 copy-start.6
  15.9 0.0 copy-start.7
  15.9 1.7 collective-permute-done.5.refs_5_.corner_below
  17.5 3.6 %collective-permute-done.4.refs_4_.corner_above = f32[8,16,128]{2,1,0:T(8,128)S(1)} collective-permute-done((f32[8,16,128]{2,1,0:T(8,128)S(1)}, f32[8,16,128]{2,1,0:T(8,128)S(1)}, u32[]{:S(2)}, u32[]{:S(2)}) %collective-permute-start.4) | collective-permute-done | bytes 65568 | tf_op jit(solution)/shard_map/ppermute | solution.py:633
  21.2 0.0 collective-permute-done.refs_2_.from_above
  21.2 0.0 collective-permute-done.1.refs_3_.from_below
  21.2 0.0 copy-done
  21.2 0.0 copy-done.1
  21.2 2.2 shard_map.121
  23.4 0.1 collective-permute-start.6
  23.5 0.0 copy-start.2
  23.5 0.0 copy-start.3
  23.5 0.0 copy-start.4
  23.5 2.6 %collective-permute-start.7 = (f32[4,16,640]{2,1,0:T(8,128)S(1)}, f32[4,16,640]{2,1,0:T(8,128)S(1)}, u32[]{:S(2)}, u32[]{:S(2)}) collective-permute-start(f32[4,16,640]{2,1,0:T(8,128)S(1)} %get-tuple-element.64.cond_first.refs_1_), channel_id=1, source_target_pairs={{0,224},{32,0},{64,32},{96,64},{128,96},{160,128},{192,160},{224,1... | collective-permute-start | bytes 491528 | tf_op jit(solution)/shard_map/ppermute | solution.py:633
  26.1 0.0 copy-done.5
  26.1 0.0 copy-done.6
  26.1 0.0 copy-done.7
  26.1 0.0 copy-done.8
  26.1 0.9 shard_map.123
  27.1 0.0 copy-done.2
  27.1 0.0 copy-done.3
  27.1 0.0 copy-done.4
  27.1 1.2 shard_map.122
  28.3 0.6 collective-permute-done.6.refs_0_
  28.8 0.0 collective-permute-done.7.refs_3_
  28.8 4.7 %shard_map.124 = (f32[8,16,512]{2,1,0:T(8,128)}, f32[4,16,640]{2,1,0:T(8,128)S(1)}, f32[4,16,640]{2,1,0:T(8,128)S(1)}) custom-call(s32[2]{0:T(128)S(1)} %pad_add_fusion.place_ref, f32[4,16,640]{2,1,0:T(8,128)S(1)} %collective-permute-done.6.refs_0_, f32[4,16,640]{2,1,0:T(8,128)S(1)} %get-tuple-element.64.cond_first.refs_1_, ...), custom_call_target="tpu_custom_call" | custom-call | tf_op jit(solution)/shard_map/pallas_call | solution.py:579
  33.5 0.0 collective-permute-start.8
  33.5 2.7 %collective-permute-start.9 = (f32[4,16,640]{2,1,0:T(8,128)S(1)}, f32[4,16,640]{2,1,0:T(8,128)S(1)}, u32[]{:S(2)}, u32[]{:S(2)}) collective-permute-start(f32[4,16,640]{2,1,0:T(8,128)S(1)} %get-tuple-element.84.refs_1_), channel_id=1, source_target_pairs={{0,224},{32,0},{64,32},{96,64},{128,96},{160,128},{192,160},{224,1... | collective-permute-start | bytes 491528 | tf_op jit(solution)/shard_map/ppermute | solution.py:633
  36.2 2.7 %collective-permute-done.8.refs_0_ = f32[4,16,640]{2,1,0:T(8,128)S(1)} collective-permute-done((f32[4,16,640]{2,1,0:T(8,128)S(1)}, f32[4,16,640]{2,1,0:T(8,128)S(1)}, u32[]{:S(2)}, u32[]{:S(2)}) %collective-permute-start.8) | collective-permute-done | bytes 163872 | tf_op jit(solution)/shard_map/ppermute | solution.py:633
  38.9 0.0 collective-permute-done.9.refs_3_
  38.9 1.9 shard_map.125
  40.8 28.6 %all_to_all.99 = f32[256,1,128]{2,1,0:T(1,128)S(1)} all-to-all(f32[256,1,128]{2,1,0:T(1,128)S(1)} %bitcast.48), channel_id=1, replica_groups=mesh['thick'=8,'facade'=32] {'thick','facade'}, dimensions={0} | all-to-all | bytes 262144 | tf_op jit(solution)/shard_map/all_to_all | solution.py:700
  69.4 0.6 shard_map.126
  70.1 18.4 %all_to_all.100 = f32[256,1,128]{2,1,0:T(1,128)S(1)} all-to-all(f32[256,1,128]{2,1,0:T(1,128)S(1)} %bitcast.49), channel_id=1, replica_groups=mesh['thick'=8,'facade'=32] {'thick','facade'}, dimensions={0} | all-to-all | bytes 262144 | tf_op jit(solution)/shard_map/all_to_all | solution.py:700
  88.4 0.6 shard_map.127
  89.0 18.4 %all_to_all.101 = f32[256,1,128]{2,1,0:T(1,128)S(1)} all-to-all(f32[256,1,128]{2,1,0:T(1,128)S(1)} %bitcast.50), channel_id=1, replica_groups=mesh['thick'=8,'facade'=32] {'thick','facade'}, dimensions={0} | all-to-all | bytes 262144 | tf_op jit(solution)/shard_map/all_to_all | solution.py:700
  107.4 0.6 shard_map.128
  107.9 18.4 %all_to_all.102 = f32[256,1,128]{2,1,0:T(1,128)S(1)} all-to-all(f32[256,1,128]{2,1,0:T(1,128)S(1)} %bitcast.51), channel_id=1, replica_groups=mesh['thick'=8,'facade'=32] {'thick','facade'}, dimensions={0} | all-to-all | bytes 262144 | tf_op jit(solution)/shard_map/all_to_all | solution.py:700
  126.3 0.6 shard_map.129
  126.9 18.4 %all_to_all.103 = f32[256,1,128]{2,1,0:T(1,128)S(1)} all-to-all(f32[256,1,128]{2,1,0:T(1,128)S(1)} %bitcast.52), channel_id=1, replica_groups=mesh['thick'=8,'facade'=32] {'thick','facade'}, dimensions={0} | all-to-all | bytes 262144 | tf_op jit(solution)/shard_map/all_to_all | solution.py:700
  145.2 0.6 shard_map.130
  145.8 18.6 %all_to_all.104 = f32[256,1,128]{2,1,0:T(1,128)S(1)} all-to-all(f32[256,1,128]{2,1,0:T(1,128)S(1)} %bitcast.53), channel_id=1, replica_groups=mesh['thick'=8,'facade'=32] {'thick','facade'}, dimensions={0} | all-to-all | bytes 262144 | tf_op jit(solution)/shard_map/all_to_all | solution.py:700
  164.4 0.6 shard_map.131
  165.0 18.4 %all_to_all.105 = f32[256,1,128]{2,1,0:T(1,128)S(1)} all-to-all(f32[256,1,128]{2,1,0:T(1,128)S(1)} %bitcast.54), channel_id=1, replica_groups=mesh['thick'=8,'facade'=32] {'thick','facade'}, dimensions={0} | all-to-all | bytes 262144 | tf_op jit(solution)/shard_map/all_to_all | solution.py:700
  183.3 0.6 shard_map.132
  183.9 18.4 %all_to_all.106 = f32[256,1,128]{2,1,0:T(1,128)S(1)} all-to-all(f32[256,1,128]{2,1,0:T(1,128)S(1)} %bitcast.55), channel_id=1, replica_groups=mesh['thick'=8,'facade'=32] {'thick','facade'}, dimensions={0} | all-to-all | bytes 262144 | tf_op jit(solution)/shard_map/all_to_all | solution.py:700
  202.3 0.6 shard_map.133
  202.8 0.0 copy-start.9
  202.9 18.5 %all_to_all.107 = f32[256,1,128]{2,1,0:T(1,128)S(1)} all-to-all(f32[256,1,128]{2,1,0:T(1,128)S(1)} %bitcast.47), channel_id=1, replica_groups=mesh['thick'=8,'facade'=32] {'thick','facade'}, dimensions={0} | all-to-all | bytes 262144 | tf_op jit(solution)/shard_map/all_to_all | solution.py:700
  221.3 0.0 copy-done.9
  221.3 1.0 shard_map.134
  (6 shorter events, 0.0 us)
Async XLA Ops:
  3.2 8.3 %collective-permute-start.2 = (f32[8,16,128]{2,1,0:T(8,128)}, f32[8,16,128]{2,1,0:T(8,128)S(1)}, u32[]{:S(2)}, u32[]{:S(2)}) collective-permute-start(f32[8,16,128]{2,1,0:T(8,128)} %get-tuple-element.61), channel_id=1, source_target_pairs={{0,1},{1,2},{2,3},{3,4},{4,5},{5,6},{6,7},{7,8},{8,9},{9,10},{10,1... | collective-permute-start | bytes 196616 | tf_op jit(solution)/shard_map/ppermute | solution.py:633
  5.9 5.6 %collective-permute-start.3 = (f32[8,16,128]{2,1,0:T(8,128)}, f32[8,16,128]{2,1,0:T(8,128)S(1)}, u32[]{:S(2)}, u32[]{:S(2)}) collective-permute-start(f32[8,16,128]{2,1,0:T(8,128)} %get-tuple-element.62), channel_id=1, source_target_pairs={{0,31},{1,0},{2,1},{3,2},{4,3},{5,4},{6,5},{7,6},{8,7},{9,8},{10,9... | collective-permute-start | bytes 196616 | tf_op jit(solution)/shard_map/ppermute | solution.py:633
  6.6 14.5 %collective-permute-start = (f32[12,16,512]{2,1,0:T(8,128)}, f32[12,16,512]{2,1,0:T(8,128)S(1)}, u32[]{:S(2)}, u32[]{:S(2)}) collective-permute-start(f32[12,16,512]{2,1,0:T(8,128)} %get-tuple-element.59), channel_id=1, source_target_pairs={{0,32},{32,64},{64,96},{96,128},{128,160},{160,192},{192,224},{224... | collective-permute-start | bytes 1179656 | tf_op jit(solution)/shard_map/ppermute | solution.py:633
  7.5 13.6 %collective-permute-start.1 = (f32[12,16,512]{2,1,0:T(8,128)}, f32[12,16,512]{2,1,0:T(8,128)S(1)}, u32[]{:S(2)}, u32[]{:S(2)}) collective-permute-start(f32[12,16,512]{2,1,0:T(8,128)} %get-tuple-element.60), channel_id=1, source_target_pairs={{0,224},{32,0},{64,32},{96,64},{128,96},{160,128},{192,160},{224,1... | collective-permute-start | bytes 1179656 | tf_op jit(solution)/shard_map/ppermute | solution.py:633
  11.5 9.7 %copy-start = (s32[8,16,512]{2,1,0:T(8,128)S(1)}, s32[8,16,512]{2,1,0:T(8,128)}, u32[]{:S(2)}) copy-start(s32[8,16,512]{2,1,0:T(8,128)} %material.3) | copy-start | bytes 786436
  11.5 9.7 %copy-start.1 = (f32[8,16,512]{2,1,0:T(8,128)S(1)}, f32[8,16,512]{2,1,0:T(8,128)}, u32[]{:S(2)}) copy-start(f32[8,16,512]{2,1,0:T(8,128)} %solid.3) | copy-start | bytes 786436
  11.5 6.0 %collective-permute-start.5 = (f32[8,16,128]{2,1,0:T(8,128)S(1)}, f32[8,16,128]{2,1,0:T(8,128)S(1)}, u32[]{:S(2)}, u32[]{:S(2)}) collective-permute-start(f32[8,16,128]{2,1,0:T(8,128)S(1)} %pad_maximum_fusion.1), channel_id=1, source_target_pairs={{0,224},{32,0},{64,32},{96,64},{128,96},{160,128},{192,160},{224,1... | collective-permute-start | bytes 196616 | tf_op jit(solution)/shard_map/ppermute | solution.py:633
  15.8 5.4 %collective-permute-start.4 = (f32[8,16,128]{2,1,0:T(8,128)S(1)}, f32[8,16,128]{2,1,0:T(8,128)S(1)}, u32[]{:S(2)}, u32[]{:S(2)}) collective-permute-start(f32[8,16,128]{2,1,0:T(8,128)S(1)} %pad_maximum_fusion), channel_id=1, source_target_pairs={{0,32},{32,64},{64,96},{96,128},{128,160},{160,192},{192,224},{224... | collective-permute-start | bytes 196616 | tf_op jit(solution)/shard_map/ppermute | solution.py:633
  15.8 10.3 %copy-start.5 = (f32[8,16,512]{2,1,0:T(8,128)S(1)}, f32[8,16,512]{2,1,0:T(8,128)}, u32[]{:S(2)}) copy-start(f32[8,16,512]{2,1,0:T(8,128)} %newer.1) | copy-start | bytes 786436
  15.8 10.3 %copy-start.6 = (f32[8,16,512]{2,1,0:T(8,128)S(1)}, f32[8,16,512]{2,1,0:T(8,128)}, u32[]{:S(2)}) copy-start(f32[8,16,512]{2,1,0:T(8,128)} %older.1) | copy-start | bytes 786436
  15.9 10.3 %copy-start.7 = (f32[8,16,512]{2,1,0:T(8,128)S(1)}, f32[8,16,512]{2,1,0:T(8,128)}, u32[]{:S(2)}) copy-start(f32[8,16,512]{2,1,0:T(8,128)} %below_spacing.1) | copy-start | bytes 786436
  15.9 10.3 %copy-start.8 = (f32[8,16,512]{2,1,0:T(8,128)S(1)}, f32[8,16,512]{2,1,0:T(8,128)}, u32[]{:S(2)}) copy-start(f32[8,16,512]{2,1,0:T(8,128)} %above_spacing.1) | copy-start | bytes 786436
  23.4 5.5 %collective-permute-start.6 = (f32[4,16,640]{2,1,0:T(8,128)S(1)}, f32[4,16,640]{2,1,0:T(8,128)S(1)}, u32[]{:S(2)}, u32[]{:S(2)}) collective-permute-start(f32[4,16,640]{2,1,0:T(8,128)S(1)} %get-tuple-element.63.cond_last.refs_2_), channel_id=1, source_target_pairs={{0,32},{32,64},{64,96},{96,128},{128,160},{160,192},{192,224},{224... | collective-permute-start | bytes 491528 | tf_op jit(solution)/shard_map/ppermute | solution.py:633
  23.5 3.6 %copy-start.2 = (f32[8,16,512]{2,1,0:T(8,128)S(1)}, f32[8,16,512]{2,1,0:T(8,128)}, u32[]{:S(2)}) copy-start(f32[8,16,512]{2,1,0:T(8,128)} %source.1) | copy-start | bytes 786436
  23.5 3.6 %copy-start.3 = (f32[8,16,512]{2,1,0:T(8,128)S(1)}, f32[8,16,512]{2,1,0:T(8,128)}, u32[]{:S(2)}) copy-start(f32[8,16,512]{2,1,0:T(8,128)} %prior.1) | copy-start | bytes 786436
  23.5 3.6 %copy-start.4 = (f32[8,16,512]{2,1,0:T(8,128)S(1)}, f32[8,16,512]{2,1,0:T(8,128)}, u32[]{:S(2)}) copy-start(f32[8,16,512]{2,1,0:T(8,128)} %temp.1) | copy-start | bytes 786436
  23.5 5.3 %collective-permute-start.7 = (f32[4,16,640]{2,1,0:T(8,128)S(1)}, f32[4,16,640]{2,1,0:T(8,128)S(1)}, u32[]{:S(2)}, u32[]{:S(2)}) collective-permute-start(f32[4,16,640]{2,1,0:T(8,128)S(1)} %get-tuple-element.64.cond_first.refs_1_), channel_id=1, source_target_pairs={{0,224},{32,0},{64,32},{96,64},{128,96},{160,128},{192,160},{224,1... | collective-permute-start | bytes 491528 | tf_op jit(solution)/shard_map/ppermute | solution.py:633
  33.5 5.4 %collective-permute-start.8 = (f32[4,16,640]{2,1,0:T(8,128)S(1)}, f32[4,16,640]{2,1,0:T(8,128)S(1)}, u32[]{:S(2)}, u32[]{:S(2)}) collective-permute-start(f32[4,16,640]{2,1,0:T(8,128)S(1)} %get-tuple-element.83.refs_2_), channel_id=1, source_target_pairs={{0,32},{32,64},{64,96},{96,128},{128,160},{160,192},{192,224},{224... | collective-permute-start | bytes 491528 | tf_op jit(solution)/shard_map/ppermute | solution.py:633
  33.5 5.4 %collective-permute-start.9 = (f32[4,16,640]{2,1,0:T(8,128)S(1)}, f32[4,16,640]{2,1,0:T(8,128)S(1)}, u32[]{:S(2)}, u32[]{:S(2)}) collective-permute-start(f32[4,16,640]{2,1,0:T(8,128)S(1)} %get-tuple-element.84.refs_1_), channel_id=1, source_target_pairs={{0,224},{32,0},{64,32},{96,64},{128,96},{160,128},{192,160},{224,1... | collective-permute-start | bytes 491528 | tf_op jit(solution)/shard_map/ppermute | solution.py:633
  202.8 18.5 %copy-start.9 = (f32[8,16,512]{2,1,0:T(8,128)S(1)}, f32[8,16,512]{2,1,0:T(8,128)}, u32[]{:S(2)}) copy-start(f32[8,16,512]{2,1,0:T(8,128)} %get-tuple-element.56.below) | copy-start | bytes 786436

commit v6 on v5

--- a/solution.py
+++ b/solution.py
@@ -62,11 +62,14 @@
 
 def launch_kernel(*refs):
     firsts, lasts, nears, fars = refs[0:5], refs[5:10], refs[10:14], refs[14:18]
-    to_left, to_right, rows_up, rows_down = refs[18:]
+    to_left, to_right, rows_up, rows_down = refs[18:22]
+    left_corners, right_corners = refs[22:24], refs[24:26]
     rows, height, _ = to_left.shape
     group = lane_iota((height, LANES)) // STRIP
     for row in range(rows):
-        for source, target, place in ((firsts, to_left, 0), (lasts, to_right, LANES - STRIP)):
+        for source, target, corners, place in (
+            (firsts, to_left, left_corners, 0), (lasts, to_right, right_corners, LANES - STRIP)
+        ):
             packed = jnp.zeros((height, LANES), f32)
             for index, ref in enumerate(source):
                 value = ref[row]
@@ -77,6 +80,10 @@
                     value = pltpu.roll(value, shift, 1)
                 packed = jnp.where(group == index, value, packed)
             target[row] = packed
+            if row < 4:
+                corners[0][row] = packed
+            if row >= rows - 4:
+                corners[1][row - rows + 4] = packed
     start = 0
     for near, far, count in zip(nears, fars, (4, 4, 3, 1)):
         for r in range(count):
@@ -159,16 +166,18 @@
     )
 
 
-def corner(message, row):
-    return message[row], message[4 + row]
+def corner(strips, row):
+    return strips[0][row], strips[1][row]
 
 
 def rho_kernel(
     rows_total, cols_total, place,
-    density, material, from_above, from_below, corner_above, corner_below, left, right,
+    density, material, from_above, from_below,
+    above_left, above_right, below_left, below_right, left, right,
     rho_out, cond_first, cond_last,
     ext, middle, summed,
 ):
+    corner_above, corner_below = (above_left, above_right), (below_left, below_right)
     rows, height, own = density.shape
     has_above, has_below, has_left, has_right = present(place, rows, own, rows_total, cols_total)
 
@@ -249,12 +258,13 @@
 
 def prepare_kernel(
     cond_first, cond_last, prior, source, temp,
-    from_above, from_below, corner_above, corner_below, left, right,
+    from_above, from_below, above_left, above_right, below_left, below_right, left, right,
     field, load, heat, depth_face, height_face, lane_face,
     depth_here, depth_there, height_here, height_there, lane_here, lane_there,
     inverse, residual, direction, dual,
 ):
     rows, height, own = prior.shape
+    corner_above, corner_below = (above_left, above_right), (below_left, below_right)
     last_level = sub_iota((height, 1)) == height - 1
 
     def place_row(target, row, main, strips, index):
@@ -589,7 +599,8 @@
 def launch_messages(density, material, source, prior, temp):
     rows, height, own = density.shape
     end = own // LANES - 1
-    block, message = (rows, height, LANES), (12, height, own)
+    block, message, half = (rows, height, LANES), (12, height, own), (4, height, LANES)
+    outs = (block, block, message, message, half, half, half, half)
     first = pl.BlockSpec(block, lambda i: (0, 0, 0))
     last = pl.BlockSpec(block, lambda i: (0, 0, end))
 
@@ -601,10 +612,10 @@
     return pl.pallas_call(
         launch_kernel,
         grid=(1,),
-        out_shape=[jax.ShapeDtypeStruct(s, f32) for s in (block, block, message, message)],
+        out_shape=[jax.ShapeDtypeStruct(s, f32) for s in outs],
         in_specs=[first] * 5 + [last] * 5
         + [layers(4, 0)] * 3 + [layers(1, 0)] + [layers(4, rows // 4 - 1)] * 3 + [layers(1, rows - 1)],
-        out_specs=[pl.BlockSpec(s, lambda i: (0, 0, 0)) for s in (block, block, message, message)],
+        out_specs=[pl.BlockSpec(s, lambda i: (0, 0, 0)) for s in outs],
     )(*strips, *strips, *layered, *layered)
 
 
@@ -635,13 +646,24 @@
     to_right, to_left = turn("facade", long, 1), turn("facade", long, -1)
     to_deeper, to_nearer = turn("thick", deep, 1), turn("thick", deep, -1)
 
-    first_strips, last_strips, rows_up, rows_down = launch_messages(
+    def diagonal(deeper, righter):
+        pairs = [
+            (i * long + j, (i + deeper) % deep * long + (j + righter) % long)
+            for i in range(deep) for j in range(long)
+        ]
+        return lambda value: lax.ppermute(value, AXES, pairs)
+
+    (
+        first_strips, last_strips, rows_up, rows_down, first_near, first_far, last_near, last_far,
+    ) = launch_messages(
         solid_occupancy, cell_material, loss_state_derivative, prior_dual_state, thermal_state
     )
+    from_above, from_below = to_deeper(rows_up), to_nearer(rows_down)
     right, left = to_left(first_strips), to_right(last_strips)
-    from_above, from_below = to_deeper(rows_up), to_nearer(rows_down)
-    corner_above = to_deeper(jnp.concatenate([left[rows - 4:], right[rows - 4:]]))
-    corner_below = to_nearer(jnp.concatenate([left[:4], right[:4]]))
+    corners = (
+        diagonal(1, 1)(last_far), diagonal(1, -1)(first_far),
+        diagonal(-1, 1)(last_near), diagonal(-1, -1)(first_near),
+    )
 
     (below, above, up, low, least, most, upper, lower, bend, tallies) = call(
         lines_kernel,
@@ -657,8 +679,7 @@
         rho_kernel, place,
         [(rows, height, width), four, four],
         (
-            solid_occupancy, cell_material, from_above, from_below,
-            corner_above, corner_below, left, right,
+            solid_occupancy, cell_material, from_above, from_below, *corners, left, right,
         ),
         [(BOTH_SIDES, height, width), (BOTH_SIDES - 4, height, width), (rows, height, width)],
         totals,
@@ -672,7 +693,7 @@
         [tall, tall, (rows + 2, height, width)] + [own_wide] * 9 + [inner] * 4,
         (
             cond_first, cond_last, prior_dual_state, loss_state_derivative, thermal_state,
-            from_above, from_below, corner_above, corner_below, left, right,
+            from_above, from_below, *corners, left, right,
         ),
     )
     dual_state, weighted_first, weighted_last = placed_call(

time: 223 us -> 229 us (1.027)
  starting transfers between devices: 17.9 us -> 25.1 us
  blocking collectives: 176 us -> 171 us
  waiting for transfers between devices: 8.58 us -> 12.3 us
    ppermute x0 -> x4, starting transfers between devices: none -> 9.98 us  [diagonal(): return lambda value: lax.ppermute(value, AXES, pairs)]
    ppermute x0 -> x4, waiting for transfers between devices: none -> 9.02 us  [diagonal(): return lambda value: lax.ppermute(value, AXES, pairs)]
    ppermute x10 -> x8, waiting for transfers between devices: 8.58 us -> 3.28 us  [turn(): return lambda value: lax.ppermute(value, axis, pairs)]
    all_to_all x9, blocking collectives: 176 us -> 171 us  [everyone(): return lax.all_to_all(rows_out, AXES, 0, 0, tiled=True)]
    ppermute x10 -> x8, starting transfers between devices: 17.9 us -> 15.2 us  [turn(): return lambda value: lax.ppermute(value, axis, pairs)]
  transfers between devices with their start and end apart: 10 -> 12, of which waited for: 4 -> 5; matrix products, arithmetic and copies ran while one was open for 0% -> 0% of each run, Pallas kernels for 1% -> 1%
where the time goes in v6:
time: 229 us
  blocking collectives  171 us (75%)
  starting transfers between devices  25.1 us (11%)
  Pallas kernels  19.3 us (8%)
  waiting for transfers between devices  12.3 us (5%)
    all_to_all x9, blocking collectives, everyone(): return lax.all_to_all(rows_out, AXES, 0, 0, tiled=True)  171 us
    ppermute x8, starting transfers between devices, turn(): return lambda value: lax.ppermute(value, axis, pairs)  15.2 us
    ppermute x4, starting transfers between devices, diagonal(): return lambda value: lax.ppermute(value, AXES, pairs)  9.98 us
    ppermute x4, waiting for transfers between devices, diagonal(): return lambda value: lax.ppermute(value, AXES, pairs)  9.02 us
    pallas_call x3, Pallas kernels, placed_call(): pl.pallas_call(with_place(kernel, *totals), out_shape=[jax.ShapeDtypeStru...  8.88 us
    pallas_call x11, Pallas kernels, call(): pl.pallas_call(kernel, out_shape=[jax.ShapeDtypeStruct(shape, f32) for sh...  7.79 us
  transfers between devices with their start and end apart: 12, of which 5 were waited for; matrix products, arithmetic and copies ran while one was open for 0% of the time, Pallas kernels for 1%

profile of v6, /device:TPU:1, one launch (start us, length us, event | category | flops | bytes accessed | tf_op | source)
XLA Modules:
  0.0 228.8 jit_solution(15480114447778271379)
XLA Ops:
  0.6 0.0 copy-start
  0.6 0.0 copy-start.1
  0.7 2.6 %shard_map.120 = (f32[8,16,128]{2,1,0:T(8,128)}, f32[8,16,128]{2,1,0:T(8,128)}, f32[12,16,512]{2,1,0:T(8,128)}, f32[12,16,512]{2,1,0:T(8,128)}, f32[4,16,128]{2,...) custom-call(f32[8,16,512]{2,1,0:T(8,128)} %solid.3, s32[8,16,512]{2,1,0:T(8,128)} %material.3, ...), custom_call_target="tpu_custom_call" | custom-call | tf_op jit(solution)/shard_map/pallas_call | solution.py:612
  3.3 2.5 %collective-permute-start = (f32[12,16,512]{2,1,0:T(8,128)}, f32[12,16,512]{2,1,0:T(8,128)S(1)}, u32[]{:S(2)}, u32[]{:S(2)}) collective-permute-start(f32[12,16,512]{2,1,0:T(8,128)} %get-tuple-element.63), channel_id=1, source_target_pairs={{0,32},{32,64},{64,96},{96,128},{128,160},{160,192},{192,224},{224... | collective-permute-start | bytes 1179656 | tf_op jit(solution)/shard_map/ppermute | solution.py:644
  5.8 4.0 %collective-permute-start.1 = (f32[12,16,512]{2,1,0:T(8,128)}, f32[12,16,512]{2,1,0:T(8,128)S(1)}, u32[]{:S(2)}, u32[]{:S(2)}) collective-permute-start(f32[12,16,512]{2,1,0:T(8,128)} %get-tuple-element.64), channel_id=1, source_target_pairs={{0,224},{32,0},{64,32},{96,64},{128,96},{160,128},{192,160},{224,1... | collective-permute-start | bytes 1179656 | tf_op jit(solution)/shard_map/ppermute | solution.py:644
  9.9 0.0 collective-permute-start.2
  9.9 0.0 collective-permute-start.3
  9.9 3.9 %collective-permute-start.4 = (f32[4,16,128]{2,1,0:T(8,128)}, f32[4,16,128]{2,1,0:T(8,128)S(1)}, u32[]{:S(2)}, u32[]{:S(2)}) collective-permute-start(f32[4,16,128]{2,1,0:T(8,128)} %get-tuple-element.67), channel_id=1, source_target_pairs={{0,225},{1,226},{2,227},{3,228},{4,229},{5,230},{6,231},{7,232},{8... | collective-permute-start | bytes 98312 | tf_op jit(solution)/shard_map/ppermute | solution.py:654
  13.7 6.7 %collective-permute-done.2.refs_4_.above_left = f32[4,16,128]{2,1,0:T(8,128)S(1)} collective-permute-done((f32[4,16,128]{2,1,0:T(8,128)}, f32[4,16,128]{2,1,0:T(8,128)S(1)}, u32[]{:S(2)}, u32[]{:S(2)}) %collective-permute-start.2) | collective-permute-done | bytes 32800 | tf_op jit(solution)/shard_map/ppermute | solution.py:654
  20.4 0.6 collective-permute-start.6
  21.0 1.0 collective-permute-done.3.refs_5_.above_right
  22.0 2.6 %collective-permute-start.7 = (f32[8,16,128]{2,1,0:T(8,128)}, f32[8,16,128]{2,1,0:T(8,128)S(1)}, u32[]{:S(2)}, u32[]{:S(2)}) collective-permute-start(f32[8,16,128]{2,1,0:T(8,128)} %get-tuple-element.70), channel_id=1, source_target_pairs={{0,31},{1,0},{2,1},{3,2},{4,3},{5,4},{6,5},{7,6},{8,7},{9,8},{10,9... | collective-permute-start | bytes 196616 | tf_op jit(solution)/shard_map/ppermute | solution.py:644
  24.6 0.0 collective-permute-done.4.refs_6_.below_left
  24.6 6.1 %collective-permute-start.5 = (f32[4,16,128]{2,1,0:T(8,128)}, f32[4,16,128]{2,1,0:T(8,128)S(1)}, u32[]{:S(2)}, u32[]{:S(2)}) collective-permute-start(f32[4,16,128]{2,1,0:T(8,128)} %get-tuple-element.68), channel_id=1, source_target_pairs={{0,255},{1,224},{2,225},{3,226},{4,227},{5,228},{6,229},{7,230},{8... | collective-permute-start | bytes 98312 | tf_op jit(solution)/shard_map/ppermute | solution.py:654
  30.7 0.1 pad_add_fusion.place_ref
  30.7 0.0 copy-start.5
  30.7 0.0 copy-start.6
  30.8 1.3 collective-permute-done.5.refs_7_.below_right
  32.1 0.0 collective-permute-done.6.refs_8_.left.refs_22_
  32.1 0.0 collective-permute-done.7.refs_9_.right.refs_23_
  32.1 0.0 collective-permute-done.refs_2_.from_above
  32.1 0.0 collective-permute-done.1.refs_3_.from_below
  32.1 0.0 copy-done
  32.1 0.0 copy-done.1
  32.1 2.2 shard_map.121
  34.3 0.4 collective-permute-start.8
  34.7 2.4 %collective-permute-start.9 = (f32[4,16,640]{2,1,0:T(8,128)S(1)}, f32[4,16,640]{2,1,0:T(8,128)S(1)}, u32[]{:S(2)}, u32[]{:S(2)}) collective-permute-start(f32[4,16,640]{2,1,0:T(8,128)S(1)} %get-tuple-element.72.cond_first.refs_1_), channel_id=1, source_target_pairs={{0,224},{32,0},{64,32},{96,64},{128,96},{160,128},{192,160},{224,1... | collective-permute-start | bytes 491528 | tf_op jit(solution)/shard_map/ppermute | solution.py:644
  37.1 0.0 copy-done.5
  37.1 0.0 copy-done.6
  37.1 0.0 copy-done.7
  37.1 0.0 copy-done.8
  37.1 0.9 shard_map.123
  38.0 0.0 copy-done.2
  38.0 0.0 copy-done.3
  38.0 0.0 copy-done.4
  38.0 1.2 shard_map.122
  39.2 0.6 collective-permute-done.8.refs_0_
  39.8 0.0 collective-permute-done.9.refs_3_
  39.8 4.8 %shard_map.124 = (f32[8,16,512]{2,1,0:T(8,128)}, f32[4,16,640]{2,1,0:T(8,128)S(1)}, f32[4,16,640]{2,1,0:T(8,128)S(1)}) custom-call(s32[2]{0:T(128)S(1)} %pad_add_fusion.place_ref, f32[4,16,640]{2,1,0:T(8,128)S(1)} %collective-permute-done.8.refs_0_, f32[4,16,640]{2,1,0:T(8,128)S(1)} %get-tuple-element.72.cond_first.refs_1_, ...), custom_call_target="tpu_custom_call" | custom-call | tf_op jit(solution)/shard_map/pallas_call | solution.py:589
  44.6 0.3 collective-permute-start.10
  44.9 2.4 %collective-permute-start.11 = (f32[4,16,640]{2,1,0:T(8,128)S(1)}, f32[4,16,640]{2,1,0:T(8,128)S(1)}, u32[]{:S(2)}, u32[]{:S(2)}) collective-permute-start(f32[4,16,640]{2,1,0:T(8,128)S(1)} %get-tuple-element.92.refs_1_), channel_id=1, source_target_pairs={{0,224},{32,0},{64,32},{96,64},{128,96},{160,128},{192,160},{224,1... | collective-permute-start | bytes 491528 | tf_op jit(solution)/shard_map/ppermute | solution.py:644
  47.3 2.7 %collective-permute-done.10.refs_0_ = f32[4,16,640]{2,1,0:T(8,128)S(1)} collective-permute-done((f32[4,16,640]{2,1,0:T(8,128)S(1)}, f32[4,16,640]{2,1,0:T(8,128)S(1)}, u32[]{:S(2)}, u32[]{:S(2)}) %collective-permute-start.10) | collective-permute-done | bytes 163872 | tf_op jit(solution)/shard_map/ppermute | solution.py:644
  50.0 0.0 collective-permute-done.11.refs_3_
  50.0 1.9 shard_map.125
  51.9 24.0 %all_to_all.99 = f32[256,1,128]{2,1,0:T(1,128)S(1)} all-to-all(f32[256,1,128]{2,1,0:T(1,128)S(1)} %bitcast.48), channel_id=1, replica_groups=mesh['thick'=8,'facade'=32] {'thick','facade'}, dimensions={0} | all-to-all | bytes 262144 | tf_op jit(solution)/shard_map/all_to_all | solution.py:721
  75.9 0.6 shard_map.126
  76.5 18.4 %all_to_all.100 = f32[256,1,128]{2,1,0:T(1,128)S(1)} all-to-all(f32[256,1,128]{2,1,0:T(1,128)S(1)} %bitcast.49), channel_id=1, replica_groups=mesh['thick'=8,'facade'=32] {'thick','facade'}, dimensions={0} | all-to-all | bytes 262144 | tf_op jit(solution)/shard_map/all_to_all | solution.py:721
  94.9 0.6 shard_map.127
  95.5 18.4 %all_to_all.101 = f32[256,1,128]{2,1,0:T(1,128)S(1)} all-to-all(f32[256,1,128]{2,1,0:T(1,128)S(1)} %bitcast.50), channel_id=1, replica_groups=mesh['thick'=8,'facade'=32] {'thick','facade'}, dimensions={0} | all-to-all | bytes 262144 | tf_op jit(solution)/shard_map/all_to_all | solution.py:721
  113.8 0.6 shard_map.128
  114.4 18.6 %all_to_all.102 = f32[256,1,128]{2,1,0:T(1,128)S(1)} all-to-all(f32[256,1,128]{2,1,0:T(1,128)S(1)} %bitcast.51), channel_id=1, replica_groups=mesh['thick'=8,'facade'=32] {'thick','facade'}, dimensions={0} | all-to-all | bytes 262144 | tf_op jit(solution)/shard_map/all_to_all | solution.py:721
  133.0 0.6 shard_map.129
  133.6 18.4 %all_to_all.103 = f32[256,1,128]{2,1,0:T(1,128)S(1)} all-to-all(f32[256,1,128]{2,1,0:T(1,128)S(1)} %bitcast.52), channel_id=1, replica_groups=mesh['thick'=8,'facade'=32] {'thick','facade'}, dimensions={0} | all-to-all | bytes 262144 | tf_op jit(solution)/shard_map/all_to_all | solution.py:721
  151.9 0.6 shard_map.130
  152.5 18.4 %all_to_all.104 = f32[256,1,128]{2,1,0:T(1,128)S(1)} all-to-all(f32[256,1,128]{2,1,0:T(1,128)S(1)} %bitcast.53), channel_id=1, replica_groups=mesh['thick'=8,'facade'=32] {'thick','facade'}, dimensions={0} | all-to-all | bytes 262144 | tf_op jit(solution)/shard_map/all_to_all | solution.py:721
  170.8 0.6 shard_map.131
  171.4 18.4 %all_to_all.105 = f32[256,1,128]{2,1,0:T(1,128)S(1)} all-to-all(f32[256,1,128]{2,1,0:T(1,128)S(1)} %bitcast.54), channel_id=1, replica_groups=mesh['thick'=8,'facade'=32] {'thick','facade'}, dimensions={0} | all-to-all | bytes 262144 | tf_op jit(solution)/shard_map/all_to_all | solution.py:721
  189.8 0.6 shard_map.132
  190.4 18.4 %all_to_all.106 = f32[256,1,128]{2,1,0:T(1,128)S(1)} all-to-all(f32[256,1,128]{2,1,0:T(1,128)S(1)} %bitcast.55), channel_id=1, replica_groups=mesh['thick'=8,'facade'=32] {'thick','facade'}, dimensions={0} | all-to-all | bytes 262144 | tf_op jit(solution)/shard_map/all_to_all | solution.py:721
  208.7 0.6 shard_map.133
  209.3 0.0 copy-start.9
  209.3 18.5 %all_to_all.107 = f32[256,1,128]{2,1,0:T(1,128)S(1)} all-to-all(f32[256,1,128]{2,1,0:T(1,128)S(1)} %bitcast.47), channel_id=1, replica_groups=mesh['thick'=8,'facade'=32] {'thick','facade'}, dimensions={0} | all-to-all | bytes 262144 | tf_op jit(solution)/shard_map/all_to_all | solution.py:721
  227.8 0.0 copy-done.9
  227.8 1.0 shard_map.134
  (6 shorter events, 0.0 us)
Async XLA Ops:
  0.6 31.5 %copy-start = (s32[8,16,512]{2,1,0:T(8,128)S(1)}, s32[8,16,512]{2,1,0:T(8,128)}, u32[]{:S(2)}) copy-start(s32[8,16,512]{2,1,0:T(8,128)} %material.3) | copy-start | bytes 786436
  0.6 31.5 %copy-start.1 = (f32[8,16,512]{2,1,0:T(8,128)S(1)}, f32[8,16,512]{2,1,0:T(8,128)}, u32[]{:S(2)}) copy-start(f32[8,16,512]{2,1,0:T(8,128)} %solid.3) | copy-start | bytes 786436
  3.3 28.8 %collective-permute-start = (f32[12,16,512]{2,1,0:T(8,128)}, f32[12,16,512]{2,1,0:T(8,128)S(1)}, u32[]{:S(2)}, u32[]{:S(2)}) collective-permute-start(f32[12,16,512]{2,1,0:T(8,128)} %get-tuple-element.63), channel_id=1, source_target_pairs={{0,32},{32,64},{64,96},{96,128},{128,160},{160,192},{192,224},{224... | collective-permute-start | bytes 1179656 | tf_op jit(solution)/shard_map/ppermute | solution.py:644
  5.8 26.3 %collective-permute-start.1 = (f32[12,16,512]{2,1,0:T(8,128)}, f32[12,16,512]{2,1,0:T(8,128)S(1)}, u32[]{:S(2)}, u32[]{:S(2)}) collective-permute-start(f32[12,16,512]{2,1,0:T(8,128)} %get-tuple-element.64), channel_id=1, source_target_pairs={{0,224},{32,0},{64,32},{96,64},{128,96},{160,128},{192,160},{224,1... | collective-permute-start | bytes 1179656 | tf_op jit(solution)/shard_map/ppermute | solution.py:644
  9.9 10.6 %collective-permute-start.2 = (f32[4,16,128]{2,1,0:T(8,128)}, f32[4,16,128]{2,1,0:T(8,128)S(1)}, u32[]{:S(2)}, u32[]{:S(2)}) collective-permute-start(f32[4,16,128]{2,1,0:T(8,128)} %get-tuple-element.65), channel_id=1, source_target_pairs={{0,33},{1,34},{2,35},{3,36},{4,37},{5,38},{6,39},{7,40},{8,41},{9,... | collective-permute-start | bytes 98312 | tf_op jit(solution)/shard_map/ppermute | solution.py:654
  9.9 12.1 %collective-permute-start.3 = (f32[4,16,128]{2,1,0:T(8,128)}, f32[4,16,128]{2,1,0:T(8,128)S(1)}, u32[]{:S(2)}, u32[]{:S(2)}) collective-permute-start(f32[4,16,128]{2,1,0:T(8,128)} %get-tuple-element.66), channel_id=1, source_target_pairs={{0,63},{1,32},{2,33},{3,34},{4,35},{5,36},{6,37},{7,38},{8,39},{9,... | collective-permute-start | bytes 98312 | tf_op jit(solution)/shard_map/ppermute | solution.py:654
  9.9 14.7 %collective-permute-start.4 = (f32[4,16,128]{2,1,0:T(8,128)}, f32[4,16,128]{2,1,0:T(8,128)S(1)}, u32[]{:S(2)}, u32[]{:S(2)}) collective-permute-start(f32[4,16,128]{2,1,0:T(8,128)} %get-tuple-element.67), channel_id=1, source_target_pairs={{0,225},{1,226},{2,227},{3,228},{4,229},{5,230},{6,231},{7,232},{8... | collective-permute-start | bytes 98312 | tf_op jit(solution)/shard_map/ppermute | solution.py:654
  20.4 11.7 %collective-permute-start.6 = (f32[8,16,128]{2,1,0:T(8,128)}, f32[8,16,128]{2,1,0:T(8,128)S(1)}, u32[]{:S(2)}, u32[]{:S(2)}) collective-permute-start(f32[8,16,128]{2,1,0:T(8,128)} %get-tuple-element.69), channel_id=1, source_target_pairs={{0,1},{1,2},{2,3},{3,4},{4,5},{5,6},{6,7},{7,8},{8,9},{9,10},{10,1... | collective-permute-start | bytes 196616 | tf_op jit(solution)/shard_map/ppermute | solution.py:644
  22.0 10.1 %collective-permute-start.7 = (f32[8,16,128]{2,1,0:T(8,128)}, f32[8,16,128]{2,1,0:T(8,128)S(1)}, u32[]{:S(2)}, u32[]{:S(2)}) collective-permute-start(f32[8,16,128]{2,1,0:T(8,128)} %get-tuple-element.70), channel_id=1, source_target_pairs={{0,31},{1,0},{2,1},{3,2},{4,3},{5,4},{6,5},{7,6},{8,7},{9,8},{10,9... | collective-permute-start | bytes 196616 | tf_op jit(solution)/shard_map/ppermute | solution.py:644
  24.6 7.5 %collective-permute-start.5 = (f32[4,16,128]{2,1,0:T(8,128)}, f32[4,16,128]{2,1,0:T(8,128)S(1)}, u32[]{:S(2)}, u32[]{:S(2)}) collective-permute-start(f32[4,16,128]{2,1,0:T(8,128)} %get-tuple-element.68), channel_id=1, source_target_pairs={{0,255},{1,224},{2,225},{3,226},{4,227},{5,228},{6,229},{7,230},{8... | collective-permute-start | bytes 98312 | tf_op jit(solution)/shard_map/ppermute | solution.py:654
  30.7 6.4 %copy-start.5 = (f32[8,16,512]{2,1,0:T(8,128)S(1)}, f32[8,16,512]{2,1,0:T(8,128)}, u32[]{:S(2)}) copy-start(f32[8,16,512]{2,1,0:T(8,128)} %newer.1) | copy-start | bytes 786436
  30.7 6.4 %copy-start.6 = (f32[8,16,512]{2,1,0:T(8,128)S(1)}, f32[8,16,512]{2,1,0:T(8,128)}, u32[]{:S(2)}) copy-start(f32[8,16,512]{2,1,0:T(8,128)} %older.1) | copy-start | bytes 786436
  30.7 6.4 %copy-start.7 = (f32[8,16,512]{2,1,0:T(8,128)S(1)}, f32[8,16,512]{2,1,0:T(8,128)}, u32[]{:S(2)}) copy-start(f32[8,16,512]{2,1,0:T(8,128)} %below_spacing.1) | copy-start | bytes 786436
  30.7 6.4 %copy-start.8 = (f32[8,16,512]{2,1,0:T(8,128)S(1)}, f32[8,16,512]{2,1,0:T(8,128)}, u32[]{:S(2)}) copy-start(f32[8,16,512]{2,1,0:T(8,128)} %above_spacing.1) | copy-start | bytes 786436
  34.3 5.5 %collective-permute-start.8 = (f32[4,16,640]{2,1,0:T(8,128)S(1)}, f32[4,16,640]{2,1,0:T(8,128)S(1)}, u32[]{:S(2)}, u32[]{:S(2)}) collective-permute-start(f32[4,16,640]{2,1,0:T(8,128)S(1)} %get-tuple-element.71.cond_last.refs_2_), channel_id=1, source_target_pairs={{0,32},{32,64},{64,96},{96,128},{128,160},{160,192},{192,224},{224... | collective-permute-start | bytes 491528 | tf_op jit(solution)/shard_map/ppermute | solution.py:644
  34.7 3.3 %copy-start.2 = (f32[8,16,512]{2,1,0:T(8,128)S(1)}, f32[8,16,512]{2,1,0:T(8,128)}, u32[]{:S(2)}) copy-start(f32[8,16,512]{2,1,0:T(8,128)} %source.1) | copy-start | bytes 786436
  34.7 3.3 %copy-start.3 = (f32[8,16,512]{2,1,0:T(8,128)S(1)}, f32[8,16,512]{2,1,0:T(8,128)}, u32[]{:S(2)}) copy-start(f32[8,16,512]{2,1,0:T(8,128)} %prior.1) | copy-start | bytes 786436
  34.7 3.3 %copy-start.4 = (f32[8,16,512]{2,1,0:T(8,128)S(1)}, f32[8,16,512]{2,1,0:T(8,128)}, u32[]{:S(2)}) copy-start(f32[8,16,512]{2,1,0:T(8,128)} %temp.1) | copy-start | bytes 786436
  34.7 5.1 %collective-permute-start.9 = (f32[4,16,640]{2,1,0:T(8,128)S(1)}, f32[4,16,640]{2,1,0:T(8,128)S(1)}, u32[]{:S(2)}, u32[]{:S(2)}) collective-permute-start(f32[4,16,640]{2,1,0:T(8,128)S(1)} %get-tuple-element.72.cond_first.refs_1_), channel_id=1, source_target_pairs={{0,224},{32,0},{64,32},{96,64},{128,96},{160,128},{192,160},{224,1... | collective-permute-start | bytes 491528 | tf_op jit(solution)/shard_map/ppermute | solution.py:644
  44.6 5.4 %collective-permute-start.10 = (f32[4,16,640]{2,1,0:T(8,128)S(1)}, f32[4,16,640]{2,1,0:T(8,128)S(1)}, u32[]{:S(2)}, u32[]{:S(2)}) collective-permute-start(f32[4,16,640]{2,1,0:T(8,128)S(1)} %get-tuple-element.91.refs_2_), channel_id=1, source_target_pairs={{0,32},{32,64},{64,96},{96,128},{128,160},{160,192},{192,224},{224... | collective-permute-start | bytes 491528 | tf_op jit(solution)/shard_map/ppermute | solution.py:644
  44.9 5.1 %collective-permute-start.11 = (f32[4,16,640]{2,1,0:T(8,128)S(1)}, f32[4,16,640]{2,1,0:T(8,128)S(1)}, u32[]{:S(2)}, u32[]{:S(2)}) collective-permute-start(f32[4,16,640]{2,1,0:T(8,128)S(1)} %get-tuple-element.92.refs_1_), channel_id=1, source_target_pairs={{0,224},{32,0},{64,32},{96,64},{128,96},{160,128},{192,160},{224,1... | collective-permute-start | bytes 491528 | tf_op jit(solution)/shard_map/ppermute | solution.py:644
  209.3 18.5 %copy-start.9 = (f32[8,16,512]{2,1,0:T(8,128)S(1)}, f32[8,16,512]{2,1,0:T(8,128)}, u32[]{:S(2)}) copy-start(f32[8,16,512]{2,1,0:T(8,128)} %get-tuple-element.60.below) | copy-start | bytes 786436

commit v7 on v5

--- a/solution.py
+++ b/solution.py
@@ -61,8 +61,8 @@
 
 
 def launch_kernel(*refs):
-    firsts, lasts, nears, fars = refs[0:5], refs[5:10], refs[10:14], refs[14:18]
-    to_left, to_right, rows_up, rows_down = refs[18:]
+    firsts, lasts, nears, fars = refs[0:5], refs[5:10], refs[10:13], refs[13:16]
+    to_left, to_right, rows_up, rows_down = refs[16:]
     rows, height, _ = to_left.shape
     group = lane_iota((height, LANES)) // STRIP
     for row in range(rows):
@@ -78,7 +78,7 @@
                 packed = jnp.where(group == index, value, packed)
             target[row] = packed
     start = 0
-    for near, far, count in zip(nears, fars, (4, 4, 3, 1)):
+    for near, far, count in zip(nears, fars, (4, 3, 1)):
         for r in range(count):
             rows_down[start + r] = near[r]
             rows_up[start + r] = far[far.shape[0] - count + r]
@@ -160,12 +160,13 @@
 
 
 def corner(message, row):
-    return message[row], message[4 + row]
+    lanes = slice(row * LANES, (row + 1) * LANES)
+    return message[4, :, lanes], message[5, :, lanes]
 
 
 def rho_kernel(
     rows_total, cols_total, place,
-    density, material, from_above, from_below, corner_above, corner_below, left, right,
+    density, material, density_above, density_below, left, right,
     rho_out, cond_first, cond_last,
     ext, middle, summed,
 ):
@@ -176,10 +177,10 @@
         return halo_lanes(strips[0] * has_left, strips[1] * has_right, index)
 
     for r in range(4):
-        ext[r, :, :own] = from_above[r] * has_above
-        ext[r, :, own:] = halo(corner(corner_above, r), 0) * has_above
-        ext[rows + 4 + r, :, :own] = from_below[r] * has_below
-        ext[rows + 4 + r, :, own:] = halo(corner(corner_below, r), 0) * has_below
+        ext[r, :, :own] = density_above[r] * has_above
+        ext[r, :, own:] = halo(corner(density_above, r), 0) * has_above
+        ext[rows + 4 + r, :, :own] = density_below[r] * has_below
+        ext[rows + 4 + r, :, own:] = halo(corner(density_below, r), 0) * has_below
     for r in range(rows):
         ext[4 + r, :, :own] = density[r]
         ext[4 + r, :, own:] = halo((left[r], right[r]), 0)
@@ -249,7 +250,7 @@
 
 def prepare_kernel(
     cond_first, cond_last, prior, source, temp,
-    from_above, from_below, corner_above, corner_below, left, right,
+    from_above, from_below, density_above, density_below, left, right,
     field, load, heat, depth_face, height_face, lane_face,
     depth_here, depth_there, height_here, height_there, lane_here, lane_there,
     inverse, residual, direction, dual,
@@ -262,15 +263,15 @@
         target[row, :, own:] = halo_lanes(strips[0], strips[1], index)
 
     for r in range(4):
-        place_row(field, r, from_above[4 + r], corner(corner_above, r), 3)
-        place_row(field, 12 + r, from_below[4 + r], corner(corner_below, r), 3)
+        place_row(field, r, from_above[r], corner(density_above, r), 3)
+        place_row(field, 12 + r, from_below[r], corner(density_below, r), 3)
     for r in range(3):
-        place_row(load, 1 + r, from_above[8 + r], corner(corner_above, 1 + r), 2)
-        place_row(load, 12 + r, from_below[8 + r], corner(corner_below, r), 2)
+        place_row(load, 1 + r, from_above[4 + r], corner(density_above, 1 + r), 2)
+        place_row(load, 12 + r, from_below[4 + r], corner(density_below, r), 2)
     load[0] = jnp.zeros(load.shape[1:], f32)
     load[15] = jnp.zeros(load.shape[1:], f32)
-    place_row(heat, 0, from_above[11], corner(corner_above, 3), 4)
-    place_row(heat, 9, from_below[11], corner(corner_below, 0), 4)
+    place_row(heat, 0, from_above[7], corner(density_above, 3), 4)
+    place_row(heat, 9, from_below[7], corner(density_below, 0), 4)
     for r in range(rows):
         strips = (left[r], right[r])
         place_row(field, 4 + r, prior[r], strips, 3)
@@ -589,7 +590,7 @@
 def launch_messages(density, material, source, prior, temp):
     rows, height, own = density.shape
     end = own // LANES - 1
-    block, message = (rows, height, LANES), (12, height, own)
+    block, message = (rows, height, LANES), (8, height, own)
     first = pl.BlockSpec(block, lambda i: (0, 0, 0))
     last = pl.BlockSpec(block, lambda i: (0, 0, end))
 
@@ -597,13 +598,13 @@
         return pl.BlockSpec((count, height, own), lambda i: (index, 0, 0))
 
     strips = (density, material, source, prior, temp)
-    layered = (density, prior, source, temp)
+    layered = (prior, source, temp)
     return pl.pallas_call(
         launch_kernel,
         grid=(1,),
         out_shape=[jax.ShapeDtypeStruct(s, f32) for s in (block, block, message, message)],
         in_specs=[first] * 5 + [last] * 5
-        + [layers(4, 0)] * 3 + [layers(1, 0)] + [layers(4, rows // 4 - 1)] * 3 + [layers(1, rows - 1)],
+        + [layers(4, 0)] * 2 + [layers(1, 0)] + [layers(4, rows // 4 - 1)] * 2 + [layers(1, rows - 1)],
         out_specs=[pl.BlockSpec(s, lambda i: (0, 0, 0)) for s in (block, block, message, message)],
     )(*strips, *strips, *layered, *layered)
 
@@ -639,9 +640,23 @@
         solid_occupancy, cell_material, loss_state_derivative, prior_dual_state, thermal_state
     )
     right, left = to_left(first_strips), to_right(last_strips)
+
+    def side_by_side(strips, start):
+        return jnp.concatenate([strips[start + r] for r in range(4)], axis=1)[None]
+
+    def density_message(start):
+        return jnp.concatenate(
+            [
+                solid_occupancy[start:start + 4],
+                side_by_side(left, start), side_by_side(right, start),
+            ]
+        )
+
+    density_up, density_down, rows_up, rows_down = lax.optimization_barrier(
+        (density_message(rows - 4), density_message(0), rows_up, rows_down)
+    )
+    density_above, density_below = to_deeper(density_up), to_nearer(density_down)
     from_above, from_below = to_deeper(rows_up), to_nearer(rows_down)
-    corner_above = to_deeper(jnp.concatenate([left[rows - 4:], right[rows - 4:]]))
-    corner_below = to_nearer(jnp.concatenate([left[:4], right[:4]]))
 
     (below, above, up, low, least, most, upper, lower, bend, tallies) = call(
         lines_kernel,
@@ -657,8 +672,7 @@
         rho_kernel, place,
         [(rows, height, width), four, four],
         (
-            solid_occupancy, cell_material, from_above, from_below,
-            corner_above, corner_below, left, right,
+            solid_occupancy, cell_material, density_above, density_below, left, right,
         ),
         [(BOTH_SIDES, height, width), (BOTH_SIDES - 4, height, width), (rows, height, width)],
         totals,
@@ -672,7 +686,7 @@
         [tall, tall, (rows + 2, height, width)] + [own_wide] * 9 + [inner] * 4,
         (
             cond_first, cond_last, prior_dual_state, loss_state_derivative, thermal_state,
-            from_above, from_below, corner_above, corner_below, left, right,
+            from_above, from_below, density_above, density_below, left, right,
         ),
     )
     dual_state, weighted_first, weighted_last = placed_call(

time: 223 us -> 222 us (level)
  transfers between devices with their start and end apart: 10 -> 10, of which waited for: 4 -> 6; matrix products, arithmetic and copies ran while one was open for 0% -> 0% of each run, Pallas kernels for 1% -> 2%
where the time goes in v7:
time: 222 us; the launch traced here: 221 us
  blocking collectives  175 us (79%)
  Pallas kernels  19 us (9%)
  starting transfers between devices  18.1 us (8%)
  waiting for transfers between devices  8.42 us (4%)
    all_to_all x9, blocking collectives, everyone(): return lax.all_to_all(rows_out, AXES, 0, 0, tiled=True)  175 us
    ppermute x10, starting transfers between devices, turn(): return lambda value: lax.ppermute(value, axis, pairs)  18.1 us
    pallas_call x3, Pallas kernels, placed_call(): pl.pallas_call(with_place(kernel, *totals), out_shape=[jax.ShapeDtypeStru...  8.76 us
    ppermute x10, waiting for transfers between devices, turn(): return lambda value: lax.ppermute(value, axis, pairs)  8.42 us
    pallas_call x11, Pallas kernels, call(): pl.pallas_call(kernel, out_shape=[jax.ShapeDtypeStruct(shape, f32) for sh...  7.78 us
  transfers between devices with their start and end apart: 10, of which 6 were waited for; matrix products, arithmetic and copies ran while one was open for 0% of the time, Pallas kernels for 2%

profile of v7, /device:TPU:1, one launch (start us, length us, event | category | flops | bytes accessed | tf_op | source)
XLA Modules:
  0.0 221.4 jit_solution(14750199310145779952)
XLA Ops:
  0.6 0.0 copy-start.1
  0.6 2.4 %shard_map.120 = (f32[8,16,128]{2,1,0:T(8,128)}, f32[8,16,128]{2,1,0:T(8,128)}, f32[8,16,512]{2,1,0:T(8,128)}, f32[8,16,512]{2,1,0:T(8,128)}) custom-call(f32[8,16,512]{2,1,0:T(8,128)} %solid.3, s32[8,16,512]{2,1,0:T(8,128)} %material.3, f32[8,16,512]{2,1,0:T(8,128)} %source.1, f32[8,16,512]{2,1,0:T(8,128)} %prior.1, f32[8,16,512]{2,1,0:T(8,128)} %temp.1, ...), custom_call_target="tpu_custom_call" | custom-call | tf_op jit(solution)/shard_map/pallas_call | solution.py:602
  3.1 2.7 %collective-permute-start = (f32[8,16,128]{2,1,0:T(8,128)}, f32[8,16,128]{2,1,0:T(8,128)S(1)}, u32[]{:S(2)}, u32[]{:S(2)}) collective-permute-start(f32[8,16,128]{2,1,0:T(8,128)} %get-tuple-element.63), channel_id=1, source_target_pairs={{0,1},{1,2},{2,3},{3,4},{4,5},{5,6},{6,7},{7,8},{8,9},{9,10},{10,1... | collective-permute-start | bytes 196616 | tf_op jit(solution)/shard_map/ppermute | solution.py:634
  5.7 0.7 collective-permute-start.1
  6.5 0.0 copy-done.1
  6.5 0.9 collective-permute-done.refs_4_.left.refs_22_
  7.4 2.2 %collective-permute-done.1.refs_5_.right.refs_23_ = f32[8,16,128]{2,1,0:T(8,128)S(1)} collective-permute-done((f32[8,16,128]{2,1,0:T(8,128)}, f32[8,16,128]{2,1,0:T(8,128)S(1)}, u32[]{:S(2)}, u32[]{:S(2)}) %collective-permute-start.1) | collective-permute-done | bytes 65568 | tf_op jit(solution)/shard_map/ppermute | solution.py:634
  9.6 0.0 copy-start.11
  9.7 0.0 copy-start.10
  9.7 0.0 copy-start
  9.7 2.0 collective-permute-start.2
  11.7 4.0 %collective-permute-start.3 = (f32[6,16,512]{2,1,0:T(8,128)S(1)}, f32[6,16,512]{2,1,0:T(8,128)S(1)}, u32[]{:S(2)}, u32[]{:S(2)}) collective-permute-start(f32[6,16,512]{2,1,0:T(8,128)S(1)} %pad_maximum_fusion.1), channel_id=1, source_target_pairs={{0,224},{32,0},{64,32},{96,64},{128,96},{160,128},{192,160},{224,1... | collective-permute-start | bytes 589832 | tf_op jit(solution)/shard_map/ppermute | solution.py:634
  15.8 0.0 copy-done.11
  15.8 0.0 collective-permute-start.6
  15.8 0.0 copy-done.10
  15.8 2.7 %collective-permute-start.7 = (f32[8,16,512]{2,1,0:T(8,128)S(1)}, f32[8,16,512]{2,1,0:T(8,128)S(1)}, u32[]{:S(2)}, u32[]{:S(2)}) collective-permute-start(f32[8,16,512]{2,1,0:T(8,128)S(1)} %copy-done.10), channel_id=1, source_target_pairs={{0,224},{32,0},{64,32},{96,64},{128,96},{160,128},{192,160},{224,1... | collective-permute-start | bytes 786440 | tf_op jit(solution)/shard_map/ppermute | solution.py:634
  18.4 0.1 pad_add_fusion.place_ref
  18.5 0.2 collective-permute-done.2.refs_2_.density_above
  18.7 0.0 collective-permute-done.3.refs_3_.density_below
  18.7 0.0 copy-done
  18.7 2.2 shard_map.121
  20.9 0.1 collective-permute-start.4
  21.0 0.0 copy-start.2
  21.0 0.0 copy-start.3
  21.0 0.0 copy-start.4
  21.1 2.8 %collective-permute-start.5 = (f32[4,16,640]{2,1,0:T(8,128)S(1)}, f32[4,16,640]{2,1,0:T(8,128)S(1)}, u32[]{:S(2)}, u32[]{:S(2)}) collective-permute-start(f32[4,16,640]{2,1,0:T(8,128)S(1)} %get-tuple-element.70.cond_first.refs_1_), channel_id=1, source_target_pairs={{0,224},{32,0},{64,32},{96,64},{128,96},{160,128},{192,160},{224,1... | collective-permute-start | bytes 491528 | tf_op jit(solution)/shard_map/ppermute | solution.py:634
  23.9 0.0 copy-done.5
  23.9 0.0 copy-done.6
  23.9 0.0 copy-done.7
  23.9 0.0 copy-done.8
  23.9 0.9 shard_map.123
  24.8 0.4 collective-permute-done.6.from_above
  25.2 0.0 collective-permute-done.7.from_below
  25.2 0.0 copy-done.2
  25.2 0.0 copy-done.3
  25.3 1.2 shard_map.122
  26.4 1.9 collective-permute-done.4.refs_0_
  28.4 0.0 collective-permute-done.5.refs_3_
  28.4 4.7 %shard_map.124 = (f32[8,16,512]{2,1,0:T(8,128)}, f32[4,16,640]{2,1,0:T(8,128)S(1)}, f32[4,16,640]{2,1,0:T(8,128)S(1)}) custom-call(s32[2]{0:T(128)S(1)} %pad_add_fusion.place_ref, f32[4,16,640]{2,1,0:T(8,128)S(1)} %collective-permute-done.4.refs_0_, f32[4,16,640]{2,1,0:T(8,128)S(1)} %get-tuple-element.70.cond_first.refs_1_, ...), custom_call_target="tpu_custom_call" | custom-call | tf_op jit(solution)/shard_map/pallas_call | solution.py:580
  33.1 0.5 collective-permute-start.8
  33.6 2.6 %collective-permute-start.9 = (f32[4,16,640]{2,1,0:T(8,128)S(1)}, f32[4,16,640]{2,1,0:T(8,128)S(1)}, u32[]{:S(2)}, u32[]{:S(2)}) collective-permute-start(f32[4,16,640]{2,1,0:T(8,128)S(1)} %get-tuple-element.92.refs_1_), channel_id=1, source_target_pairs={{0,224},{32,0},{64,32},{96,64},{128,96},{160,128},{192,160},{224,1... | collective-permute-start | bytes 491528 | tf_op jit(solution)/shard_map/ppermute | solution.py:634
  36.2 2.7 %collective-permute-done.8.refs_0_ = f32[4,16,640]{2,1,0:T(8,128)S(1)} collective-permute-done((f32[4,16,640]{2,1,0:T(8,128)S(1)}, f32[4,16,640]{2,1,0:T(8,128)S(1)}, u32[]{:S(2)}, u32[]{:S(2)}) %collective-permute-start.8) | collective-permute-done | bytes 163872 | tf_op jit(solution)/shard_map/ppermute | solution.py:634
  38.9 0.0 collective-permute-done.9.refs_3_
  38.9 1.9 shard_map.125
  40.8 27.7 %all_to_all.99 = f32[256,1,128]{2,1,0:T(1,128)S(1)} all-to-all(f32[256,1,128]{2,1,0:T(1,128)S(1)} %bitcast.88), channel_id=1, replica_groups=mesh['thick'=8,'facade'=32] {'thick','facade'}, dimensions={0} | all-to-all | bytes 262144 | tf_op jit(solution)/shard_map/all_to_all | solution.py:714
  68.5 0.6 shard_map.126
  69.1 18.4 %all_to_all.100 = f32[256,1,128]{2,1,0:T(1,128)S(1)} all-to-all(f32[256,1,128]{2,1,0:T(1,128)S(1)} %bitcast.89), channel_id=1, replica_groups=mesh['thick'=8,'facade'=32] {'thick','facade'}, dimensions={0} | all-to-all | bytes 262144 | tf_op jit(solution)/shard_map/all_to_all | solution.py:714
  87.5 0.6 shard_map.127
  88.0 18.4 %all_to_all.101 = f32[256,1,128]{2,1,0:T(1,128)S(1)} all-to-all(f32[256,1,128]{2,1,0:T(1,128)S(1)} %bitcast.90), channel_id=1, replica_groups=mesh['thick'=8,'facade'=32] {'thick','facade'}, dimensions={0} | all-to-all | bytes 262144 | tf_op jit(solution)/shard_map/all_to_all | solution.py:714
  106.4 0.6 shard_map.128
  107.0 18.4 %all_to_all.102 = f32[256,1,128]{2,1,0:T(1,128)S(1)} all-to-all(f32[256,1,128]{2,1,0:T(1,128)S(1)} %bitcast.91), channel_id=1, replica_groups=mesh['thick'=8,'facade'=32] {'thick','facade'}, dimensions={0} | all-to-all | bytes 262144 | tf_op jit(solution)/shard_map/all_to_all | solution.py:714
  125.3 0.6 shard_map.129
  125.9 18.4 %all_to_all.103 = f32[256,1,128]{2,1,0:T(1,128)S(1)} all-to-all(f32[256,1,128]{2,1,0:T(1,128)S(1)} %bitcast.92), channel_id=1, replica_groups=mesh['thick'=8,'facade'=32] {'thick','facade'}, dimensions={0} | all-to-all | bytes 262144 | tf_op jit(solution)/shard_map/all_to_all | solution.py:714
  144.3 0.6 shard_map.130
  144.9 18.6 %all_to_all.104 = f32[256,1,128]{2,1,0:T(1,128)S(1)} all-to-all(f32[256,1,128]{2,1,0:T(1,128)S(1)} %bitcast.93), channel_id=1, replica_groups=mesh['thick'=8,'facade'=32] {'thick','facade'}, dimensions={0} | all-to-all | bytes 262144 | tf_op jit(solution)/shard_map/all_to_all | solution.py:714
  163.4 0.6 shard_map.131
  164.0 18.4 %all_to_all.105 = f32[256,1,128]{2,1,0:T(1,128)S(1)} all-to-all(f32[256,1,128]{2,1,0:T(1,128)S(1)} %bitcast.94), channel_id=1, replica_groups=mesh['thick'=8,'facade'=32] {'thick','facade'}, dimensions={0} | all-to-all | bytes 262144 | tf_op jit(solution)/shard_map/all_to_all | solution.py:714
  182.4 0.6 shard_map.132
  182.9 18.4 %all_to_all.106 = f32[256,1,128]{2,1,0:T(1,128)S(1)} all-to-all(f32[256,1,128]{2,1,0:T(1,128)S(1)} %bitcast.95), channel_id=1, replica_groups=mesh['thick'=8,'facade'=32] {'thick','facade'}, dimensions={0} | all-to-all | bytes 262144 | tf_op jit(solution)/shard_map/all_to_all | solution.py:714
  201.3 0.6 shard_map.133
  201.9 0.0 copy-start.9
  201.9 18.5 %all_to_all.107 = f32[256,1,128]{2,1,0:T(1,128)S(1)} all-to-all(f32[256,1,128]{2,1,0:T(1,128)S(1)} %bitcast.87), channel_id=1, replica_groups=mesh['thick'=8,'facade'=32] {'thick','facade'}, dimensions={0} | all-to-all | bytes 262144 | tf_op jit(solution)/shard_map/all_to_all | solution.py:714
  220.4 0.0 copy-done.9
  220.4 1.0 shard_map.134
  (13 shorter events, 0.1 us)
Async XLA Ops:
  0.6 5.8 %copy-start.1 = (f32[8,16,512]{2,1,0:T(8,128)S(1)}, f32[8,16,512]{2,1,0:T(8,128)}, u32[]{:S(2)}) copy-start(f32[8,16,512]{2,1,0:T(8,128)} %solid.3) | copy-start | bytes 786436
  3.1 4.3 %collective-permute-start = (f32[8,16,128]{2,1,0:T(8,128)}, f32[8,16,128]{2,1,0:T(8,128)S(1)}, u32[]{:S(2)}, u32[]{:S(2)}) collective-permute-start(f32[8,16,128]{2,1,0:T(8,128)} %get-tuple-element.63), channel_id=1, source_target_pairs={{0,1},{1,2},{2,3},{3,4},{4,5},{5,6},{6,7},{7,8},{8,9},{9,10},{10,1... | collective-permute-start | bytes 196616 | tf_op jit(solution)/shard_map/ppermute | solution.py:634
  5.7 3.9 %collective-permute-start.1 = (f32[8,16,128]{2,1,0:T(8,128)}, f32[8,16,128]{2,1,0:T(8,128)S(1)}, u32[]{:S(2)}, u32[]{:S(2)}) collective-permute-start(f32[8,16,128]{2,1,0:T(8,128)} %get-tuple-element.64), channel_id=1, source_target_pairs={{0,31},{1,0},{2,1},{3,2},{4,3},{5,4},{6,5},{7,6},{8,7},{9,8},{10,9... | collective-permute-start | bytes 196616 | tf_op jit(solution)/shard_map/ppermute | solution.py:634
  9.6 6.1 %copy-start.11 = (f32[8,16,512]{2,1,0:T(8,128)S(1)}, f32[8,16,512]{2,1,0:T(8,128)}, u32[]{:S(2)}) copy-start(f32[8,16,512]{2,1,0:T(8,128)} %get-tuple-element.72) | copy-start | bytes 786436
  9.7 6.1 %copy-start.10 = (f32[8,16,512]{2,1,0:T(8,128)S(1)}, f32[8,16,512]{2,1,0:T(8,128)}, u32[]{:S(2)}) copy-start(f32[8,16,512]{2,1,0:T(8,128)} %get-tuple-element.73) | copy-start | bytes 786436
  9.7 9.0 %copy-start = (s32[8,16,512]{2,1,0:T(8,128)S(1)}, s32[8,16,512]{2,1,0:T(8,128)}, u32[]{:S(2)}) copy-start(s32[8,16,512]{2,1,0:T(8,128)} %material.3) | copy-start | bytes 786436
  9.7 9.0 %collective-permute-start.2 = (f32[6,16,512]{2,1,0:T(8,128)S(1)}, f32[6,16,512]{2,1,0:T(8,128)S(1)}, u32[]{:S(2)}, u32[]{:S(2)}) collective-permute-start(f32[6,16,512]{2,1,0:T(8,128)S(1)} %pad_maximum_fusion), channel_id=1, source_target_pairs={{0,32},{32,64},{64,96},{96,128},{128,160},{160,192},{192,224},{224... | collective-permute-start | bytes 589832 | tf_op jit(solution)/shard_map/ppermute | solution.py:634
  11.7 7.0 %collective-permute-start.3 = (f32[6,16,512]{2,1,0:T(8,128)S(1)}, f32[6,16,512]{2,1,0:T(8,128)S(1)}, u32[]{:S(2)}, u32[]{:S(2)}) collective-permute-start(f32[6,16,512]{2,1,0:T(8,128)S(1)} %pad_maximum_fusion.1), channel_id=1, source_target_pairs={{0,224},{32,0},{64,32},{96,64},{128,96},{160,128},{192,160},{224,1... | collective-permute-start | bytes 589832 | tf_op jit(solution)/shard_map/ppermute | solution.py:634
  15.8 9.5 %collective-permute-start.6 = (f32[8,16,512]{2,1,0:T(8,128)S(1)}, f32[8,16,512]{2,1,0:T(8,128)S(1)}, u32[]{:S(2)}, u32[]{:S(2)}) collective-permute-start(f32[8,16,512]{2,1,0:T(8,128)S(1)} %copy-done.11), channel_id=1, source_target_pairs={{0,32},{32,64},{64,96},{96,128},{128,160},{160,192},{192,224},{224... | collective-permute-start | bytes 786440 | tf_op jit(solution)/shard_map/ppermute | solution.py:634
  15.8 9.5 %collective-permute-start.7 = (f32[8,16,512]{2,1,0:T(8,128)S(1)}, f32[8,16,512]{2,1,0:T(8,128)S(1)}, u32[]{:S(2)}, u32[]{:S(2)}) collective-permute-start(f32[8,16,512]{2,1,0:T(8,128)S(1)} %copy-done.10), channel_id=1, source_target_pairs={{0,224},{32,0},{64,32},{96,64},{128,96},{160,128},{192,160},{224,1... | collective-permute-start | bytes 786440 | tf_op jit(solution)/shard_map/ppermute | solution.py:634
  18.5 5.4 %copy-start.5 = (f32[8,16,512]{2,1,0:T(8,128)S(1)}, f32[8,16,512]{2,1,0:T(8,128)}, u32[]{:S(2)}) copy-start(f32[8,16,512]{2,1,0:T(8,128)} %newer.1) | copy-start | bytes 786436
  18.5 5.4 %copy-start.6 = (f32[8,16,512]{2,1,0:T(8,128)S(1)}, f32[8,16,512]{2,1,0:T(8,128)}, u32[]{:S(2)}) copy-start(f32[8,16,512]{2,1,0:T(8,128)} %older.1) | copy-start | bytes 786436
  18.5 5.4 %copy-start.7 = (f32[8,16,512]{2,1,0:T(8,128)S(1)}, f32[8,16,512]{2,1,0:T(8,128)}, u32[]{:S(2)}) copy-start(f32[8,16,512]{2,1,0:T(8,128)} %below_spacing.1) | copy-start | bytes 786436
  18.5 5.4 %copy-start.8 = (f32[8,16,512]{2,1,0:T(8,128)S(1)}, f32[8,16,512]{2,1,0:T(8,128)}, u32[]{:S(2)}) copy-start(f32[8,16,512]{2,1,0:T(8,128)} %above_spacing.1) | copy-start | bytes 786436
  20.9 7.5 %collective-permute-start.4 = (f32[4,16,640]{2,1,0:T(8,128)S(1)}, f32[4,16,640]{2,1,0:T(8,128)S(1)}, u32[]{:S(2)}, u32[]{:S(2)}) collective-permute-start(f32[4,16,640]{2,1,0:T(8,128)S(1)} %get-tuple-element.69.cond_last.refs_2_), channel_id=1, source_target_pairs={{0,32},{32,64},{64,96},{96,128},{128,160},{160,192},{192,224},{224... | collective-permute-start | bytes 491528 | tf_op jit(solution)/shard_map/ppermute | solution.py:634
  21.0 4.2 %copy-start.2 = (f32[8,16,512]{2,1,0:T(8,128)S(1)}, f32[8,16,512]{2,1,0:T(8,128)}, u32[]{:S(2)}) copy-start(f32[8,16,512]{2,1,0:T(8,128)} %source.1) | copy-start | bytes 786436
  21.0 4.2 %copy-start.3 = (f32[8,16,512]{2,1,0:T(8,128)S(1)}, f32[8,16,512]{2,1,0:T(8,128)}, u32[]{:S(2)}) copy-start(f32[8,16,512]{2,1,0:T(8,128)} %prior.1) | copy-start | bytes 786436
  21.0 4.2 %copy-start.4 = (f32[8,16,512]{2,1,0:T(8,128)S(1)}, f32[8,16,512]{2,1,0:T(8,128)}, u32[]{:S(2)}) copy-start(f32[8,16,512]{2,1,0:T(8,128)} %temp.1) | copy-start | bytes 786436
  21.1 7.3 %collective-permute-start.5 = (f32[4,16,640]{2,1,0:T(8,128)S(1)}, f32[4,16,640]{2,1,0:T(8,128)S(1)}, u32[]{:S(2)}, u32[]{:S(2)}) collective-permute-start(f32[4,16,640]{2,1,0:T(8,128)S(1)} %get-tuple-element.70.cond_first.refs_1_), channel_id=1, source_target_pairs={{0,224},{32,0},{64,32},{96,64},{128,96},{160,128},{192,160},{224,1... | collective-permute-start | bytes 491528 | tf_op jit(solution)/shard_map/ppermute | solution.py:634
  33.1 5.8 %collective-permute-start.8 = (f32[4,16,640]{2,1,0:T(8,128)S(1)}, f32[4,16,640]{2,1,0:T(8,128)S(1)}, u32[]{:S(2)}, u32[]{:S(2)}) collective-permute-start(f32[4,16,640]{2,1,0:T(8,128)S(1)} %get-tuple-element.91.refs_2_), channel_id=1, source_target_pairs={{0,32},{32,64},{64,96},{96,128},{128,160},{160,192},{192,224},{224... | collective-permute-start | bytes 491528 | tf_op jit(solution)/shard_map/ppermute | solution.py:634
  33.6 5.3 %collective-permute-start.9 = (f32[4,16,640]{2,1,0:T(8,128)S(1)}, f32[4,16,640]{2,1,0:T(8,128)S(1)}, u32[]{:S(2)}, u32[]{:S(2)}) collective-permute-start(f32[4,16,640]{2,1,0:T(8,128)S(1)} %get-tuple-element.92.refs_1_), channel_id=1, source_target_pairs={{0,224},{32,0},{64,32},{96,64},{128,96},{160,128},{192,160},{224,1... | collective-permute-start | bytes 491528 | tf_op jit(solution)/shard_map/ppermute | solution.py:634
  201.9 18.5 %copy-start.9 = (f32[8,16,512]{2,1,0:T(8,128)S(1)}, f32[8,16,512]{2,1,0:T(8,128)}, u32[]{:S(2)}) copy-start(f32[8,16,512]{2,1,0:T(8,128)} %get-tuple-element.60.below) | copy-start | bytes 786436

commit v8 on v7

--- a/solution.py
+++ b/solution.py
@@ -61,8 +61,7 @@
 
 
 def launch_kernel(*refs):
-    firsts, lasts, nears, fars = refs[0:5], refs[5:10], refs[10:13], refs[13:16]
-    to_left, to_right, rows_up, rows_down = refs[16:]
+    firsts, lasts, to_left, to_right = refs[0:5], refs[5:10], refs[10], refs[11]
     rows, height, _ = to_left.shape
     group = lane_iota((height, LANES)) // STRIP
     for row in range(rows):
@@ -77,6 +76,10 @@
                     value = pltpu.roll(value, shift, 1)
                 packed = jnp.where(group == index, value, packed)
             target[row] = packed
+
+
+def rows_kernel(*refs):
+    nears, fars, rows_up, rows_down = refs[0:3], refs[3:6], refs[6], refs[7]
     start = 0
     for near, far, count in zip(nears, fars, (4, 3, 1)):
         for r in range(count):
@@ -599,14 +602,22 @@
 
     strips = (density, material, source, prior, temp)
     layered = (prior, source, temp)
-    return pl.pallas_call(
-        launch_kernel,
-        grid=(1,),
-        out_shape=[jax.ShapeDtypeStruct(s, f32) for s in (block, block, message, message)],
-        in_specs=[first] * 5 + [last] * 5
-        + [layers(4, 0)] * 2 + [layers(1, 0)] + [layers(4, rows // 4 - 1)] * 2 + [layers(1, rows - 1)],
-        out_specs=[pl.BlockSpec(s, lambda i: (0, 0, 0)) for s in (block, block, message, message)],
-    )(*strips, *strips, *layered, *layered)
+
+    def same(shape):
+        return [jax.ShapeDtypeStruct(shape, f32)] * 2, [pl.BlockSpec(shape, lambda i: (0, 0, 0))] * 2
+
+    shapes, specs = same(block)
+    to_sides = pl.pallas_call(
+        launch_kernel, grid=(1,), out_shape=shapes, out_specs=specs,
+        in_specs=[first] * 5 + [last] * 5,
+    )(*strips, *strips)
+    shapes, specs = same(message)
+    to_depths = pl.pallas_call(
+        rows_kernel, grid=(1,), out_shape=shapes, out_specs=specs,
+        in_specs=[layers(4, 0)] * 2 + [layers(1, 0)]
+        + [layers(4, rows // 4 - 1)] * 2 + [layers(1, rows - 1)],
+    )(*layered, *layered)
+    return (*to_sides, *to_depths)
 
 
 def on_device(
@@ -652,11 +663,9 @@
             ]
         )
 
-    density_up, density_down, rows_up, rows_down = lax.optimization_barrier(
-        (density_message(rows - 4), density_message(0), rows_up, rows_down)
-    )
-    density_above, density_below = to_deeper(density_up), to_nearer(density_down)
     from_above, from_below = to_deeper(rows_up), to_nearer(rows_down)
+    density_above = to_deeper(density_message(rows - 4))
+    density_below = to_nearer(density_message(0))
 
     (below, above, up, low, least, most, upper, lower, bend, tallies) = call(
         lines_kernel,

time: 222 us -> 222 us (level)
  transfers between devices with their start and end apart: 10 -> 10, of which waited for: 6 -> 5; matrix products, arithmetic and copies ran while one was open for 0% -> 0% of each run, Pallas kernels for 2% -> 3%
where the time goes in v8:
time: 222 us
  blocking collectives  173 us (78%)
  Pallas kernels  20.5 us (9%)
  starting transfers between devices  17.4 us (8%)
  waiting for transfers between devices  9.55 us (4%)
    all_to_all x9, blocking collectives, everyone(): return lax.all_to_all(rows_out, AXES, 0, 0, tiled=True)  173 us
    ppermute x10, starting transfers between devices, turn(): return lambda value: lax.ppermute(value, axis, pairs)  17.4 us
    ppermute x10, waiting for transfers between devices, turn(): return lambda value: lax.ppermute(value, axis, pairs)  9.55 us
    pallas_call x3, Pallas kernels, placed_call(): pl.pallas_call(with_place(kernel, *totals), out_shape=[jax.ShapeDtypeStru...  8.76 us
    pallas_call x11, Pallas kernels, call(): pl.pallas_call(kernel, out_shape=[jax.ShapeDtypeStruct(shape, f32) for sh...  7.78 us
  transfers between devices with their start and end apart: 10, of which 5 were waited for; matrix products, arithmetic and copies ran while one was open for 0% of the time, Pallas kernels for 3%

profile of v8, /device:TPU:1, one launch (start us, length us, event | category | flops | bytes accessed | tf_op | source)
XLA Modules:
  0.0 222.0 jit_solution(15870529199256703123)
XLA Ops:
  0.6 0.0 copy-start.1
  0.6 2.0 shard_map.120
  2.7 2.6 %collective-permute-start = (f32[8,16,128]{2,1,0:T(8,128)}, f32[8,16,128]{2,1,0:T(8,128)S(1)}, u32[]{:S(2)}, u32[]{:S(2)}) collective-permute-start(f32[8,16,128]{2,1,0:T(8,128)} %get-tuple-element.59), channel_id=1, source_target_pairs={{0,1},{1,2},{2,3},{3,4},{4,5},{5,6},{6,7},{7,8},{8,9},{9,10},{10,1... | collective-permute-start | bytes 196616 | tf_op jit(solution)/shard_map/ppermute | solution.py:645
  5.3 0.7 collective-permute-start.1
  6.0 0.0 copy-done.1
  6.0 0.9 collective-permute-done.refs_4_.left.refs_22_
  6.9 2.2 %collective-permute-done.1.refs_5_.right.refs_23_ = f32[8,16,128]{2,1,0:T(8,128)S(1)} collective-permute-done((f32[8,16,128]{2,1,0:T(8,128)}, f32[8,16,128]{2,1,0:T(8,128)S(1)}, u32[]{:S(2)}, u32[]{:S(2)}) %collective-permute-start.1) | collective-permute-done | bytes 65568 | tf_op jit(solution)/shard_map/ppermute | solution.py:645
  9.2 5.9 %collective-permute-start.3 = (f32[6,16,512]{2,1,0:T(8,128)S(1)}, f32[6,16,512]{2,1,0:T(8,128)S(1)}, u32[]{:S(2)}, u32[]{:S(2)}) collective-permute-start(f32[6,16,512]{2,1,0:T(8,128)S(1)} %pad_maximum_fusion.1), channel_id=1, source_target_pairs={{0,224},{32,0},{64,32},{96,64},{128,96},{160,128},{192,160},{224,1... | collective-permute-start | bytes 589832 | tf_op jit(solution)/shard_map/ppermute | solution.py:645
  15.2 0.0 copy-start
  15.2 0.1 collective-permute-start.2
  15.3 1.9 shard_map.122
  17.2 0.0 collective-permute-start.6
  17.3 2.7 %collective-permute-start.7 = (f32[8,16,512]{2,1,0:T(8,128)}, f32[8,16,512]{2,1,0:T(8,128)S(1)}, u32[]{:S(2)}, u32[]{:S(2)}) collective-permute-start(f32[8,16,512]{2,1,0:T(8,128)} %get-tuple-element.65), channel_id=1, source_target_pairs={{0,224},{32,0},{64,32},{96,64},{128,96},{160,128},{192,160},{224,1... | collective-permute-start | bytes 786440 | tf_op jit(solution)/shard_map/ppermute | solution.py:645
  19.9 0.1 pad_add_fusion.place_ref
  20.0 0.0 copy-start.5
  20.0 0.0 copy-start.7
  20.0 0.0 collective-permute-done.3.refs_3_.density_below
  20.0 1.0 collective-permute-done.2.refs_2_.density_above
  21.0 0.0 copy-done
  21.0 2.2 shard_map.121
  23.2 0.1 collective-permute-start.4
  23.3 0.0 copy-start.2
  23.3 0.0 copy-start.3
  23.3 0.0 copy-start.4
  23.3 2.6 %collective-permute-start.5 = (f32[4,16,640]{2,1,0:T(8,128)S(1)}, f32[4,16,640]{2,1,0:T(8,128)S(1)}, u32[]{:S(2)}, u32[]{:S(2)}) collective-permute-start(f32[4,16,640]{2,1,0:T(8,128)S(1)} %get-tuple-element.62.cond_first.refs_1_), channel_id=1, source_target_pairs={{0,224},{32,0},{64,32},{96,64},{128,96},{160,128},{192,160},{224,1... | collective-permute-start | bytes 491528 | tf_op jit(solution)/shard_map/ppermute | solution.py:645
  26.0 0.0 copy-done.5
  26.0 0.0 copy-done.6
  26.0 0.0 copy-done.7
  26.0 0.0 copy-done.8
  26.0 0.9 shard_map.124
  26.9 0.0 collective-permute-done.6.from_above
  26.9 0.0 collective-permute-done.7.from_below
  26.9 0.0 copy-done.2
  26.9 0.0 copy-done.3
  26.9 0.0 copy-done.4
  26.9 1.2 shard_map.123
  28.1 2.7 %collective-permute-done.4.refs_0_ = f32[4,16,640]{2,1,0:T(8,128)S(1)} collective-permute-done((f32[4,16,640]{2,1,0:T(8,128)S(1)}, f32[4,16,640]{2,1,0:T(8,128)S(1)}, u32[]{:S(2)}, u32[]{:S(2)}) %collective-permute-start.4) | collective-permute-done | bytes 163872 | tf_op jit(solution)/shard_map/ppermute | solution.py:645
  30.8 0.0 collective-permute-done.5.refs_3_
  30.8 4.7 %shard_map.125 = (f32[8,16,512]{2,1,0:T(8,128)}, f32[4,16,640]{2,1,0:T(8,128)S(1)}, f32[4,16,640]{2,1,0:T(8,128)S(1)}) custom-call(s32[2]{0:T(128)S(1)} %pad_add_fusion.place_ref, f32[4,16,640]{2,1,0:T(8,128)S(1)} %collective-permute-done.4.refs_0_, f32[4,16,640]{2,1,0:T(8,128)S(1)} %get-tuple-element.62.cond_first.refs_1_, ...), custom_call_target="tpu_custom_call" | custom-call | tf_op jit(solution)/shard_map/pallas_call | solution.py:583
  35.5 0.0 collective-permute-start.8
  35.5 2.7 %collective-permute-start.9 = (f32[4,16,640]{2,1,0:T(8,128)S(1)}, f32[4,16,640]{2,1,0:T(8,128)S(1)}, u32[]{:S(2)}, u32[]{:S(2)}) collective-permute-start(f32[4,16,640]{2,1,0:T(8,128)S(1)} %get-tuple-element.84.refs_1_), channel_id=1, source_target_pairs={{0,224},{32,0},{64,32},{96,64},{128,96},{160,128},{192,160},{224,1... | collective-permute-start | bytes 491528 | tf_op jit(solution)/shard_map/ppermute | solution.py:645
  38.2 2.7 %collective-permute-done.8.refs_0_ = f32[4,16,640]{2,1,0:T(8,128)S(1)} collective-permute-done((f32[4,16,640]{2,1,0:T(8,128)S(1)}, f32[4,16,640]{2,1,0:T(8,128)S(1)}, u32[]{:S(2)}, u32[]{:S(2)}) %collective-permute-start.8) | collective-permute-done | bytes 163872 | tf_op jit(solution)/shard_map/ppermute | solution.py:645
  40.9 0.0 collective-permute-done.9.refs_3_
  40.9 1.9 shard_map.126
  42.8 26.3 %all_to_all.99 = f32[256,1,128]{2,1,0:T(1,128)S(1)} all-to-all(f32[256,1,128]{2,1,0:T(1,128)S(1)} %bitcast.88), channel_id=1, replica_groups=mesh['thick'=8,'facade'=32] {'thick','facade'}, dimensions={0} | all-to-all | bytes 262144 | tf_op jit(solution)/shard_map/all_to_all | solution.py:723
  69.0 0.6 shard_map.127
  69.7 18.4 %all_to_all.100 = f32[256,1,128]{2,1,0:T(1,128)S(1)} all-to-all(f32[256,1,128]{2,1,0:T(1,128)S(1)} %bitcast.89), channel_id=1, replica_groups=mesh['thick'=8,'facade'=32] {'thick','facade'}, dimensions={0} | all-to-all | bytes 262144 | tf_op jit(solution)/shard_map/all_to_all | solution.py:723
  88.0 0.6 shard_map.128
  88.6 18.4 %all_to_all.101 = f32[256,1,128]{2,1,0:T(1,128)S(1)} all-to-all(f32[256,1,128]{2,1,0:T(1,128)S(1)} %bitcast.90), channel_id=1, replica_groups=mesh['thick'=8,'facade'=32] {'thick','facade'}, dimensions={0} | all-to-all | bytes 262144 | tf_op jit(solution)/shard_map/all_to_all | solution.py:723
  107.0 0.6 shard_map.129
  107.5 18.4 %all_to_all.102 = f32[256,1,128]{2,1,0:T(1,128)S(1)} all-to-all(f32[256,1,128]{2,1,0:T(1,128)S(1)} %bitcast.91), channel_id=1, replica_groups=mesh['thick'=8,'facade'=32] {'thick','facade'}, dimensions={0} | all-to-all | bytes 262144 | tf_op jit(solution)/shard_map/all_to_all | solution.py:723
  125.9 0.6 shard_map.130
  126.5 18.4 %all_to_all.103 = f32[256,1,128]{2,1,0:T(1,128)S(1)} all-to-all(f32[256,1,128]{2,1,0:T(1,128)S(1)} %bitcast.92), channel_id=1, replica_groups=mesh['thick'=8,'facade'=32] {'thick','facade'}, dimensions={0} | all-to-all | bytes 262144 | tf_op jit(solution)/shard_map/all_to_all | solution.py:723
  144.8 0.6 shard_map.131
  145.4 18.6 %all_to_all.104 = f32[256,1,128]{2,1,0:T(1,128)S(1)} all-to-all(f32[256,1,128]{2,1,0:T(1,128)S(1)} %bitcast.93), channel_id=1, replica_groups=mesh['thick'=8,'facade'=32] {'thick','facade'}, dimensions={0} | all-to-all | bytes 262144 | tf_op jit(solution)/shard_map/all_to_all | solution.py:723
  164.0 0.6 shard_map.132
  164.6 18.4 %all_to_all.105 = f32[256,1,128]{2,1,0:T(1,128)S(1)} all-to-all(f32[256,1,128]{2,1,0:T(1,128)S(1)} %bitcast.94), channel_id=1, replica_groups=mesh['thick'=8,'facade'=32] {'thick','facade'}, dimensions={0} | all-to-all | bytes 262144 | tf_op jit(solution)/shard_map/all_to_all | solution.py:723
  182.9 0.6 shard_map.133
  183.5 18.4 %all_to_all.106 = f32[256,1,128]{2,1,0:T(1,128)S(1)} all-to-all(f32[256,1,128]{2,1,0:T(1,128)S(1)} %bitcast.95), channel_id=1, replica_groups=mesh['thick'=8,'facade'=32] {'thick','facade'}, dimensions={0} | all-to-all | bytes 262144 | tf_op jit(solution)/shard_map/all_to_all | solution.py:723
  201.9 0.6 shard_map.134
  202.4 0.0 copy-start.9
  202.5 18.5 %all_to_all.107 = f32[256,1,128]{2,1,0:T(1,128)S(1)} all-to-all(f32[256,1,128]{2,1,0:T(1,128)S(1)} %bitcast.87), channel_id=1, replica_groups=mesh['thick'=8,'facade'=32] {'thick','facade'}, dimensions={0} | all-to-all | bytes 262144 | tf_op jit(solution)/shard_map/all_to_all | solution.py:723
  220.9 0.0 copy-done.9
  220.9 1.0 shard_map.135
  (10 shorter events, 0.1 us)
Async XLA Ops:
  0.6 5.4 %copy-start.1 = (f32[8,16,512]{2,1,0:T(8,128)S(1)}, f32[8,16,512]{2,1,0:T(8,128)}, u32[]{:S(2)}) copy-start(f32[8,16,512]{2,1,0:T(8,128)} %solid.3) | copy-start | bytes 786436
  2.7 4.2 %collective-permute-start = (f32[8,16,128]{2,1,0:T(8,128)}, f32[8,16,128]{2,1,0:T(8,128)S(1)}, u32[]{:S(2)}, u32[]{:S(2)}) collective-permute-start(f32[8,16,128]{2,1,0:T(8,128)} %get-tuple-element.59), channel_id=1, source_target_pairs={{0,1},{1,2},{2,3},{3,4},{4,5},{5,6},{6,7},{7,8},{8,9},{9,10},{10,1... | collective-permute-start | bytes 196616 | tf_op jit(solution)/shard_map/ppermute | solution.py:645
  5.3 3.9 %collective-permute-start.1 = (f32[8,16,128]{2,1,0:T(8,128)}, f32[8,16,128]{2,1,0:T(8,128)S(1)}, u32[]{:S(2)}, u32[]{:S(2)}) collective-permute-start(f32[8,16,128]{2,1,0:T(8,128)} %get-tuple-element.60), channel_id=1, source_target_pairs={{0,31},{1,0},{2,1},{3,2},{4,3},{5,4},{6,5},{7,6},{8,7},{9,8},{10,9... | collective-permute-start | bytes 196616 | tf_op jit(solution)/shard_map/ppermute | solution.py:645
  9.2 10.8 %collective-permute-start.3 = (f32[6,16,512]{2,1,0:T(8,128)S(1)}, f32[6,16,512]{2,1,0:T(8,128)S(1)}, u32[]{:S(2)}, u32[]{:S(2)}) collective-permute-start(f32[6,16,512]{2,1,0:T(8,128)S(1)} %pad_maximum_fusion.1), channel_id=1, source_target_pairs={{0,224},{32,0},{64,32},{96,64},{128,96},{160,128},{192,160},{224,1... | collective-permute-start | bytes 589832 | tf_op jit(solution)/shard_map/ppermute | solution.py:645
  15.2 5.8 %copy-start = (s32[8,16,512]{2,1,0:T(8,128)S(1)}, s32[8,16,512]{2,1,0:T(8,128)}, u32[]{:S(2)}) copy-start(s32[8,16,512]{2,1,0:T(8,128)} %material.3) | copy-start | bytes 786436
  15.2 5.8 %collective-permute-start.2 = (f32[6,16,512]{2,1,0:T(8,128)S(1)}, f32[6,16,512]{2,1,0:T(8,128)S(1)}, u32[]{:S(2)}, u32[]{:S(2)}) collective-permute-start(f32[6,16,512]{2,1,0:T(8,128)S(1)} %pad_maximum_fusion), channel_id=1, source_target_pairs={{0,32},{32,64},{64,96},{96,128},{128,160},{160,192},{192,224},{224... | collective-permute-start | bytes 589832 | tf_op jit(solution)/shard_map/ppermute | solution.py:645
  17.2 9.7 %collective-permute-start.6 = (f32[8,16,512]{2,1,0:T(8,128)}, f32[8,16,512]{2,1,0:T(8,128)S(1)}, u32[]{:S(2)}, u32[]{:S(2)}) collective-permute-start(f32[8,16,512]{2,1,0:T(8,128)} %get-tuple-element.64), channel_id=1, source_target_pairs={{0,32},{32,64},{64,96},{96,128},{128,160},{160,192},{192,224},{224... | collective-permute-start | bytes 786440 | tf_op jit(solution)/shard_map/ppermute | solution.py:645
  17.3 9.7 %collective-permute-start.7 = (f32[8,16,512]{2,1,0:T(8,128)}, f32[8,16,512]{2,1,0:T(8,128)S(1)}, u32[]{:S(2)}, u32[]{:S(2)}) collective-permute-start(f32[8,16,512]{2,1,0:T(8,128)} %get-tuple-element.65), channel_id=1, source_target_pairs={{0,224},{32,0},{64,32},{96,64},{128,96},{160,128},{192,160},{224,1... | collective-permute-start | bytes 786440 | tf_op jit(solution)/shard_map/ppermute | solution.py:645
  20.0 6.0 %copy-start.5 = (f32[8,16,512]{2,1,0:T(8,128)S(1)}, f32[8,16,512]{2,1,0:T(8,128)}, u32[]{:S(2)}) copy-start(f32[8,16,512]{2,1,0:T(8,128)} %newer.1) | copy-start | bytes 786436
  20.0 6.0 %copy-start.6 = (f32[8,16,512]{2,1,0:T(8,128)S(1)}, f32[8,16,512]{2,1,0:T(8,128)}, u32[]{:S(2)}) copy-start(f32[8,16,512]{2,1,0:T(8,128)} %older.1) | copy-start | bytes 786436
  20.0 6.0 %copy-start.7 = (f32[8,16,512]{2,1,0:T(8,128)S(1)}, f32[8,16,512]{2,1,0:T(8,128)}, u32[]{:S(2)}) copy-start(f32[8,16,512]{2,1,0:T(8,128)} %below_spacing.1) | copy-start | bytes 786436
  20.0 6.0 %copy-start.8 = (f32[8,16,512]{2,1,0:T(8,128)S(1)}, f32[8,16,512]{2,1,0:T(8,128)}, u32[]{:S(2)}) copy-start(f32[8,16,512]{2,1,0:T(8,128)} %above_spacing.1) | copy-start | bytes 786436
  23.2 7.6 %collective-permute-start.4 = (f32[4,16,640]{2,1,0:T(8,128)S(1)}, f32[4,16,640]{2,1,0:T(8,128)S(1)}, u32[]{:S(2)}, u32[]{:S(2)}) collective-permute-start(f32[4,16,640]{2,1,0:T(8,128)S(1)} %get-tuple-element.61.cond_last.refs_2_), channel_id=1, source_target_pairs={{0,32},{32,64},{64,96},{96,128},{128,160},{160,192},{192,224},{224... | collective-permute-start | bytes 491528 | tf_op jit(solution)/shard_map/ppermute | solution.py:645
  23.3 3.6 %copy-start.2 = (f32[8,16,512]{2,1,0:T(8,128)S(1)}, f32[8,16,512]{2,1,0:T(8,128)}, u32[]{:S(2)}) copy-start(f32[8,16,512]{2,1,0:T(8,128)} %source.1) | copy-start | bytes 786436
  23.3 3.6 %copy-start.3 = (f32[8,16,512]{2,1,0:T(8,128)S(1)}, f32[8,16,512]{2,1,0:T(8,128)}, u32[]{:S(2)}) copy-start(f32[8,16,512]{2,1,0:T(8,128)} %prior.1) | copy-start | bytes 786436
  23.3 3.6 %copy-start.4 = (f32[8,16,512]{2,1,0:T(8,128)S(1)}, f32[8,16,512]{2,1,0:T(8,128)}, u32[]{:S(2)}) copy-start(f32[8,16,512]{2,1,0:T(8,128)} %temp.1) | copy-start | bytes 786436
  23.3 7.4 %collective-permute-start.5 = (f32[4,16,640]{2,1,0:T(8,128)S(1)}, f32[4,16,640]{2,1,0:T(8,128)S(1)}, u32[]{:S(2)}, u32[]{:S(2)}) collective-permute-start(f32[4,16,640]{2,1,0:T(8,128)S(1)} %get-tuple-element.62.cond_first.refs_1_), channel_id=1, source_target_pairs={{0,224},{32,0},{64,32},{96,64},{128,96},{160,128},{192,160},{224,1... | collective-permute-start | bytes 491528 | tf_op jit(solution)/shard_map/ppermute | solution.py:645
  35.5 5.4 %collective-permute-start.8 = (f32[4,16,640]{2,1,0:T(8,128)S(1)}, f32[4,16,640]{2,1,0:T(8,128)S(1)}, u32[]{:S(2)}, u32[]{:S(2)}) collective-permute-start(f32[4,16,640]{2,1,0:T(8,128)S(1)} %get-tuple-element.83.refs_2_), channel_id=1, source_target_pairs={{0,32},{32,64},{64,96},{96,128},{128,160},{160,192},{192,224},{224... | collective-permute-start | bytes 491528 | tf_op jit(solution)/shard_map/ppermute | solution.py:645
  35.5 5.4 %collective-permute-start.9 = (f32[4,16,640]{2,1,0:T(8,128)S(1)}, f32[4,16,640]{2,1,0:T(8,128)S(1)}, u32[]{:S(2)}, u32[]{:S(2)}) collective-permute-start(f32[4,16,640]{2,1,0:T(8,128)S(1)} %get-tuple-element.84.refs_1_), channel_id=1, source_target_pairs={{0,224},{32,0},{64,32},{96,64},{128,96},{160,128},{192,160},{224,1... | collective-permute-start | bytes 491528 | tf_op jit(solution)/shard_map/ppermute | solution.py:645
  202.4 18.5 %copy-start.9 = (f32[8,16,512]{2,1,0:T(8,128)S(1)}, f32[8,16,512]{2,1,0:T(8,128)}, u32[]{:S(2)}) copy-start(f32[8,16,512]{2,1,0:T(8,128)} %get-tuple-element.56.below) | copy-start | bytes 786436
